TPU v7x, 32 devices: a whole 2x2x4 slice. The times are simulated.
32 devices in a mesh: ctx: 4 (over z), tp: 4 (over y, core), dp: 2 (over x).
Axes of the slice: x: 2, y: 2, z: 4, core: 2. Of those that a mesh axis runs over, the one named last changes fastest.
Arguments:
- queries: bfloat16 [4096, 2048], P(('dp', 'ctx'), 'tp'), parts along dimension 0, may hold values from -6 to 6
- keys: bfloat16 [4096, 512], P(('dp', 'ctx'), 'tp'), parts along dimension 0, may hold values from -6 to 6
- values: bfloat16 [4096, 512], P(('dp', 'ctx'), 'tp'), parts along dimension 0, may hold values from -6 to 6
- outputs: bfloat16 [4096, 2048], P(('dp', 'ctx'), 'tp'), parts along dimension 0, may hold values from -4 to 4
- out_grads: bfloat16 [4096, 2048], P(('dp', 'ctx'), 'tp'), parts along dimension 0, may hold values from -6 to 6
- log_norms: float32 [16, 4096], P('tp', ('dp', 'ctx')), parts along dimension 1, may hold values from 3 to 6
- stretch_order: int32 [16], P('dp'), parts along dimension 0, may hold values from 0 to 7, each once
Outputs:
- grad_queries: bfloat16 [4096, 2048], P(('dp', 'ctx'), 'tp'), parts along dimension 0
- grad_keys: bfloat16 [4096, 512], P(('dp', 'ctx'), 'tp'), parts along dimension 0
- grad_values: bfloat16 [4096, 512], P(('dp', 'ctx'), 'tp'), parts along dimension 0
There are 2 independent parts, one for each index of `dp`. A program takes and returns all parts, laid end to end along the dimension named above; each array names one. Nothing has to cross between parts.
Inputs may be any that keep to these rules, and one draw needn't show every extreme that they name: stretch_order is a permutation of the 8 sequence blocks of 256 tokens.
All inputs are finite; a program needn't handle non-finite values.
Results may differ from a plain program's by a relative error of at most 0.023.
Values may be sent and summed in bfloat16 or wider, within the bound.
No kernel may reach another device: no remote copies, remote signals or barrier semaphores. Data moves between devices by JAX's collectives and lax.ppermute only.
A program may use at most 64 MiB of HBM per device.

v0:
```python
import jax
import jax.numpy as jnp
from jax import lax
from jax.sharding import PartitionSpec as P

QH = 16
KVH = 4
HD = 128


def positions_of(stretch_order, first_stretch, count, stretch_size):
    offsets = jnp.arange(count, dtype=jnp.int32)
    stretch_ids = first_stretch + offsets // stretch_size
    return jnp.take(stretch_order, stretch_ids) * stretch_size + offsets % stretch_size


def tile_grads(
    query_heads, grad_heads, norm_heads, delta_rows, query_pos, key_block, value_block, key_pos
):
    block_rows = key_block.shape[0]
    kv_local = query_heads.shape[1]
    score_scale = HD ** (-0.5)
    key_heads = key_block.reshape(block_rows, kv_local, HD)
    value_heads = value_block.reshape(block_rows, kv_local, HD)
    scores = (
        jnp.einsum("rhgd,chd->hgrc", query_heads, key_heads, preferred_element_type=jnp.float32)
        * score_scale
    )
    allowed = key_pos[None, :] <= query_pos[:, None]
    probs = jnp.where(
        allowed[None, None], jnp.exp(scores - norm_heads[:, :, :, None]), jnp.float32(0.0)
    )
    probs_low = probs.astype(jnp.bfloat16)
    grad_value = jnp.einsum(
        "hgrc,rhgd->chd", probs_low, grad_heads, preferred_element_type=jnp.float32
    )
    grad_probs = jnp.einsum(
        "rhgd,chd->hgrc", grad_heads, value_heads, preferred_element_type=jnp.float32
    )
    grad_scores = (score_scale * probs * (grad_probs - delta_rows[:, :, :, None])).astype(
        jnp.bfloat16
    )
    grad_query = jnp.einsum(
        "hgrc,chd->rhgd", grad_scores, key_heads, preferred_element_type=jnp.float32
    )
    grad_key = jnp.einsum(
        "hgrc,rhgd->chd", grad_scores, query_heads, preferred_element_type=jnp.float32
    )
    return (
        grad_query,
        grad_key.reshape(block_rows, kv_local * HD),
        grad_value.reshape(block_rows, kv_local * HD),
    )


def shards(queries, keys, values, outputs, out_grads, log_norms, stretch_order):
    local_rows = queries.shape[0]
    stretch_size = local_rows // 2
    kv_local = keys.shape[1] // HD
    width = kv_local * HD
    group_size = QH // KVH
    my_index = lax.axis_index("ctx")
    query_heads = queries.reshape(local_rows, kv_local, group_size, HD)
    grad_heads = out_grads.reshape(local_rows, kv_local, group_size, HD)
    output_heads = outputs.reshape(local_rows, kv_local, group_size, HD)
    delta_rows = jnp.sum(
        grad_heads.astype(jnp.float32) * output_heads.astype(jnp.float32), axis=3
    ).transpose(1, 2, 0)
    norm_heads = log_norms.reshape(kv_local, group_size, local_rows)
    query_pos = positions_of(stretch_order, my_index * 2, local_rows, stretch_size)

    def attend_block(key_block, value_block, key_pos):
        return tile_grads(
            query_heads,
            grad_heads,
            norm_heads,
            delta_rows,
            query_pos,
            key_block,
            value_block,
            key_pos,
        )

    grad_start = jnp.zeros((local_rows, kv_local, group_size, HD), jnp.float32)
    key_all, value_all = (
        lax.all_gather(keys, "ctx", axis=0, tiled=True),
        lax.all_gather(values, "ctx", axis=0, tiled=True),
    )
    total_rows = key_all.shape[0]
    block_size = 2 * local_rows
    all_pos = positions_of(stretch_order, jnp.int32(0), total_rows, stretch_size)

    def visit(block_index, state_tuple):
        grad_query, grad_term = state_tuple
        start_row = block_index * block_size
        key_block = lax.dynamic_slice_in_dim(key_all, start_row, block_size, 0)
        value_block = lax.dynamic_slice_in_dim(value_all, start_row, block_size, 0)
        key_pos = lax.dynamic_slice_in_dim(all_pos, start_row, block_size, 0)
        query_add, grad_key, grad_value = attend_block(key_block, value_block, key_pos)
        grad_term = lax.dynamic_update_slice_in_dim(
            grad_term, jnp.concatenate([grad_key, grad_value], axis=1), start_row, 0
        )
        return (grad_query + query_add, grad_term)

    term_start = jnp.zeros((total_rows, 2 * width), jnp.float32)
    grad_query, grad_term = lax.fori_loop(
        0, total_rows // block_size, visit, (grad_start, term_start)
    )
    summed = lax.psum_scatter(
        grad_term.astype(jnp.bfloat16), "ctx", scatter_dimension=0, tiled=True
    ).astype(jnp.float32)
    grad_queries = grad_query.reshape(local_rows, kv_local * group_size * HD).astype(jnp.bfloat16)
    grad_keys = summed[:, :width].astype(jnp.bfloat16)
    grad_values = summed[:, width:].astype(jnp.bfloat16)
    return (grad_queries, grad_keys, grad_values)


def solution(mesh):
    return jax.shard_map(
        shards,
        mesh=mesh,
        in_specs=(
            P(("dp", "ctx"), "tp"),
            P(("dp", "ctx"), "tp"),
            P(("dp", "ctx"), "tp"),
            P(("dp", "ctx"), "tp"),
            P(("dp", "ctx"), "tp"),
            P("tp", ("dp", "ctx")),
            P("dp"),
        ),
        out_specs=(P(("dp", "ctx"), "tp"), P(("dp", "ctx"), "tp"), P(("dp", "ctx"), "tp")),
        check_vma=False,
    )
```

profile of v0, /device:TPU:0, one launch (start us, length us, event | category | flops | bytes accessed | tf_op | source)
XLA Modules:
  0.0 122.5 jit_solution(14824775570330600056)
XLA Ops:
  7.3 1.6 %fusion.55 = (s32[1]{0:T(128)}, s32[1]{0:T(128)}, s32[1]{0:T(128)}, s32[1]{0:T(128)}, s32[1]{0:T(128)}, /*index=5*/s32[1]{0:T(128)}, s32[1]{0:T(128)}, s32[1]{0:T(128)}) fusion(s32[8]{0:T(128)} %param.15), kind=kLoop, calls=%fused_computation.94 | loop fusion | bytes 64 | tf_op jit(solution)/shard_map/jit(_take)/gather | solution.py:14
  8.9 1.3 %copy.27 = bf16[512,512]{0,1:T(8,128)(2,1)S(1)} copy(bf16[512,512]{1,0:T(8,128)(2,1)} %param.9) | data formatting | bytes 1048576 | tf_op args[0]
  10.2 17.6 %all_gather.6 = bf16[2048,128]{1,0:T(8,128)(2,1)S(1)} all-gather(bf16[512,128]{1,0:T(8,128)(2,1)} %param.10), channel_id=1, replica_groups=mesh['ctx'=4,'tp'=4,'dp'=2] {'ctx'}, dimensions={0}, use_global_device_ids=true | all-gather | bytes 655360 | tf_op jit(solution)/shard_map/all_gather | solution.py:86
  27.7 17.7 %all_gather.7 = bf16[2048,128]{1,0:T(8,128)(2,1)} all-gather(bf16[512,128]{1,0:T(8,128)(2,1)} %param.11), channel_id=1, replica_groups=mesh['ctx'=4,'tp'=4,'dp'=2] {'ctx'}, dimensions={0}, use_global_device_ids=true | all-gather | bytes 655360 | tf_op jit(solution)/shard_map/all_gather | solution.py:87
  45.4 2.0 %copy.28 = bf16[512,512]{0,1:T(8,128)(2,1)} copy(bf16[512,512]{1,0:T(8,128)(2,1)} %param.13) | data formatting | bytes 1048576 | tf_op args[4]
  47.5 1.3 %copy.29 = f32[512,512]{0,1:T(8,128)S(1)} copy(bf16[512,512]{1,0:T(8,128)(2,1)} %param.12) | data formatting | bytes 1572864 | tf_op jit(solution)/shard_map/convert_element_type | solution.py:67
  48.7 1.2 multiply_reduce_fusion
  49.9 4.4 %compare_select_fusion.9 = s32[2048,1]{0,1:T(1,128)S(1)} fusion(s32[]{:T(128)} %bitcast.1, s32[]{:T(128)} %bitcast.2, s32[]{:T(128)} %bitcast.3, s32[]{:T(128)} %bitcast.4, s32[]{:T(128)} %bitcast.5, s32[]{:T(128)} %bitcast.7, s32[]{:T(128)} %bitcast.6), kind=kLoop, calls=%fused_computation.65 | loop fusion | flops 47104 | bytes 8220 | tf_op jit(solution)/shard_map/jit(_take)/gather | solution.py:14
  55.0 1.1 broadcast_in_dim.55.clone
  56.0 30.7 %while.16 = (s32[]{:T(128)}, f32[512,1,4,128]{0,3,2,1:T(8,128)S(1)}, bf16[2048,256]{1,0:T(8,128)(2,1)}, bf16[2048,128]{1,0:T(8,128)(2,1)S(1)}, s32[2048]{0:T(102...) while((s32[]{:T(128)}, ...), condition=%wide.region_2.3_spmd.clone, body=%wide.region_1.2_spmd.clone.sunk | while | flops 2709551104 | bytes 52245920 | solution.py:106
  56.1 4.4 %compare_select_fusion.17 = s32[512,1]{0,1:T(1,128)S(1)} fusion(s32[]{:T(128)} %get-tuple-element.481, s32[]{:T(128)} %get-tuple-element.482, s32[]{:T(128)} %get-tuple-element.483, s32[]{:T(128)} %get-tuple-element.484, s32[]{:T(128)} %get-tuple-element.485, s32[]{:T(128)} %get-tuple-element.486, s32[]{:T(128)} %get-tuple-element.487, ...), kind=kLoop, calls=%fused_computation.35.clone.1 | loop fusion | flops 12288 | bytes 2080 | tf_op jit(solution)/shard_map/jit(_take)/gather | solution.py:14
  61.6 1.2 %fusion.83 = f32[1024,512,4]{1,0,2:T(8,128)S(1)} fusion(bf16[512,1,4,128]{0,3,2,1:T(8,128)(2,1)S(1)} %get-tuple-element.475, bf16[2048,128]{1,0:T(8,128)(2,1)S(1)} %get-tuple-element.473, s32[]{:T(128)S(6)} %select_n.372), kind=kOutput, calls=%fused_computation.21.clone.1 | convolution fusion | flops 536870912 | bytes 9175044 | tf_op jit(solution)/shard_map/while/body/eval_jaxpr/rhgd,chd->hgrc/dot_general | solution.py:26
  62.8 2.0 %fusion.87 = bf16[1024,128]{0,1:T(8,128)(2,1)S(1)} fusion(f32[1024,512,4]{1,0,2:T(8,128)S(1)} %fusion.83, f32[4,512]{1,0:T(4,128)S(1)} %copy-done.2, pred[512,1024]{0,1:T(8,128)(4,1)S(1)} %broadcast_compare_fusion.2, bf16[512,1,4,128]{0,3,2,1:T(8,128)(2,1)S(1)} %copy-done), kind=kOutput, calls=%fused_computation.14.clone.1 | convolution fusion | flops 545259520 | bytes 9707520 | tf_op jit(solution)/shard_map/while/body/eval_jaxpr/hgrc,rhgd->chd/dot_general | solution.py:34
  64.8 3.2 %fusion.85 = bf16[4,512,1024]{1,2,0:T(8,128)(2,1)S(1)} fusion(f32[1024,512,4]{1,0,2:T(8,128)S(1)} %fusion.83, f32[4,512]{1,0:T(4,128)S(1)} %bitcast.131, f32[4,512]{1,0:T(4,128)S(1)} %copy-done.2, pred[512,1024]{0,1:T(8,128)(4,1)S(1)} %broadcast_compare_fusion.2, bf16[512,1,4,128]{0,3,2,1:T(8,128)(2,1)S(1)} %copy-done, ...), kind=kOutput, calls=%fused_computation.9.clone.1 | convolution fusion | flops 551550976 | bytes 13910020 | tf_op jit(solution)/shard_map/while/body/eval_jaxpr/rhgd,chd->hgrc/dot_general | solution.py:37
  68.0 1.5 %convolution_bitcast_fusion.3 = bf16[1024,128]{0,1:T(8,128)(2,1)S(1)} fusion(bf16[4,512,1024]{1,2,0:T(8,128)(2,1)S(1)} %fusion.85, bf16[512,1,4,128]{0,3,2,1:T(8,128)(2,1)S(1)} %get-tuple-element.475), kind=kOutput, calls=%fused_computation.15.clone.1 | convolution fusion | flops 536870912 | bytes 4980736 | tf_op jit(solution)/shard_map/while/body/eval_jaxpr/hgrc,rhgd->chd/dot_general | solution.py:46
  71.4 4.4 %compare_select_fusion.17 = s32[512,1]{0,1:T(1,128)S(1)} fusion(s32[]{:T(128)} %get-tuple-element.481, s32[]{:T(128)} %get-tuple-element.482, s32[]{:T(128)} %get-tuple-element.483, s32[]{:T(128)} %get-tuple-element.484, s32[]{:T(128)} %get-tuple-element.485, s32[]{:T(128)} %get-tuple-element.486, s32[]{:T(128)} %get-tuple-element.487, ...), kind=kLoop, calls=%fused_computation.35.clone.1 | loop fusion | flops 12288 | bytes 2080 | tf_op jit(solution)/shard_map/jit(_take)/gather | solution.py:14
  76.9 1.2 %fusion.83 = f32[1024,512,4]{1,0,2:T(8,128)S(1)} fusion(bf16[512,1,4,128]{0,3,2,1:T(8,128)(2,1)S(1)} %get-tuple-element.475, bf16[2048,128]{1,0:T(8,128)(2,1)S(1)} %get-tuple-element.473, s32[]{:T(128)S(6)} %select_n.372), kind=kOutput, calls=%fused_computation.21.clone.1 | convolution fusion | flops 536870912 | bytes 9175044 | tf_op jit(solution)/shard_map/while/body/eval_jaxpr/rhgd,chd->hgrc/dot_general | solution.py:26
  78.2 2.0 %fusion.87 = bf16[1024,128]{0,1:T(8,128)(2,1)S(1)} fusion(f32[1024,512,4]{1,0,2:T(8,128)S(1)} %fusion.83, f32[4,512]{1,0:T(4,128)S(1)} %copy-done.2, pred[512,1024]{0,1:T(8,128)(4,1)S(1)} %broadcast_compare_fusion.2, bf16[512,1,4,128]{0,3,2,1:T(8,128)(2,1)S(1)} %copy-done), kind=kOutput, calls=%fused_computation.14.clone.1 | convolution fusion | flops 545259520 | bytes 9707520 | tf_op jit(solution)/shard_map/while/body/eval_jaxpr/hgrc,rhgd->chd/dot_general | solution.py:34
  80.2 3.2 %fusion.85 = bf16[4,512,1024]{1,2,0:T(8,128)(2,1)S(1)} fusion(f32[1024,512,4]{1,0,2:T(8,128)S(1)} %fusion.83, f32[4,512]{1,0:T(4,128)S(1)} %bitcast.131, f32[4,512]{1,0:T(4,128)S(1)} %copy-done.2, pred[512,1024]{0,1:T(8,128)(4,1)S(1)} %broadcast_compare_fusion.2, bf16[512,1,4,128]{0,3,2,1:T(8,128)(2,1)S(1)} %copy-done, ...), kind=kOutput, calls=%fused_computation.9.clone.1 | convolution fusion | flops 551550976 | bytes 13910020 | tf_op jit(solution)/shard_map/while/body/eval_jaxpr/rhgd,chd->hgrc/dot_general | solution.py:37
  83.3 1.5 %convolution_bitcast_fusion.3 = bf16[1024,128]{0,1:T(8,128)(2,1)S(1)} fusion(bf16[4,512,1024]{1,2,0:T(8,128)(2,1)S(1)} %fusion.85, bf16[512,1,4,128]{0,3,2,1:T(8,128)(2,1)S(1)} %get-tuple-element.475), kind=kOutput, calls=%fused_computation.15.clone.1 | convolution fusion | flops 536870912 | bytes 4980736 | tf_op jit(solution)/shard_map/while/body/eval_jaxpr/hgrc,rhgd->chd/dot_general | solution.py:46
  85.9 0.9 constant_dynamic-update-slice_fusion.2
  86.8 1.0 copy.38
  87.9 26.1 %reduce-scatter.2.cloned.1.call-done = bf16[512,256]{1,0:T(8,128)(2,1)} async-done(((bf16[2048,256]{1,0:T(8,128)(2,1)}), bf16[512,256]{1,0:T(8,128)(2,1)}) %reduce-scatter.2.cloned.1.call-update) | async-done | bytes 262160 | tf_op jit(solution)/shard_map/reduce_scatter | solution.py:109
  113.9 1.7 %fusion.54 = (bf16[512,128]{1,0:T(8,128)(2,1)}, bf16[512,128]{1,0:T(8,128)(2,1)}) fusion(bf16[512,256]{1,0:T(8,128)(2,1)} %reduce-scatter.2.cloned.1.call-done), kind=kLoop, calls=%fused_computation.93 | loop fusion | bytes 524288 | tf_op jit(solution)/shard_map/slice | solution.py:114
  (33 shorter events, 5.9 us)
Async XLA Ops:
  7.2 106.8 %reduce-scatter.2.cloned.1.call-start = ((), (), s32[]{:S(2)}) async-start(), calls=%async_computation.1 | async-start | bytes 1310720 | tf_op jit(solution)/shard_map/reduce_scatter | solution.py:109
  56.0 6.7 %copy-start = (bf16[512,1,4,128]{0,3,2,1:T(8,128)(2,1)S(1)}, bf16[512,1,4,128]{0,3,2,1:T(8,128)(2,1)}, u32[]{:S(2)}) copy-start(bf16[512,1,4,128]{0,3,2,1:T(8,128)(2,1)} %get-tuple-element.478) | copy-start | bytes 1572868 | tf_op jit(solution)/shard_map/while
  56.0 6.8 %copy-start.2 = (f32[4,512]{1,0:T(4,128)S(1)}, f32[4,512]{1,0:T(4,128)}, u32[]{:S(2)}) copy-start(f32[4,512]{1,0:T(4,128)} %get-tuple-element.476) | copy-start | bytes 24580 | tf_op jit(solution)/shard_map/while
  62.8 2.0 %copy-start.1 = (bf16[2048,128]{1,0:T(8,128)(2,1)S(1)}, bf16[2048,128]{1,0:T(8,128)(2,1)}, u32[]{:S(2)}) copy-start(bf16[2048,128]{1,0:T(8,128)(2,1)} %get-tuple-element.477) | copy-start | bytes 1572868 | tf_op jit(solution)/shard_map/while
  71.4 6.7 %copy-start = (bf16[512,1,4,128]{0,3,2,1:T(8,128)(2,1)S(1)}, bf16[512,1,4,128]{0,3,2,1:T(8,128)(2,1)}, u32[]{:S(2)}) copy-start(bf16[512,1,4,128]{0,3,2,1:T(8,128)(2,1)} %get-tuple-element.478) | copy-start | bytes 1572868 | tf_op jit(solution)/shard_map/while
  71.4 6.8 %copy-start.2 = (f32[4,512]{1,0:T(4,128)S(1)}, f32[4,512]{1,0:T(4,128)}, u32[]{:S(2)}) copy-start(f32[4,512]{1,0:T(4,128)} %get-tuple-element.476) | copy-start | bytes 24580 | tf_op jit(solution)/shard_map/while
  78.1 2.0 %copy-start.1 = (bf16[2048,128]{1,0:T(8,128)(2,1)S(1)}, bf16[2048,128]{1,0:T(8,128)(2,1)}, u32[]{:S(2)}) copy-start(bf16[2048,128]{1,0:T(8,128)(2,1)} %get-tuple-element.477) | copy-start | bytes 1572868 | tf_op jit(solution)/shard_map/while
Sparse Core Ops, SparseCore 0:
  86.9 26.9 reduce-scatter.1
where the time goes:
time: 123 us; the launch traced here: 122 us
  blocking collectives  35.3 us (29%)
  waiting for transfers between devices  26.1 us (21%)
  other arithmetic  17.4 us (14%)
  matrix products  17.4 us (14%)
  between operations  14.1 us (11%)
  local copies, waits for them, and re-layouts  12.1 us (10%)
    reduce_scatter x1, waiting for transfers between devices, shards(): lax.psum_scatter(grad_term.astype(jnp.bfloat16), 'ctx', scatter_dimension...  26.1 us
    all_gather x1, blocking collectives, shards(): lax.all_gather(values, 'ctx', axis=0, tiled=True)  17.7 us
    all_gather x1, blocking collectives, shards(): lax.all_gather(keys, 'ctx', axis=0, tiled=True)  17.6 us
    gather x6, other arithmetic, positions_of(): jnp.take(stretch_order, stretch_ids) * stretch_size + offsets % stretch_size  13.3 us
    dot_general x2, matrix products, tile_grads(): jnp.einsum('rhgd,chd->hgrc', grad_heads, value_heads, preferred_element_t...  6.33 us
    dot_general x2, matrix products, tile_grads(): jnp.einsum('hgrc,rhgd->chd', probs_low, grad_heads, preferred_element_typ...  3.99 us
    unnamed x2, local copies, waits for them, and re-layouts  3.3 us
    dot_general x2, matrix products, tile_grads(): jnp.einsum('hgrc,rhgd->chd', grad_scores, query_heads, preferred_element_...  2.94 us
  transfers between devices with their start and end apart: 1, of which 1 were waited for; matrix products, arithmetic and copies ran while one was open for 1% of the time, Pallas kernels for 0%

commit v1 on v0

v1 whole, which is shorter than its diff:
```python
import functools
import math

import jax
import jax.numpy as jnp
from jax import lax
from jax.experimental import pallas as pl
from jax.experimental.pallas import tpu as pltpu
from jax.sharding import PartitionSpec as P

HD = 128
SCALE = HD ** (-0.5)
LOG2E = math.log2(math.e)
F32 = jnp.float32
BF16 = jnp.bfloat16
VMEM_LIMIT = 48 * 1024 * 1024


def tile_terms(a, b, diagonal, key, value, key_t, qt, q, gt, g, norm, delta, dqt, dk, dv):
    size = key.shape[0]
    heads = norm.shape[0]
    for h in range(heads):
        cols = pl.ds(h * size, size)
        rows = pl.ds(a * size, size)
        lanes = pl.ds(h * HD, HD)
        scores = jnp.dot(key, qt[a, :, cols], preferred_element_type=F32)
        grad_probs = jnp.dot(value, gt[a, :, cols], preferred_element_type=F32)
        probs = jnp.exp2(scores * (SCALE * LOG2E) - norm[pl.ds(h, 1), rows] * LOG2E)
        if diagonal:
            key_at = lax.broadcasted_iota(jnp.int32, (size, size), 0)
            query_at = lax.broadcasted_iota(jnp.int32, (size, size), 1)
            probs = jnp.where(key_at <= query_at, probs, 0.0)
        grad_scores = (probs * (grad_probs - delta[pl.ds(h, 1), rows])).astype(BF16)
        dv[b] += jnp.dot(probs.astype(BF16), g[rows, lanes], preferred_element_type=F32)
        dk[b] += jnp.dot(grad_scores, q[rows, lanes], preferred_element_type=F32)
        dqt[a, :, cols] += jnp.dot(key_t, grad_scores, preferred_element_type=F32)


def own_kernel(order, q, g, o, k, v, norm, qt, gt, delta, dqt, dk, dv):
    me = lax.axis_index("ctx")
    size = q.shape[0] // 2
    heads = norm.shape[0]
    dqt[...] = jnp.zeros_like(dqt)
    dk[...] = jnp.zeros_like(dk)
    dv[...] = jnp.zeros_like(dv)
    for a in range(2):
        rows = pl.ds(a * size, size)
        for h in range(heads):
            lanes = pl.ds(h * HD, HD)
            cols = pl.ds(h * size, size)
            qt[a, :, cols] = q[rows, lanes].T
            grad = g[rows, lanes]
            gt[a, :, cols] = grad.T
            prod = grad.astype(F32) * o[rows, lanes].astype(F32)
            delta[pl.ds(h, 1), rows] = jnp.sum(prod.T, axis=0, keepdims=True)
    for b in range(2):
        rows = pl.ds(b * size, size)
        key, value = k[rows, :], v[rows, :]
        key_t = key.T
        for a in range(2):
            run = functools.partial(
                tile_terms, a, b, a == b, key, value, key_t, qt, q, gt, g, norm, delta, dqt, dk, dv
            )
            if a == b:
                run()
            else:
                pl.when(order[2 * me + b] < order[2 * me + a])(run)


def remote_kernel(partner, order, kv, q, g, qt, gt, norm, delta, dqt_in, dqt, part, dk, dv):
    me = lax.axis_index("ctx")
    other = partner(me)
    size = q.shape[0] // 2
    dqt[...] = dqt_in[...]
    dk[...] = jnp.zeros_like(dk)
    dv[...] = jnp.zeros_like(dv)
    for b in range(2):
        key = kv[pl.ds(b * size, size), :]
        value = kv[pl.ds((2 + b) * size, size), :]
        key_t = key.T
        for a in range(2):
            run = functools.partial(
                tile_terms, a, b, False, key, value, key_t, qt, q, gt, g, norm, delta, dqt, dk, dv
            )
            pl.when(order[2 * other + b] < order[2 * me + a])(run)
        part[pl.ds(b * size, size), :] = (dk[b] * SCALE).astype(BF16)
        part[pl.ds((2 + b) * size, size), :] = dv[b].astype(BF16)


def queries_kernel(dqt, dq):
    size = dq.shape[0] // 2
    for a in range(2):
        for h in range(dq.shape[1] // HD):
            tile = dqt[a, :, pl.ds(h * size, size)] * SCALE
            dq[pl.ds(a * size, size), pl.ds(h * HD, HD)] = tile.T.astype(BF16)


def sums_kernel(dk, dv, *refs):
    parts, (out_k, out_v) = refs[:-2], refs[-2:]
    size = dk.shape[1]
    for b in range(2):
        rows = pl.ds(b * size, size)
        key_sum, value_sum = dk[b] * SCALE, dv[b]
        for part in parts:
            key_sum += part[rows, :].astype(F32)
            value_sum += part[pl.ds((2 + b) * size, size), :].astype(F32)
        out_k[rows, :] = key_sum.astype(BF16)
        out_v[rows, :] = value_sum.astype(BF16)


SMEM = pl.BlockSpec(memory_space=pltpu.SMEM)
VMEM = pl.BlockSpec(memory_space=pltpu.VMEM)


def call(body, outs, n_in, smem=0, scratch=(), aliases=None, flops=0, moved=0):
    return pl.pallas_call(
        body,
        out_shape=[jax.ShapeDtypeStruct(s, t) for s, t in outs],
        in_specs=[SMEM] * smem + [VMEM] * (n_in - smem),
        out_specs=[VMEM] * len(outs),
        scratch_shapes=list(scratch),
        input_output_aliases=aliases or {},
        compiler_params=pltpu.CompilerParams(vmem_limit_bytes=VMEM_LIMIT),
        cost_estimate=pl.CostEstimate(flops=flops, bytes_accessed=moved, transcendentals=0),
    )


def partner_of(n, s):
    if n & (n - 1) == 0:
        return lambda i: i ^ s
    return lambda i: lax.rem(i + n - s, n) if not isinstance(i, int) else (i + n - s) % n


def shards(n, queries, keys, values, outputs, out_grads, log_norms, stretch_order):
    rows = queries.shape[0]
    size = rows // 2
    heads = queries.shape[1] // HD
    work = 5 * 2 * rows * rows * heads * HD
    kv = jnp.concatenate([keys, values], axis=0)
    partners = [partner_of(n, s) for s in range(1, n)]
    arrived = [lax.ppermute(kv, "ctx", [(p(i), i) for i in range(n)]) for p in partners]
    wide = (2, HD, heads * size)
    qt, gt, delta, dqt, dk, dv = call(
        own_kernel,
        [(wide, BF16), (wide, BF16), ((heads, rows), F32), (wide, F32), ((2, size, HD), F32), ((2, size, HD), F32)],
        7,
        smem=1,
        flops=work,
        moved=8 * rows * heads * HD,
    )(stretch_order, queries, out_grads, outputs, keys, values, log_norms)
    returned = []
    for p, got in zip(partners, arrived):
        dqt, part = call(
            functools.partial(remote_kernel, p),
            [(wide, F32), ((4 * size, HD), BF16)],
            9,
            smem=1,
            scratch=[pltpu.VMEM((2, size, HD), F32)] * 2,
            aliases={8: 0},
            flops=work,
            moved=8 * rows * heads * HD,
        )(stretch_order, got, queries, out_grads, qt, gt, log_norms, delta, dqt)
        returned.append(lax.ppermute(part, "ctx", [(i, p(i)) for i in range(n)]))
    (grad_queries,) = call(queries_kernel, [(queries.shape, BF16)], 1, moved=6 * rows * heads * HD)(dqt)
    grad_keys, grad_values = call(sums_kernel, [(keys.shape, BF16), (values.shape, BF16)], 2 + len(returned), moved=16 * rows * HD)(
        dk, dv, *returned
    )
    return grad_queries, grad_keys, grad_values


def solution(mesh):
    return jax.shard_map(
        functools.partial(shards, mesh.shape["ctx"]),
        mesh=mesh,
        in_specs=(
            P(("dp", "ctx"), "tp"),
            P(("dp", "ctx"), "tp"),
            P(("dp", "ctx"), "tp"),
            P(("dp", "ctx"), "tp"),
            P(("dp", "ctx"), "tp"),
            P("tp", ("dp", "ctx")),
            P("dp"),
        ),
        out_specs=(P(("dp", "ctx"), "tp"), P(("dp", "ctx"), "tp"), P(("dp", "ctx"), "tp")),
        check_vma=False,
    )
```

time: 123 us -> 56.5 us (0.46)
  blocking collectives: 35.3 us -> 0 us
  matrix products: 17.4 us -> 0 us
  Pallas kernels: 0 us -> 17.4 us
  other arithmetic: 17.4 us -> 0 us
  between operations: 14.1 us -> 0.75 us
  starting transfers between devices: 0.04 us -> 11.6 us
  local copies, waits for them, and re-layouts: 12.1 us -> 4.12 us
  waiting for transfers between devices: 26.1 us -> 22.2 us
    all_gather x2 -> x0, blocking collectives: 35.3 us -> none  [the longest x1 17.7 us: shards(): lax.all_gather(values, 'ctx', axis=0, tiled=True)]
    reduce_scatter x1 -> x0, waiting for transfers between devices: 26.1 us -> none  [shards(): lax.psum_scatter(grad_term.astype(jnp.bfloat16), 'ctx', scatter_dimension...]
    ppermute x0 -> x6, waiting for transfers between devices: none -> 22.2 us  [the longest x3 14.8 us: shards(): returned.append(lax.ppermute(part, 'ctx', [(i, p(i)) for i in range(n)]))]
    pallas_call x0 -> x6, Pallas kernels: none -> 17.4 us  [the longest x3 11.6 us: shards(): call(functools.partial(remote_kernel, p), [(wide, F32), ((4 * size, HD),...]
    dot_general x10 -> x0, matrix products: 17.4 us -> none  [the longest x2 6.33 us: tile_grads(): jnp.einsum('rhgd,chd->hgrc', grad_heads, value_heads, preferred_element_t...]
    gather x6 -> x0, other arithmetic: 13.3 us -> none  [positions_of(): jnp.take(stretch_order, stretch_ids) * stretch_size + offsets % stretch_size]
    ppermute x0 -> x6, starting transfers between devices: none -> 11.6 us  [the longest x3 5.94 us: shards(): returned.append(lax.ppermute(part, 'ctx', [(i, p(i)) for i in range(n)]))]
    convert_element_type x2 -> x0, local copies, waits for them, and re-layouts: 2.26 us -> none  [the longest x1 1.25 us: shards(): output_heads.astype(jnp.float32)]
  transfers between devices with their start and end apart: 1 -> 6, of which waited for: 1 -> 4; matrix products, arithmetic and copies ran while one was open for 1% -> 0% of each run, Pallas kernels for 0% -> 22%
where the time goes in v1:
time: 56.5 us; the launch traced here: 56.2 us
  waiting for transfers between devices  22.2 us (39%)
  Pallas kernels  17.4 us (31%)
  starting transfers between devices  11.6 us (21%)
  local copies, waits for them, and re-layouts  4.12 us (7%)
  between operations  0.75 us (1%)
    ppermute x3, waiting for transfers between devices, shards(): returned.append(lax.ppermute(part, 'ctx', [(i, p(i)) for i in range(n)]))  14.8 us
    pallas_call x3, Pallas kernels, shards(): call(functools.partial(remote_kernel, p), [(wide, F32), ((4 * size, HD),...  11.6 us
    ppermute x3, waiting for transfers between devices, shards(): lax.ppermute(kv, 'ctx', [(p(i), i) for i in range(n)])  7.39 us
    ppermute x3, starting transfers between devices, shards(): returned.append(lax.ppermute(part, 'ctx', [(i, p(i)) for i in range(n)]))  5.94 us
    ppermute x3, starting transfers between devices, shards(): lax.ppermute(kv, 'ctx', [(p(i), i) for i in range(n)])  5.68 us
    unnamed x15, local copies, waits for them, and re-layouts  4.1 us
    pallas_call x1, Pallas kernels, shards(): call(own_kernel, [(wide, BF16), (wide, BF16), ((heads, rows), F32), (wide...  4.05 us
  transfers between devices with their start and end apart: 6, of which 4 were waited for; matrix products, arithmetic and copies ran while one was open for 0% of the time, Pallas kernels for 22%

profile of v1, /device:TPU:0, one launch (start us, length us, event | category | flops | bytes accessed | tf_op | source)
XLA Modules:
  0.0 56.2 jit_solution(1543718931142568492)
XLA Ops:
  0.6 1.0 %constant_dynamic-update-slice_fusion.1 = bf16[1024,128]{1,0:T(8,128)(2,1)S(1)} fusion(bf16[512,128]{1,0:T(8,128)(2,1)} %k.1), kind=kLoop, calls=%fused_computation.1 | loop fusion | bytes 262144
  1.6 0.0 copy-done.1
  1.6 0.0 copy-start
  1.6 0.0 copy-start.5
  1.6 0.0 copy-start.6
  1.7 3.1 %collective-permute-start.2 = (bf16[1024,128]{1,0:T(8,128)(2,1)S(1)}, bf16[1024,128]{1,0:T(8,128)(2,1)S(1)}, u32[]{:S(2)}, u32[]{:S(2)}) collective-permute-start(bf16[1024,128]{1,0:T(8,128)(2,1)S(1)} %constant_dynamic-update-slice_fusion), channel_id=1, source_target_pairs={{8,0},{0,8},{24,16},{16,24},{9,1},{1,9},{25,17},{17,25},{10,2},{2,... | collective-permute-start | bytes 786440 | tf_op jit(solution)/shard_map/ppermute | solution.py:141
  4.8 2.6 %collective-permute-start.1 = (bf16[1024,128]{1,0:T(8,128)(2,1)S(1)}, bf16[1024,128]{1,0:T(8,128)(2,1)S(1)}, u32[]{:S(2)}, u32[]{:S(2)}) collective-permute-start(bf16[1024,128]{1,0:T(8,128)(2,1)S(1)} %constant_dynamic-update-slice_fusion), channel_id=1, source_target_pairs={{16,0},{24,8},{0,16},{8,24},{17,1},{25,9},{1,17},{9,25},{18,2},{26... | collective-permute-start | bytes 786440 | tf_op jit(solution)/shard_map/ppermute | solution.py:141
  7.4 0.0 copy-start.2
  7.4 1.0 %copy-done.2 = bf16[512,512]{1,0:T(8,128)(2,1)S(1)} copy-done((bf16[512,512]{1,0:T(8,128)(2,1)S(1)}, bf16[512,512]{1,0:T(8,128)(2,1)}, u32[]{:S(2)}) %copy-start.2) | copy-done | bytes 524312
  8.4 1.0 %copy-done.3 = bf16[512,512]{1,0:T(8,128)(2,1)S(1)} copy-done((bf16[512,512]{1,0:T(8,128)(2,1)S(1)}, bf16[512,512]{1,0:T(8,128)(2,1)}, u32[]{:S(2)}) %copy-start.3) | copy-done | bytes 524312
  9.5 1.0 %copy-done.4 = bf16[512,512]{1,0:T(8,128)(2,1)S(1)} copy-done((bf16[512,512]{1,0:T(8,128)(2,1)S(1)}, bf16[512,512]{1,0:T(8,128)(2,1)}, u32[]{:S(2)}) %copy-start.4) | copy-done | bytes 524312
  10.5 4.0 %shard_map.94 = (bf16[2,128,1024]{2,1,0:T(8,128)(2,1)S(1)}, bf16[2,128,1024]{2,1,0:T(8,128)(2,1)S(1)}, f32[4,512]{1,0:T(4,128)S(1)}, f32[2,128,1024]{2,1,0:T(8,1...) custom-call(s32[8]{0:T(128)S(1)} %copy-done.6, bf16[512,512]{1,0:T(8,128)(2,1)S(1)} %copy-done.3, ...), custom_call_target="tpu_custom_call" | custom-call | flops 1342177280 | bytes 2097152 | tf_op jit(solution)/shard_map/pallas_call | solution.py:143
  14.5 1.4 %collective-permute-done.2.kv = bf16[1024,128]{1,0:T(8,128)(2,1)S(1)} collective-permute-done((bf16[1024,128]{1,0:T(8,128)(2,1)S(1)}, bf16[1024,128]{1,0:T(8,128)(2,1)S(1)}, u32[]{:S(2)}, u32[]{:S(2)}) %collective-permute-start.2) | collective-permute-done | bytes 262176 | tf_op jit(solution)/shard_map/ppermute | solution.py:141
  15.9 4.2 %shard_map.95 = (f32[2,128,1024]{2,1,0:T(8,128)S(1)}, bf16[1024,128]{1,0:T(8,128)(2,1)S(1)}) custom-call(s32[8]{0:T(128)S(1)} %copy-done.6, bf16[1024,128]{1,0:T(8,128)(2,1)S(1)} %collective-permute-done.2.kv, bf16[512,512]{1,0:T(8,128)(2,1)S(1)} %copy-done.3, bf16[512,512]{1,0:T(8,128)(2,1)S(1)} %copy-done.4, ...), custom_call_target="tpu_custom_call", output_to_operand_aliasing={{0}: (8, {})} | custom-call | flops 1342177280 | bytes 2097152 | tf_op jit(solution)/shard_map/pallas_call | solution.py:153
  20.1 6.0 %collective-permute-done.1.kv = bf16[1024,128]{1,0:T(8,128)(2,1)S(1)} collective-permute-done((bf16[1024,128]{1,0:T(8,128)(2,1)S(1)}, bf16[1024,128]{1,0:T(8,128)(2,1)S(1)}, u32[]{:S(2)}, u32[]{:S(2)}) %collective-permute-start.1) | collective-permute-done | bytes 262176 | tf_op jit(solution)/shard_map/ppermute | solution.py:141
  26.1 3.2 %shard_map.96 = (f32[2,128,1024]{2,1,0:T(8,128)S(1)}, bf16[1024,128]{1,0:T(8,128)(2,1)S(1)}) custom-call(s32[8]{0:T(128)S(1)} %copy-done.6, bf16[1024,128]{1,0:T(8,128)(2,1)S(1)} %collective-permute-done.1.kv, bf16[512,512]{1,0:T(8,128)(2,1)S(1)} %copy-done.3, bf16[512,512]{1,0:T(8,128)(2,1)S(1)} %copy-done.4, ...), custom_call_target="tpu_custom_call", output_to_operand_aliasing={{0}: (8, {})} | custom-call | flops 1342177280 | bytes 2097152 | tf_op jit(solution)/shard_map/pallas_call | solution.py:153
  29.4 4.2 %shard_map.97 = (f32[2,128,1024]{2,1,0:T(8,128)S(1)}, bf16[1024,128]{1,0:T(8,128)(2,1)S(1)}) custom-call(s32[8]{0:T(128)S(1)} %copy-done.6, bf16[1024,128]{1,0:T(8,128)(2,1)S(1)} %collective-permute-done.kv, bf16[512,512]{1,0:T(8,128)(2,1)S(1)} %copy-done.3, bf16[512,512]{1,0:T(8,128)(2,1)S(1)} %copy-done.4, ...), custom_call_target="tpu_custom_call", output_to_operand_aliasing={{0}: (8, {})} | custom-call | flops 1342177280 | bytes 2097152 | tf_op jit(solution)/shard_map/pallas_call | solution.py:153
  33.6 1.4 %collective-permute-start.5 = (bf16[1024,128]{1,0:T(8,128)(2,1)S(1)}, bf16[1024,128]{1,0:T(8,128)(2,1)S(1)}, u32[]{:S(2)}, u32[]{:S(2)}) collective-permute-start(bf16[1024,128]{1,0:T(8,128)(2,1)S(1)} %get-tuple-element.28), channel_id=1, source_target_pairs={{0,24},{8,16},{16,8},{24,0},{1,25},{9,17},{17,9},{25,1},{2,26},{10... | collective-permute-start | bytes 786440 | tf_op jit(solution)/shard_map/ppermute | solution.py:163
  35.0 4.0 %collective-permute-start.4 = (bf16[1024,128]{1,0:T(8,128)(2,1)S(1)}, bf16[1024,128]{1,0:T(8,128)(2,1)S(1)}, u32[]{:S(2)}, u32[]{:S(2)}) collective-permute-start(bf16[1024,128]{1,0:T(8,128)(2,1)S(1)} %get-tuple-element.27), channel_id=1, source_target_pairs={{0,16},{8,24},{16,0},{24,8},{1,17},{9,25},{17,1},{25,9},{2,18},{10... | collective-permute-start | bytes 786440 | tf_op jit(solution)/shard_map/ppermute | solution.py:163
  39.0 0.5 collective-permute-start.3
  39.5 1.0 %shard_map.98 = bf16[512,512]{1,0:T(8,128)(2,1)} custom-call(f32[2,128,1024]{2,1,0:T(8,128)S(1)} %get-tuple-element.23.dqt), custom_call_target="tpu_custom_call" | custom-call | bytes 1572864 | tf_op jit(solution)/shard_map/pallas_call | solution.py:164
  40.5 4.1 %collective-permute-done.5.refs_2_ = bf16[1024,128]{1,0:T(8,128)(2,1)S(1)} collective-permute-done((bf16[1024,128]{1,0:T(8,128)(2,1)S(1)}, bf16[1024,128]{1,0:T(8,128)(2,1)S(1)}, u32[]{:S(2)}, u32[]{:S(2)}) %collective-permute-start.5) | collective-permute-done | bytes 262176 | tf_op jit(solution)/shard_map/ppermute | solution.py:163
  44.7 10.7 %collective-permute-done.4.refs_1_ = bf16[1024,128]{1,0:T(8,128)(2,1)S(1)} collective-permute-done((bf16[1024,128]{1,0:T(8,128)(2,1)S(1)}, bf16[1024,128]{1,0:T(8,128)(2,1)S(1)}, u32[]{:S(2)}, u32[]{:S(2)}) %collective-permute-start.4) | collective-permute-done | bytes 262176 | tf_op jit(solution)/shard_map/ppermute | solution.py:163
  55.3 0.8 %shard_map.99 = (bf16[512,128]{1,0:T(8,128)(2,1)}, bf16[512,128]{1,0:T(8,128)(2,1)}) custom-call(f32[2,256,128]{2,1,0:T(8,128)S(1)} %get-tuple-element.24.dk, f32[2,256,128]{2,1,0:T(8,128)S(1)} %get-tuple-element.25.dv, bf16[1024,128]{1,0:T(8,128)(2,1)S(1)} %collective-permute-done.3.refs_0_, bf16[1024,128]{1,0:T(8,128)(2,1)S(1)} %collective-permute-done.4.refs_1_, ...), custom_call_target="tpu_custom_call" | custom-call | bytes 1048576 | tf_op jit(solution)/shard_map/pallas_call | solution.py:165
  (10 shorter events, 0.0 us)
Async XLA Ops:
  0.6 1.0 %copy-start.1 = (bf16[512,128]{1,0:T(8,128)(2,1)S(1)}, bf16[512,128]{1,0:T(8,128)(2,1)}, u32[]{:S(2)}) copy-start(bf16[512,128]{1,0:T(8,128)(2,1)} %v.1) | copy-start | bytes 393220
  1.6 5.7 %copy-start = (bf16[512,128]{1,0:T(8,128)(2,1)S(1)}, bf16[512,128]{1,0:T(8,128)(2,1)}, u32[]{:S(2)}) copy-start(bf16[512,128]{1,0:T(8,128)(2,1)} %k.1) | copy-start | bytes 393220
  1.6 5.7 %copy-start.5 = (f32[4,512]{1,0:T(4,128)S(1)}, f32[4,512]{1,0:T(4,128)}, u32[]{:S(2)}) copy-start(f32[4,512]{1,0:T(4,128)} %norm.7) | copy-start | bytes 24580
  1.6 5.7 %copy-start.6 = (s32[8]{0:T(128)S(1)}, s32[8]{0:T(128)}, u32[]{:S(2)}) copy-start(s32[8]{0:T(128)} %order.7) | copy-start | bytes 100
  1.7 14.2 %collective-permute-start.2 = (bf16[1024,128]{1,0:T(8,128)(2,1)S(1)}, bf16[1024,128]{1,0:T(8,128)(2,1)S(1)}, u32[]{:S(2)}, u32[]{:S(2)}) collective-permute-start(bf16[1024,128]{1,0:T(8,128)(2,1)S(1)} %constant_dynamic-update-slice_fusion), channel_id=1, source_target_pairs={{8,0},{0,8},{24,16},{16,24},{9,1},{1,9},{25,17},{17,25},{10,2},{2,... | collective-permute-start | bytes 786440 | tf_op jit(solution)/shard_map/ppermute | solution.py:141
  4.8 21.4 %collective-permute-start.1 = (bf16[1024,128]{1,0:T(8,128)(2,1)S(1)}, bf16[1024,128]{1,0:T(8,128)(2,1)S(1)}, u32[]{:S(2)}, u32[]{:S(2)}) collective-permute-start(bf16[1024,128]{1,0:T(8,128)(2,1)S(1)} %constant_dynamic-update-slice_fusion), channel_id=1, source_target_pairs={{16,0},{24,8},{0,16},{8,24},{17,1},{25,9},{1,17},{9,25},{18,2},{26... | collective-permute-start | bytes 786440 | tf_op jit(solution)/shard_map/ppermute | solution.py:141
  7.3 22.0 %collective-permute-start = (bf16[1024,128]{1,0:T(8,128)(2,1)S(1)}, bf16[1024,128]{1,0:T(8,128)(2,1)S(1)}, u32[]{:S(2)}, u32[]{:S(2)}) collective-permute-start(bf16[1024,128]{1,0:T(8,128)(2,1)S(1)} %constant_dynamic-update-slice_fusion), channel_id=1, source_target_pairs={{24,0},{16,8},{8,16},{0,24},{25,1},{17,9},{9,17},{1,25},{26,2},{18... | collective-permute-start | bytes 786440 | tf_op jit(solution)/shard_map/ppermute | solution.py:141
  7.4 1.0 %copy-start.2 = (bf16[512,512]{1,0:T(8,128)(2,1)S(1)}, bf16[512,512]{1,0:T(8,128)(2,1)}, u32[]{:S(2)}) copy-start(bf16[512,512]{1,0:T(8,128)(2,1)} %o.1) | copy-start | bytes 1572868
  8.4 1.0 %copy-start.3 = (bf16[512,512]{1,0:T(8,128)(2,1)S(1)}, bf16[512,512]{1,0:T(8,128)(2,1)}, u32[]{:S(2)}) copy-start(bf16[512,512]{1,0:T(8,128)(2,1)} %q.7) | copy-start | bytes 1572868
  9.5 1.0 %copy-start.4 = (bf16[512,512]{1,0:T(8,128)(2,1)S(1)}, bf16[512,512]{1,0:T(8,128)(2,1)}, u32[]{:S(2)}) copy-start(bf16[512,512]{1,0:T(8,128)(2,1)} %g.7) | copy-start | bytes 1572868
  33.6 11.1 %collective-permute-start.5 = (bf16[1024,128]{1,0:T(8,128)(2,1)S(1)}, bf16[1024,128]{1,0:T(8,128)(2,1)S(1)}, u32[]{:S(2)}, u32[]{:S(2)}) collective-permute-start(bf16[1024,128]{1,0:T(8,128)(2,1)S(1)} %get-tuple-element.28), channel_id=1, source_target_pairs={{0,24},{8,16},{16,8},{24,0},{1,25},{9,17},{17,9},{25,1},{2,26},{10... | collective-permute-start | bytes 786440 | tf_op jit(solution)/shard_map/ppermute | solution.py:163
  35.0 20.4 %collective-permute-start.4 = (bf16[1024,128]{1,0:T(8,128)(2,1)S(1)}, bf16[1024,128]{1,0:T(8,128)(2,1)S(1)}, u32[]{:S(2)}, u32[]{:S(2)}) collective-permute-start(bf16[1024,128]{1,0:T(8,128)(2,1)S(1)} %get-tuple-element.27), channel_id=1, source_target_pairs={{0,16},{8,24},{16,0},{24,8},{1,17},{9,25},{17,1},{25,9},{2,18},{10... | collective-permute-start | bytes 786440 | tf_op jit(solution)/shard_map/ppermute | solution.py:163
  39.0 16.3 %collective-permute-start.3 = (bf16[1024,128]{1,0:T(8,128)(2,1)S(1)}, bf16[1024,128]{1,0:T(8,128)(2,1)S(1)}, u32[]{:S(2)}, u32[]{:S(2)}) collective-permute-start(bf16[1024,128]{1,0:T(8,128)(2,1)S(1)} %get-tuple-element.26), channel_id=1, source_target_pairs={{0,8},{8,0},{16,24},{24,16},{1,9},{9,1},{17,25},{25,17},{2,10},{10... | collective-permute-start | bytes 786440 | tf_op jit(solution)/shard_map/ppermute | solution.py:163

commit v2 on v1

--- a/solution.py
+++ b/solution.py
@@ -36,13 +36,21 @@
         dqt[a, :, cols] += jnp.dot(key_t, grad_scores, preferred_element_type=F32)
 
 
-def own_kernel(order, q, g, o, k, v, norm, qt, gt, delta, dqt, dk, dv):
+def own_kernel(order, kv, norm, q_hbm, g_hbm, o_hbm, q, g, qt, gt, delta, dqt, dk, dv, o, sems):
     me = lax.axis_index("ctx")
     size = q.shape[0] // 2
     heads = norm.shape[0]
+    loads = [
+        pltpu.make_async_copy(src, dst, sems.at[i])
+        for i, (src, dst) in enumerate(((q_hbm, q), (g_hbm, g), (o_hbm, o)))
+    ]
+    for load in loads:
+        load.start()
     dqt[...] = jnp.zeros_like(dqt)
     dk[...] = jnp.zeros_like(dk)
     dv[...] = jnp.zeros_like(dv)
+    for load in loads:
+        load.wait()
     for a in range(2):
         rows = pl.ds(a * size, size)
         for h in range(heads):
@@ -54,8 +62,8 @@
             prod = grad.astype(F32) * o[rows, lanes].astype(F32)
             delta[pl.ds(h, 1), rows] = jnp.sum(prod.T, axis=0, keepdims=True)
     for b in range(2):
-        rows = pl.ds(b * size, size)
-        key, value = k[rows, :], v[rows, :]
+        key = kv[pl.ds(b * size, size), :]
+        value = kv[pl.ds((2 + b) * size, size), :]
         key_t = key.T
         for a in range(2):
             run = functools.partial(
@@ -65,6 +73,7 @@
                 run()
             else:
                 pl.when(order[2 * me + b] < order[2 * me + a])(run)
+        dk[b] *= SCALE
 
 
 def remote_kernel(partner, order, kv, q, g, qt, gt, norm, delta, dqt_in, dqt, part, dk, dv):
@@ -99,30 +108,43 @@
     parts, (out_k, out_v) = refs[:-2], refs[-2:]
     size = dk.shape[1]
     for b in range(2):
-        rows = pl.ds(b * size, size)
-        key_sum, value_sum = dk[b] * SCALE, dv[b]
+        key_sum, value_sum = dk[b], dv[b]
         for part in parts:
-            key_sum += part[rows, :].astype(F32)
+            key_sum += part[pl.ds(b * size, size), :].astype(F32)
             value_sum += part[pl.ds((2 + b) * size, size), :].astype(F32)
-        out_k[rows, :] = key_sum.astype(BF16)
-        out_v[rows, :] = value_sum.astype(BF16)
+        if len(out_k.shape) == 3:
+            out_k[b] = key_sum
+            out_v[b] = value_sum
+        else:
+            out_k[pl.ds(b * size, size), :] = key_sum.astype(BF16)
+            out_v[pl.ds(b * size, size), :] = value_sum.astype(BF16)
+
+
+def token_kernel(x, *refs):
+    pass
 
 
 SMEM = pl.BlockSpec(memory_space=pltpu.SMEM)
 VMEM = pl.BlockSpec(memory_space=pltpu.VMEM)
-
-
-def call(body, outs, n_in, smem=0, scratch=(), aliases=None, flops=0, moved=0):
+ANY = pl.BlockSpec(memory_space=pl.ANY)
+HBM = pl.BlockSpec(memory_space=pltpu.HBM)
+
+
+def call(body, outs, in_specs, out_spec=VMEM, scratch=(), aliases=None, flops=0, moved=0):
     return pl.pallas_call(
         body,
         out_shape=[jax.ShapeDtypeStruct(s, t) for s, t in outs],
-        in_specs=[SMEM] * smem + [VMEM] * (n_in - smem),
-        out_specs=[VMEM] * len(outs),
+        in_specs=in_specs,
+        out_specs=[out_spec] * len(outs),
         scratch_shapes=list(scratch),
         input_output_aliases=aliases or {},
         compiler_params=pltpu.CompilerParams(vmem_limit_bytes=VMEM_LIMIT),
         cost_estimate=pl.CostEstimate(flops=flops, bytes_accessed=moved, transcendentals=0),
     )
+
+
+def after(x, *others):
+    return call(token_kernel, [(x.shape, x.dtype)], [ANY] * (1 + len(others)), out_spec=ANY, aliases={0: 0})(x, *others)[0]
 
 
 def partner_of(n, s):
@@ -137,34 +159,63 @@
     heads = queries.shape[1] // HD
     work = 5 * 2 * rows * rows * heads * HD
     kv = jnp.concatenate([keys, values], axis=0)
-    partners = [partner_of(n, s) for s in range(1, n)]
-    arrived = [lax.ppermute(kv, "ctx", [(p(i), i) for i in range(n)]) for p in partners]
     wide = (2, HD, heads * size)
-    qt, gt, delta, dqt, dk, dv = call(
-        own_kernel,
-        [(wide, BF16), (wide, BF16), ((heads, rows), F32), (wide, F32), ((2, size, HD), F32), ((2, size, HD), F32)],
-        7,
-        smem=1,
-        flops=work,
-        moved=8 * rows * heads * HD,
-    )(stretch_order, queries, out_grads, outputs, keys, values, log_norms)
-    returned = []
-    for p, got in zip(partners, arrived):
-        dqt, part = call(
-            functools.partial(remote_kernel, p),
-            [(wide, F32), ((4 * size, HD), BF16)],
-            9,
-            smem=1,
+    part_type = ((4 * size, HD), BF16)
+    sums_type = ((2, size, HD), F32)
+
+    def send(x, pairs):
+        return lax.ppermute(x, "ctx", pairs)
+
+    def own():
+        return call(
+            own_kernel,
+            [(queries.shape, BF16), (queries.shape, BF16), (wide, BF16), (wide, BF16),
+             ((heads, rows), F32), (wide, F32), sums_type, sums_type],
+            [SMEM, VMEM, VMEM, HBM, HBM, HBM],
+            scratch=[pltpu.VMEM(queries.shape, BF16), pltpu.SemaphoreType.DMA((3,))],
+            flops=work,
+        )(stretch_order, kv, log_norms, queries, out_grads, outputs)
+
+    def remote(partner, kv, q, g, qt, gt, delta, dqt):
+        return call(
+            functools.partial(remote_kernel, partner),
+            [(wide, F32), part_type],
+            [SMEM] + [VMEM] * 8,
             scratch=[pltpu.VMEM((2, size, HD), F32)] * 2,
             aliases={8: 0},
             flops=work,
-            moved=8 * rows * heads * HD,
-        )(stretch_order, got, queries, out_grads, qt, gt, log_norms, delta, dqt)
-        returned.append(lax.ppermute(part, "ctx", [(i, p(i)) for i in range(n)]))
-    (grad_queries,) = call(queries_kernel, [(queries.shape, BF16)], 1, moved=6 * rows * heads * HD)(dqt)
-    grad_keys, grad_values = call(sums_kernel, [(keys.shape, BF16), (values.shape, BF16)], 2 + len(returned), moved=16 * rows * HD)(
-        dk, dv, *returned
-    )
+        )(stretch_order, kv, q, g, qt, gt, log_norms, delta, dqt)
+
+    def sums(dk, dv, parts, outs):
+        return call(sums_kernel, outs, [VMEM] * (2 + len(parts)), moved=16 * rows * HD)(dk, dv, *parts)
+
+    last = [(keys.shape, BF16), (values.shape, BF16)]
+    if n == 4:
+        swap = [[(i, i ^ s) for i in range(n)] for s in range(n)]
+        kv_3 = send(kv, swap[3])
+        kv_1 = send(kv, swap[1])
+        q, g, qt, gt, delta, dqt, dk, dv = own()
+        same = (q, g, qt, gt, delta)
+        dqt, part_1 = remote(lambda i: i ^ 1, kv_1, *same, dqt)
+        back_1 = send(part_1, swap[1])
+        kv_3 = after(kv_3, part_1)
+        kv_2 = send(kv_3, swap[1])
+        dqt, part_3 = remote(lambda i: i ^ 3, kv_3, *same, dqt)
+        back_3 = send(part_3, swap[3])
+        dqt, part_2 = remote(lambda i: i ^ 2, kv_2, *same, dqt)
+        back_2 = send(part_2, swap[2])
+        dk, dv = sums(dk, dv, [back_1, back_3], [sums_type] * 2)
+        returned = [back_2]
+    else:
+        partners = [partner_of(n, s) for s in range(1, n)]
+        arrived = [send(kv, [(p(i), i) for i in range(n)]) for p in partners]
+        q, g, qt, gt, delta, dqt, dk, dv = own()
+        returned = []
+        for p, got in zip(partners, arrived):
+            dqt, part = remote(p, got, q, g, qt, gt, delta, dqt)
+            returned.append(send(part, [(i, p(i)) for i in range(n)]))
+    (grad_queries,) = call(queries_kernel, [(queries.shape, BF16)], [VMEM])(dqt)
+    grad_keys, grad_values = sums(dk, dv, returned, last)
     return grad_queries, grad_keys, grad_values
 
 

time: 56.5 us -> 50.5 us (0.89); the launches traced: 56.2 us -> 50.8 us
  waiting for transfers between devices: 22.2 us -> 16.4 us
  starting transfers between devices: 11.6 us -> 14.1 us
  Pallas kernels: 17.4 us -> 15.4 us
    ppermute x6, waiting for transfers between devices: 22.2 us -> 16.4 us  [send(): return lax.ppermute(x, 'ctx', pairs)]
    ppermute x6, starting transfers between devices: 11.6 us -> 14.1 us  [send(): return lax.ppermute(x, 'ctx', pairs)]
    pallas_call x6 -> x8, Pallas kernels: 17.4 us -> 15.4 us  [the longest x3 9.34 us: remote(): call(functools.partial(remote_kernel, partner), [(wide, F32), part_type],...]
    unnamed x15 -> x13, local copies, waits for them, and re-layouts: 4.1 us -> 4.09 us
  transfers between devices with their start and end apart: 6 -> 6, of which waited for: 4 -> 4; matrix products, arithmetic and copies ran while one was open for 0% -> 0% of each run, Pallas kernels for 22% -> 29%
where the time goes in v2:
time: 50.5 us; the launch traced here: 50.8 us
  waiting for transfers between devices  16.4 us (32%)
  Pallas kernels  15.4 us (30%)
  starting transfers between devices  14.1 us (28%)
  local copies, waits for them, and re-layouts  4.11 us (8%)
  between operations  0.72 us (1%)
    ppermute x6, waiting for transfers between devices, send(): return lax.ppermute(x, 'ctx', pairs)  16.4 us
    ppermute x6, starting transfers between devices, send(): return lax.ppermute(x, 'ctx', pairs)  14.1 us
    pallas_call x3, Pallas kernels, remote(): call(functools.partial(remote_kernel, partner), [(wide, F32), part_type],...  9.34 us
    pallas_call x1, Pallas kernels, own(): call(own_kernel, [(queries.shape, BF16), (queries.shape, BF16), (wide, BF...  4.25 us
    unnamed x13, local copies, waits for them, and re-layouts  4.09 us
  transfers between devices with their start and end apart: 6, of which 4 were waited for; matrix products, arithmetic and copies ran while one was open for 0% of the time, Pallas kernels for 29%

profile of v2, /device:TPU:0, one launch (start us, length us, event | category | flops | bytes accessed | tf_op | source)
XLA Modules:
  0.0 50.8 jit_solution(15360026233218717101)
XLA Ops:
  0.6 0.9 %constant_dynamic-update-slice_fusion.1 = bf16[1024,128]{1,0:T(8,128)(2,1)S(1)} fusion(bf16[512,128]{1,0:T(8,128)(2,1)} %param.8), kind=kLoop, calls=%fused_computation.1 | loop fusion | bytes 262144
  1.6 0.0 copy-done.5
  1.6 0.0 copy-start.3
  1.6 0.0 copy-start.4
  1.7 3.1 %collective-permute-start.1 = (bf16[1024,128]{1,0:T(8,128)(2,1)S(1)}, bf16[1024,128]{1,0:T(8,128)(2,1)S(1)}, u32[]{:S(2)}, u32[]{:S(2)}) collective-permute-start(bf16[1024,128]{1,0:T(8,128)(2,1)S(1)} %constant_dynamic-update-slice_fusion.kv), channel_id=1, source_target_pairs={{0,8},{8,0},{16,24},{24,16},{1,9},{9,1},{17,25},{25,17},{2,10},{10... | collective-permute-start | bytes 786440 | tf_op jit(solution)/shard_map/ppermute | solution.py:167
  4.7 2.5 %collective-permute-start = (bf16[1024,128]{1,0:T(8,128)(2,1)S(1)}, bf16[1024,128]{1,0:T(8,128)(2,1)S(1)}, u32[]{:S(2)}, u32[]{:S(2)}) collective-permute-start(bf16[1024,128]{1,0:T(8,128)(2,1)S(1)} %constant_dynamic-update-slice_fusion.kv), channel_id=1, source_target_pairs={{0,24},{8,16},{16,8},{24,0},{1,25},{9,17},{17,9},{25,1},{2,26},{10... | collective-permute-start | bytes 786440 | tf_op jit(solution)/shard_map/ppermute | solution.py:167
  7.2 1.0 %copy-done = bf16[512,512]{1,0:T(8,128)(2,1)S(1)} copy-done((bf16[512,512]{1,0:T(8,128)(2,1)S(1)}, bf16[512,512]{1,0:T(8,128)(2,1)}, u32[]{:S(2)}) %copy-start) | copy-done | bytes 524312
  8.3 1.0 %copy-done.1 = bf16[512,512]{1,0:T(8,128)(2,1)S(1)} copy-done((bf16[512,512]{1,0:T(8,128)(2,1)S(1)}, bf16[512,512]{1,0:T(8,128)(2,1)}, u32[]{:S(2)}) %copy-start.1) | copy-done | bytes 524312
  9.3 1.0 %copy-done.2 = bf16[512,512]{1,0:T(8,128)(2,1)S(1)} copy-done((bf16[512,512]{1,0:T(8,128)(2,1)S(1)}, bf16[512,512]{1,0:T(8,128)(2,1)}, u32[]{:S(2)}) %copy-start.2) | copy-done | bytes 524312
  10.4 4.2 %shard_map.94 = (bf16[512,512]{1,0:T(8,128)(2,1)S(1)}, bf16[512,512]{1,0:T(8,128)(2,1)S(1)}, bf16[2,128,1024]{2,1,0:T(8,128)(2,1)S(1)}, bf16[2,128,1024]{2,1,0:T...) custom-call(s32[8]{0:T(128)S(1)} %copy-done.4, ...), custom_call_target="tpu_custom_call" | custom-call | flops 1342177280 | tf_op jit(solution)/shard_map/pallas_call | solution.py:170
  14.6 4.2 %shard_map.95 = (f32[2,128,1024]{2,1,0:T(8,128)S(1)}, bf16[1024,128]{1,0:T(8,128)(2,1)S(1)}) custom-call(s32[8]{0:T(128)S(1)} %copy-done.4, bf16[1024,128]{1,0:T(8,128)(2,1)S(1)} %collective-permute-done.1.kv, bf16[512,512]{1,0:T(8,128)(2,1)S(1)} %get-tuple-element.21.q, bf16[512,512]{1,0:T(8,128)(2,1)S(1)} %get-tuple-element.22.g, ...), custom_call_target="tpu_custom_call", output_to_operand_aliasing={{0}: (8, {})} | custom-call | flops 1342177280 | tf_op jit(solution)/shard_map/pallas_call | solution.py:180
  18.8 0.2 collective-permute-done.x
  19.0 0.6 %collective-permute-start.2 = (bf16[1024,128]{1,0:T(8,128)(2,1)S(1)}, bf16[1024,128]{1,0:T(8,128)(2,1)S(1)}, u32[]{:S(2)}, u32[]{:S(2)}) collective-permute-start(bf16[1024,128]{1,0:T(8,128)(2,1)S(1)} %shard_map.96.kv), channel_id=1, source_target_pairs={{0,8},{8,0},{16,24},{24,16},{1,9},{9,1},{17,25},{25,17},{2,10},{10... | collective-permute-start | bytes 786440 | tf_op jit(solution)/shard_map/ppermute | solution.py:167
  19.6 1.4 %collective-permute-start.3 = (bf16[1024,128]{1,0:T(8,128)(2,1)S(1)}, bf16[1024,128]{1,0:T(8,128)(2,1)S(1)}, u32[]{:S(2)}, u32[]{:S(2)}) collective-permute-start(bf16[1024,128]{1,0:T(8,128)(2,1)S(1)} %get-tuple-element.27.refs_0_), channel_id=1, source_target_pairs={{0,8},{8,0},{16,24},{24,16},{1,9},{9,1},{17,25},{25,17},{2,10},{10... | collective-permute-start | bytes 786440 | tf_op jit(solution)/shard_map/ppermute | solution.py:167
  21.0 3.2 %shard_map.97 = (f32[2,128,1024]{2,1,0:T(8,128)S(1)}, bf16[1024,128]{1,0:T(8,128)(2,1)S(1)}) custom-call(s32[8]{0:T(128)S(1)} %copy-done.4, bf16[1024,128]{1,0:T(8,128)(2,1)S(1)} %shard_map.96.kv, bf16[512,512]{1,0:T(8,128)(2,1)S(1)} %get-tuple-element.21.q, bf16[512,512]{1,0:T(8,128)(2,1)S(1)} %get-tuple-element.22.g, ...), custom_call_target="tpu_custom_call", output_to_operand_aliasing={{0}: (8, {})} | custom-call | flops 1342177280 | tf_op jit(solution)/shard_map/pallas_call | solution.py:180
  24.2 2.5 %collective-permute-start.4 = (bf16[1024,128]{1,0:T(8,128)(2,1)S(1)}, bf16[1024,128]{1,0:T(8,128)(2,1)S(1)}, u32[]{:S(2)}, u32[]{:S(2)}) collective-permute-start(bf16[1024,128]{1,0:T(8,128)(2,1)S(1)} %get-tuple-element.33), channel_id=1, source_target_pairs={{0,24},{8,16},{16,8},{24,0},{1,25},{9,17},{17,9},{25,1},{2,26},{10... | collective-permute-start | bytes 786440 | tf_op jit(solution)/shard_map/ppermute | solution.py:167
  26.7 1.5 %collective-permute-done.2.kv = bf16[1024,128]{1,0:T(8,128)(2,1)S(1)} collective-permute-done((bf16[1024,128]{1,0:T(8,128)(2,1)S(1)}, bf16[1024,128]{1,0:T(8,128)(2,1)S(1)}, u32[]{:S(2)}, u32[]{:S(2)}) %collective-permute-start.2) | collective-permute-done | bytes 262176 | tf_op jit(solution)/shard_map/ppermute | solution.py:167
  28.2 1.9 %shard_map.98 = (f32[2,128,1024]{2,1,0:T(8,128)S(1)}, bf16[1024,128]{1,0:T(8,128)(2,1)S(1)}) custom-call(s32[8]{0:T(128)S(1)} %copy-done.4, bf16[1024,128]{1,0:T(8,128)(2,1)S(1)} %collective-permute-done.2.kv, bf16[512,512]{1,0:T(8,128)(2,1)S(1)} %get-tuple-element.21.q, bf16[512,512]{1,0:T(8,128)(2,1)S(1)} %get-tuple-element.22.g, ...), custom_call_target="tpu_custom_call", output_to_operand_aliasing={{0}: (8, {})} | custom-call | flops 1342177280 | tf_op jit(solution)/shard_map/pallas_call | solution.py:180
  30.2 4.0 %collective-permute-start.5 = (bf16[1024,128]{1,0:T(8,128)(2,1)S(1)}, bf16[1024,128]{1,0:T(8,128)(2,1)S(1)}, u32[]{:S(2)}, u32[]{:S(2)}) collective-permute-start(bf16[1024,128]{1,0:T(8,128)(2,1)S(1)} %get-tuple-element.36), channel_id=1, source_target_pairs={{0,16},{8,24},{16,0},{24,8},{1,17},{9,25},{17,1},{25,9},{2,18},{10... | collective-permute-start | bytes 786440 | tf_op jit(solution)/shard_map/ppermute | solution.py:167
  34.2 1.0 %shard_map.99 = bf16[512,512]{1,0:T(8,128)(2,1)} custom-call(f32[2,128,1024]{2,1,0:T(8,128)S(1)} %get-tuple-element.30.dqt), custom_call_target="tpu_custom_call" | custom-call | tf_op jit(solution)/shard_map/pallas_call | solution.py:217
  35.2 5.5 %collective-permute-done.4.refs_1_ = bf16[1024,128]{1,0:T(8,128)(2,1)S(1)} collective-permute-done((bf16[1024,128]{1,0:T(8,128)(2,1)S(1)}, bf16[1024,128]{1,0:T(8,128)(2,1)S(1)}, u32[]{:S(2)}, u32[]{:S(2)}) %collective-permute-start.4) | collective-permute-done | bytes 262176 | tf_op jit(solution)/shard_map/ppermute | solution.py:167
  40.7 0.1 shard_map.100
  40.8 9.2 %collective-permute-done.5.refs_0_ = bf16[1024,128]{1,0:T(8,128)(2,1)S(1)} collective-permute-done((bf16[1024,128]{1,0:T(8,128)(2,1)S(1)}, bf16[1024,128]{1,0:T(8,128)(2,1)S(1)}, u32[]{:S(2)}, u32[]{:S(2)}) %collective-permute-start.5) | collective-permute-done | bytes 262176 | tf_op jit(solution)/shard_map/ppermute | solution.py:167
  50.0 0.7 %shard_map.101 = (bf16[512,128]{1,0:T(8,128)(2,1)}, bf16[512,128]{1,0:T(8,128)(2,1)}) custom-call(f32[2,256,128]{2,1,0:T(8,128)S(1)} %get-tuple-element.34.dk, f32[2,256,128]{2,1,0:T(8,128)S(1)} %get-tuple-element.35.dv, bf16[1024,128]{1,0:T(8,128)(2,1)S(1)} %collective-permute-done.5.refs_0_), custom_call_target="tpu_custom_call" | custom-call | bytes 1048576 | tf_op jit(solution)/shard_map/pallas_call | solution.py:190
  (10 shorter events, 0.0 us)
Async XLA Ops:
  0.6 1.0 %copy-start.5 = (bf16[512,128]{1,0:T(8,128)(2,1)S(1)}, bf16[512,128]{1,0:T(8,128)(2,1)}, u32[]{:S(2)}) copy-start(bf16[512,128]{1,0:T(8,128)(2,1)} %param.9) | copy-start | bytes 393220
  1.6 5.6 %copy-start.3 = (f32[4,512]{1,0:T(4,128)S(1)}, f32[4,512]{1,0:T(4,128)}, u32[]{:S(2)}) copy-start(f32[4,512]{1,0:T(4,128)} %norm.7) | copy-start | bytes 24580
  1.6 5.6 %copy-start.4 = (s32[8]{0:T(128)S(1)}, s32[8]{0:T(128)}, u32[]{:S(2)}) copy-start(s32[8]{0:T(128)} %order.7) | copy-start | bytes 100
  1.7 13.0 %collective-permute-start.1 = (bf16[1024,128]{1,0:T(8,128)(2,1)S(1)}, bf16[1024,128]{1,0:T(8,128)(2,1)S(1)}, u32[]{:S(2)}, u32[]{:S(2)}) collective-permute-start(bf16[1024,128]{1,0:T(8,128)(2,1)S(1)} %constant_dynamic-update-slice_fusion.kv), channel_id=1, source_target_pairs={{0,8},{8,0},{16,24},{24,16},{1,9},{9,1},{17,25},{25,17},{2,10},{10... | collective-permute-start | bytes 786440 | tf_op jit(solution)/shard_map/ppermute | solution.py:167
  4.7 14.2 %collective-permute-start = (bf16[1024,128]{1,0:T(8,128)(2,1)S(1)}, bf16[1024,128]{1,0:T(8,128)(2,1)S(1)}, u32[]{:S(2)}, u32[]{:S(2)}) collective-permute-start(bf16[1024,128]{1,0:T(8,128)(2,1)S(1)} %constant_dynamic-update-slice_fusion.kv), channel_id=1, source_target_pairs={{0,24},{8,16},{16,8},{24,0},{1,25},{9,17},{17,9},{25,1},{2,26},{10... | collective-permute-start | bytes 786440 | tf_op jit(solution)/shard_map/ppermute | solution.py:167
  7.2 1.0 %copy-start = (bf16[512,512]{1,0:T(8,128)(2,1)S(1)}, bf16[512,512]{1,0:T(8,128)(2,1)}, u32[]{:S(2)}) copy-start(bf16[512,512]{1,0:T(8,128)(2,1)} %q_hbm.1) | copy-start | bytes 1572868
  8.3 1.0 %copy-start.1 = (bf16[512,512]{1,0:T(8,128)(2,1)S(1)}, bf16[512,512]{1,0:T(8,128)(2,1)}, u32[]{:S(2)}) copy-start(bf16[512,512]{1,0:T(8,128)(2,1)} %g_hbm.1) | copy-start | bytes 1572868
  9.3 1.0 %copy-start.2 = (bf16[512,512]{1,0:T(8,128)(2,1)S(1)}, bf16[512,512]{1,0:T(8,128)(2,1)}, u32[]{:S(2)}) copy-start(bf16[512,512]{1,0:T(8,128)(2,1)} %o_hbm.1) | copy-start | bytes 1572868
  19.0 9.2 %collective-permute-start.2 = (bf16[1024,128]{1,0:T(8,128)(2,1)S(1)}, bf16[1024,128]{1,0:T(8,128)(2,1)S(1)}, u32[]{:S(2)}, u32[]{:S(2)}) collective-permute-start(bf16[1024,128]{1,0:T(8,128)(2,1)S(1)} %shard_map.96.kv), channel_id=1, source_target_pairs={{0,8},{8,0},{16,24},{24,16},{1,9},{9,1},{17,25},{25,17},{2,10},{10... | collective-permute-start | bytes 786440 | tf_op jit(solution)/shard_map/ppermute | solution.py:167
  19.6 21.2 %collective-permute-start.3 = (bf16[1024,128]{1,0:T(8,128)(2,1)S(1)}, bf16[1024,128]{1,0:T(8,128)(2,1)S(1)}, u32[]{:S(2)}, u32[]{:S(2)}) collective-permute-start(bf16[1024,128]{1,0:T(8,128)(2,1)S(1)} %get-tuple-element.27.refs_0_), channel_id=1, source_target_pairs={{0,8},{8,0},{16,24},{24,16},{1,9},{9,1},{17,25},{25,17},{2,10},{10... | collective-permute-start | bytes 786440 | tf_op jit(solution)/shard_map/ppermute | solution.py:167
  24.2 16.5 %collective-permute-start.4 = (bf16[1024,128]{1,0:T(8,128)(2,1)S(1)}, bf16[1024,128]{1,0:T(8,128)(2,1)S(1)}, u32[]{:S(2)}, u32[]{:S(2)}) collective-permute-start(bf16[1024,128]{1,0:T(8,128)(2,1)S(1)} %get-tuple-element.33), channel_id=1, source_target_pairs={{0,24},{8,16},{16,8},{24,0},{1,25},{9,17},{17,9},{25,1},{2,26},{10... | collective-permute-start | bytes 786440 | tf_op jit(solution)/shard_map/ppermute | solution.py:167
  30.2 19.9 %collective-permute-start.5 = (bf16[1024,128]{1,0:T(8,128)(2,1)S(1)}, bf16[1024,128]{1,0:T(8,128)(2,1)S(1)}, u32[]{:S(2)}, u32[]{:S(2)}) collective-permute-start(bf16[1024,128]{1,0:T(8,128)(2,1)S(1)} %get-tuple-element.36), channel_id=1, source_target_pairs={{0,16},{8,24},{16,0},{24,8},{1,17},{9,25},{17,1},{25,9},{2,18},{10... | collective-permute-start | bytes 786440 | tf_op jit(solution)/shard_map/ppermute | solution.py:167

commit v3 on v2

v3 whole, which is shorter than its diff:
```python
import functools
import math

import jax
import jax.numpy as jnp
from jax import lax
from jax.experimental import pallas as pl
from jax.experimental.pallas import tpu as pltpu
from jax.sharding import PartitionSpec as P

HD = 128
SCALE = HD ** (-0.5)
LOG2E = math.log2(math.e)
F32 = jnp.float32
BF16 = jnp.bfloat16
VMEM_LIMIT = 48 * 1024 * 1024


def low_terms(start, width, key, value, state, diagonal, ps, ds):
    _, _, qt, gt, norm, delta = state
    size = key.shape[0]
    for at in range(0, width, size):
        cols = pl.ds(start + at, size)
        scores = jnp.dot(key, qt[:, cols], preferred_element_type=F32)
        grad_probs = jnp.dot(value, gt[:, cols], preferred_element_type=F32)
        probs = jnp.exp2(scores * (SCALE * LOG2E) - norm[:, cols])
        if diagonal:
            key_at = lax.broadcasted_iota(jnp.int32, probs.shape, 0)
            query_at = lax.broadcasted_iota(jnp.int32, probs.shape, 1)
            probs = jnp.where(key_at <= query_at, probs, 0.0)
        ps[:, at : at + size] = probs.astype(BF16)
        ds[:, at : at + size] = (probs * (grad_probs - delta[:, cols])).astype(BF16)


def key_terms(start, width, state, ps, ds):
    q4, g4 = state[:2]
    rows = pl.ds(start, width)
    grad_key = jnp.dot(ds[:, :width], q4[rows, :], preferred_element_type=F32)
    grad_value = jnp.dot(ps[:, :width], g4[rows, :], preferred_element_type=F32)
    return grad_key * SCALE, grad_value


def own_kernel(order, kv, log_norms, q, g, o, kv_out, q4, g4, qt, gt, norm, delta, dqt, dk, dv, ps, ds):
    me = lax.axis_index("ctx")
    size = q.shape[0] // 2
    heads = log_norms.shape[0]
    width = heads * size
    kv_out[...] = kv[...]
    for a in range(2):
        rows = pl.ds(a * size, size)
        for h in range(heads):
            lanes = pl.ds(h * HD, HD)
            cols = pl.ds(a * width + h * size, size)
            query, grad = q[rows, lanes], g[rows, lanes]
            q4[cols, :] = query
            g4[cols, :] = grad
            qt[:, cols] = query.T
            gt[:, cols] = grad.T
            prod = grad.astype(F32) * o[rows, lanes].astype(F32)
            delta[:, cols] = jnp.sum(prod.T, axis=0, keepdims=True)
            norm[:, cols] = log_norms[pl.ds(h, 1), rows] * LOG2E
    state = (q4, g4, qt, gt, norm, delta)
    for a in range(2):
        key, value = kv[pl.ds(2 * a * size, size), :], kv[pl.ds((2 * a + 1) * size, size), :]
        rows, cols = pl.ds(a * size, size), pl.ds(a * width, width)
        low_terms(a * width, width, key, value, state, True, ps, ds)
        dk[rows, :], dv[rows, :] = key_terms(a * width, width, state, ps, ds)
        dqt[:, cols] = jnp.dot(key.T, ds[...], preferred_element_type=F32)
    late = (order[2 * me] < order[2 * me + 1]).astype(jnp.int32)
    start = pl.multiple_of(late * width, width)
    key_at = pl.multiple_of((1 - late) * 2 * size, size)
    key, value = kv[pl.ds(key_at, size), :], kv[pl.ds(key_at + size, size), :]
    low_terms(start, width, key, value, state, False, ps, ds)
    rows = pl.ds(pl.multiple_of((1 - late) * size, size), size)
    grad_key, grad_value = key_terms(start, width, state, ps, ds)
    dk[rows, :] += grad_key
    dv[rows, :] += grad_value
    dqt[:, pl.ds(start, width)] += jnp.dot(key.T, ds[...], preferred_element_type=F32)


def remote_kernel(partner, first, order, kv, q4, g4, qt, gt, norm, delta, dqt_in, dqt, part, ps, ds):
    me = lax.axis_index("ctx")
    other = partner(me)
    total = q4.shape[0]
    width = total // 2
    size = ps.shape[0]
    state = (q4, g4, qt, gt, norm, delta)
    for b in range(kv.shape[0] // (2 * size)):
        keys_at, values_at = pl.ds(2 * b * size, size), pl.ds((2 * b + 1) * size, size)
        before = dqt_in if b == 0 else dqt
        sees = [order[2 * other + first + b] < order[2 * me + a] for a in range(2)]
        count = sees[0].astype(jnp.int32) + sees[1].astype(jnp.int32)

        def some(start, span):
            key, value = kv[keys_at, :], kv[values_at, :]
            low_terms(start, span, key, value, state, False, ps, ds)
            grad_key, grad_value = key_terms(start, span, state, ps, ds)
            part[keys_at, :] = grad_key.astype(BF16)
            part[values_at, :] = grad_value.astype(BF16)
            cols = pl.ds(start, span)
            dqt[:, cols] = before[:, cols] + jnp.dot(key.T, ds[:, :span], preferred_element_type=F32)

        @pl.when(count == 2)
        def _():
            some(0, total)

        @pl.when(count == 1)
        def _():
            seeing = sees[1].astype(jnp.int32)
            some(pl.multiple_of(seeing * width, width), width)
            if b == 0:
                rest = pl.ds(pl.multiple_of((1 - seeing) * width, width), width)
                dqt[:, rest] = dqt_in[:, rest]

        @pl.when(count == 0)
        def _():
            part[keys_at, :] = jnp.zeros((size, HD), BF16)
            part[values_at, :] = jnp.zeros((size, HD), BF16)
            if b == 0:
                dqt[...] = dqt_in[...]


def queries_kernel(dqt, dq):
    size = dq.shape[0] // 2
    heads = dq.shape[1] // HD
    for a in range(2):
        for h in range(heads):
            tile = dqt[:, pl.ds((a * heads + h) * size, size)] * SCALE
            dq[pl.ds(a * size, size), pl.ds(h * HD, HD)] = tile.T.astype(BF16)


def sums_kernel(dk, dv, *refs):
    parts, (out_k, out_v) = refs[:-2], refs[-2:]
    size = dk.shape[0] // 2
    for b in range(2):
        rows = pl.ds(b * size, size)
        key_sum, value_sum = dk[rows, :], dv[rows, :]
        for part in parts:
            key_sum += part[pl.ds(2 * b * size, size), :].astype(F32)
            value_sum += part[pl.ds((2 * b + 1) * size, size), :].astype(F32)
        out_k[rows, :] = key_sum.astype(out_k.dtype)
        out_v[rows, :] = value_sum.astype(out_v.dtype)


def token_kernel(x, *refs):
    pass


SMEM = pl.BlockSpec(memory_space=pltpu.SMEM)
VMEM = pl.BlockSpec(memory_space=pltpu.VMEM)
ANY = pl.BlockSpec(memory_space=pl.ANY)


def call(body, outs, in_specs, out_spec=VMEM, scratch=(), aliases=None, flops=0, moved=0):
    return pl.pallas_call(
        body,
        out_shape=[jax.ShapeDtypeStruct(s, t) for s, t in outs],
        in_specs=in_specs,
        out_specs=[out_spec] * len(outs),
        scratch_shapes=list(scratch),
        input_output_aliases=aliases or {},
        compiler_params=pltpu.CompilerParams(vmem_limit_bytes=VMEM_LIMIT),
        cost_estimate=pl.CostEstimate(flops=flops, bytes_accessed=moved, transcendentals=0),
    )


def after(x, *others):
    return call(token_kernel, [(x.shape, x.dtype)], [ANY] * (1 + len(others)), out_spec=ANY, aliases={0: 0})(x, *others)[0]


def partner_of(n, s):
    if n & (n - 1) == 0:
        return lambda i: i ^ s
    return lambda i: lax.rem(i + n - s, n) if not isinstance(i, int) else (i + n - s) % n


def shards(n, queries, keys, values, outputs, out_grads, log_norms, stretch_order):
    rows = queries.shape[0]
    size = rows // 2
    heads = queries.shape[1] // HD
    work = 5 * 2 * rows * rows * heads * HD
    total = 2 * heads * size
    wide = (HD, total)
    tall = (total, HD)
    line = (1, total)
    whole_type = ((4 * size, HD), BF16)
    sums_type = ((rows, HD), F32)

    def send(x, pairs):
        return lax.ppermute(x, "ctx", pairs)

    def own(kv):
        return call(
            own_kernel,
            [whole_type, (tall, BF16), (tall, BF16), (wide, BF16), (wide, BF16), (line, F32), (line, F32), (wide, F32), sums_type, sums_type],
            [SMEM] + [VMEM] * 5,
            scratch=[pltpu.VMEM((size, heads * size), BF16)] * 2,
            flops=work,
        )(stretch_order, kv, log_norms, queries, out_grads, outputs)

    def remote(partner, first, kv, *state):
        return call(
            functools.partial(remote_kernel, partner, first),
            [(wide, F32), (kv.shape, BF16)],
            [SMEM] + [VMEM] * 8,
            scratch=[pltpu.VMEM((size, total), BF16)] * 2,
            aliases={8: 0},
            flops=work * kv.shape[0] // (4 * size),
        )(stretch_order, kv, *state)

    def sums(dk, dv, parts, outs):
        return call(sums_kernel, outs, [VMEM] * (2 + len(parts)), moved=16 * rows * HD)(dk, dv, *parts)

    last = [(keys.shape, BF16), (values.shape, BF16)]
    kv = jnp.concatenate([keys[:size], values[:size], keys[size:], values[size:]], axis=0)
    if n == 4:
        swap = [[(i, i ^ s) for i in range(n)] for s in range(n)]
        kv_3 = send(kv, swap[3])
        kv, *same, dqt, dk, dv = own(kv)
        kv_1 = send(kv, swap[1])
        kv_3 = after(kv_3, dk)
        kv_2 = send(kv_3, swap[1])
        dqt, part_3 = remote(lambda i: i ^ 3, 0, kv_3, *same, dqt)
        back_3 = send(part_3, swap[3])
        kv_1 = after(kv_1, part_3)
        dqt, part_1 = remote(lambda i: i ^ 1, 0, kv_1, *same, dqt)
        back_1 = send(part_1, swap[1])
        dqt, part_2 = remote(lambda i: i ^ 2, 0, kv_2, *same, dqt)
        back_2 = send(part_2, swap[2])
        dk, dv = sums(dk, dv, [back_3, back_1], [sums_type] * 2)
        returned = [back_2]
    else:
        kv, *same, dqt, dk, dv = own(kv)
        partners = [partner_of(n, s) for s in range(1, n)]
        arrived = [send(kv, [(p(i), i) for i in range(n)]) for p in partners]
        returned = []
        for p, got in zip(partners, arrived):
            dqt, part = remote(p, 0, got, *same, dqt)
            returned.append(send(part, [(i, p(i)) for i in range(n)]))
    (grad_queries,) = call(queries_kernel, [(queries.shape, BF16)], [VMEM])(dqt)
    grad_keys, grad_values = sums(dk, dv, returned, last)
    return grad_queries, grad_keys, grad_values


def solution(mesh):
    return jax.shard_map(
        functools.partial(shards, mesh.shape["ctx"]),
        mesh=mesh,
        in_specs=(
            P(("dp", "ctx"), "tp"),
            P(("dp", "ctx"), "tp"),
            P(("dp", "ctx"), "tp"),
            P(("dp", "ctx"), "tp"),
            P(("dp", "ctx"), "tp"),
            P("tp", ("dp", "ctx")),
            P("dp"),
        ),
        out_specs=(P(("dp", "ctx"), "tp"), P(("dp", "ctx"), "tp"), P(("dp", "ctx"), "tp")),
        check_vma=False,
    )
```

time: 50.5 us -> 46.1 us (0.913); the launches traced: 50.8 us -> 45.7 us
  Pallas kernels: 15.4 us -> 7.94 us
  starting transfers between devices: 14.1 us -> 20.3 us
  waiting for transfers between devices: 16.4 us -> 13.9 us
  local copies, waits for them, and re-layouts: 4.11 us -> 2.79 us
    pallas_call x4, Pallas kernels: 13.6 us -> 6.1 us  [the longest x3 3.22 us: remote(): call(functools.partial(remote_kernel, partner, first), [(wide, F32), (kv....]
    ppermute x6, starting transfers between devices: 14.1 us -> 20.3 us  [send(): return lax.ppermute(x, 'ctx', pairs)]
    ppermute x6, waiting for transfers between devices: 16.4 us -> 13.9 us  [send(): return lax.ppermute(x, 'ctx', pairs)]
    unnamed x13 -> x10, local copies, waits for them, and re-layouts: 4.09 us -> 1.75 us
    slice x0 -> x1, local copies, waits for them, and re-layouts: none -> 1.04 us  [shards(): keys[:size]]
  transfers between devices with their start and end apart: 6 -> 6, of which waited for: 4 -> 4; matrix products, arithmetic and copies ran while one was open for 0% -> 0% of each run, Pallas kernels for 29% -> 16%
where the time goes in v3:
time: 46.1 us; the launch traced here: 45.7 us
  starting transfers between devices  20.3 us (44%)
  waiting for transfers between devices  13.9 us (30%)
  Pallas kernels  7.94 us (17%)
  local copies, waits for them, and re-layouts  2.79 us (6%)
  between operations  0.73 us (2%)
    ppermute x6, starting transfers between devices, send(): return lax.ppermute(x, 'ctx', pairs)  20.3 us
    ppermute x6, waiting for transfers between devices, send(): return lax.ppermute(x, 'ctx', pairs)  13.9 us
    pallas_call x3, Pallas kernels, remote(): call(functools.partial(remote_kernel, partner, first), [(wide, F32), (kv....  3.22 us
    pallas_call x1, Pallas kernels, own(): call(own_kernel, [whole_type, (tall, BF16), (tall, BF16), (wide, BF16), (...  2.89 us
    unnamed x10, local copies, waits for them, and re-layouts  1.75 us
    slice x1, local copies, waits for them, and re-layouts, shards(): keys[:size]  1.04 us
    pallas_call x1, Pallas kernels, shards(): grad_queries, = call(queries_kernel, [(queries.shape, BF16)], [VMEM])(dqt)  1 us
  transfers between devices with their start and end apart: 6, of which 4 were waited for; matrix products, arithmetic and copies ran while one was open for 0% of the time, Pallas kernels for 16%

profile of v3, /device:TPU:0, one launch (start us, length us, event | category | flops | bytes accessed | tf_op | source)
XLA Modules:
  0.0 45.7 jit_solution(1048747754604778031)
XLA Ops:
  0.7 1.0 %fusion = (bf16[256,128]{1,0:T(8,128)(2,1)S(1)}, bf16[256,128]{1,0:T(8,128)(2,1)S(1)}, bf16[256,128]{1,0:T(8,128)(2,1)S(1)}, bf16[256,128]{1,0:T(8,128)(2,1)S(1)}) fusion(bf16[512,128]{1,0:T(8,128)(2,1)} %param.8, bf16[512,128]{1,0:T(8,128)(2,1)} %param.9), kind=kLoop, calls=%fused_computation.1 | loop fusion | bytes 524288 | tf_op jit(solution)/shard_map/slice | solution.py:215
  1.7 0.0 copy-start.4
  1.7 5.1 %collective-permute-start = (bf16[1024,128]{1,0:T(8,128)(2,1)S(1)}, bf16[1024,128]{1,0:T(8,128)(2,1)S(1)}, u32[]{:S(2)}, u32[]{:S(2)}) collective-permute-start(bf16[1024,128]{1,0:T(8,128)(2,1)S(1)} %pad_maximum_fusion.kv), channel_id=1, source_target_pairs={{0,24},{8,16},{16,8},{24,0},{1,25},{9,17},{17,9},{25,1},{2,26},{10... | collective-permute-start | bytes 786440 | tf_op jit(solution)/shard_map/ppermute | solution.py:190
  6.8 0.0 copy-done.1
  6.9 1.0 %copy-done.2 = bf16[512,512]{1,0:T(8,128)(2,1)S(1)} copy-done((bf16[512,512]{1,0:T(8,128)(2,1)S(1)}, bf16[512,512]{1,0:T(8,128)(2,1)}, u32[]{:S(2)}) %copy-start.2) | copy-done | bytes 524312
  7.9 0.7 %copy-done.3 = f32[4,512]{1,0:T(4,128)S(1)} copy-done((f32[4,512]{1,0:T(4,128)S(1)}, f32[4,512]{1,0:T(4,128)}, u32[]{:S(2)}) %copy-start.3) | copy-done | bytes 8216
  8.6 2.9 %shard_map.94 = (bf16[1024,128]{1,0:T(8,128)(2,1)S(1)}, bf16[2048,128]{1,0:T(8,128)(2,1)S(1)}, bf16[2048,128]{1,0:T(8,128)(2,1)S(1)}, bf16[128,2048]{1,0:T(8,128...) custom-call(s32[8]{0:T(128)S(1)} %copy-done.4, ...), custom_call_target="tpu_custom_call" | custom-call | flops 1342177280 | tf_op jit(solution)/shard_map/pallas_call | solution.py:193
  11.5 0.1 collective-permute-start.2
  11.6 1.8 %collective-permute-done.x = bf16[1024,128]{1,0:T(8,128)(2,1)S(1)} collective-permute-done((bf16[1024,128]{1,0:T(8,128)(2,1)S(1)}, bf16[1024,128]{1,0:T(8,128)(2,1)S(1)}, u32[]{:S(2)}, u32[]{:S(2)}) %collective-permute-start) | collective-permute-done | bytes 262176 | tf_op jit(solution)/shard_map/ppermute | solution.py:190
  13.3 5.1 %collective-permute-start.1 = (bf16[1024,128]{1,0:T(8,128)(2,1)S(1)}, bf16[1024,128]{1,0:T(8,128)(2,1)S(1)}, u32[]{:S(2)}, u32[]{:S(2)}) collective-permute-start(bf16[1024,128]{1,0:T(8,128)(2,1)S(1)} %shard_map.95.kv), channel_id=1, source_target_pairs={{0,8},{8,0},{16,24},{24,16},{1,9},{9,1},{17,25},{25,17},{2,10},{10... | collective-permute-start | bytes 786440 | tf_op jit(solution)/shard_map/ppermute | solution.py:190
  18.5 1.5 %shard_map.96 = (f32[128,2048]{1,0:T(8,128)S(1)}, bf16[1024,128]{1,0:T(8,128)(2,1)S(1)}) custom-call(s32[8]{0:T(128)S(1)} %copy-done.4, bf16[1024,128]{1,0:T(8,128)(2,1)S(1)} %shard_map.95.kv, bf16[2048,128]{1,0:T(8,128)(2,1)S(1)} %get-tuple-element.24.q4, bf16[2048,128]{1,0:T(8,128)(2,1)S(1)} %get-tuple-element.25.g4, ...), custom_call_target="tpu_custom_call", output_to_operand_aliasing={{0}: (8, {})} | custom-call | flops 1342177280 | tf_op jit(solution)/shard_map/pallas_call | solution.py:202
  20.0 3.8 %collective-permute-start.3 = (bf16[1024,128]{1,0:T(8,128)(2,1)S(1)}, bf16[1024,128]{1,0:T(8,128)(2,1)S(1)}, u32[]{:S(2)}, u32[]{:S(2)}) collective-permute-start(bf16[1024,128]{1,0:T(8,128)(2,1)S(1)} %get-tuple-element.32.refs_0_), channel_id=1, source_target_pairs={{0,24},{8,16},{16,8},{24,0},{1,25},{9,17},{17,9},{25,1},{2,26},{10... | collective-permute-start | bytes 786440 | tf_op jit(solution)/shard_map/ppermute | solution.py:190
  23.8 0.0 collective-permute-done.2.x
  23.8 0.9 %shard_map.98 = (f32[128,2048]{1,0:T(8,128)S(1)}, bf16[1024,128]{1,0:T(8,128)(2,1)S(1)}) custom-call(s32[8]{0:T(128)S(1)} %copy-done.4, bf16[1024,128]{1,0:T(8,128)(2,1)S(1)} %shard_map.97.kv, bf16[2048,128]{1,0:T(8,128)(2,1)S(1)} %get-tuple-element.24.q4, bf16[2048,128]{1,0:T(8,128)(2,1)S(1)} %get-tuple-element.25.g4, ...), custom_call_target="tpu_custom_call", output_to_operand_aliasing={{0}: (8, {})} | custom-call | flops 1342177280 | tf_op jit(solution)/shard_map/pallas_call | solution.py:202
  24.8 0.6 %collective-permute-start.4 = (bf16[1024,128]{1,0:T(8,128)(2,1)S(1)}, bf16[1024,128]{1,0:T(8,128)(2,1)S(1)}, u32[]{:S(2)}, u32[]{:S(2)}) collective-permute-start(bf16[1024,128]{1,0:T(8,128)(2,1)S(1)} %get-tuple-element.37), channel_id=1, source_target_pairs={{0,8},{8,0},{16,24},{24,16},{1,9},{9,1},{17,25},{25,17},{2,10},{10... | collective-permute-start | bytes 786440 | tf_op jit(solution)/shard_map/ppermute | solution.py:190
  25.3 0.5 %collective-permute-done.1.kv = bf16[1024,128]{1,0:T(8,128)(2,1)S(1)} collective-permute-done((bf16[1024,128]{1,0:T(8,128)(2,1)S(1)}, bf16[1024,128]{1,0:T(8,128)(2,1)S(1)}, u32[]{:S(2)}, u32[]{:S(2)}) %collective-permute-start.1) | collective-permute-done | bytes 262176 | tf_op jit(solution)/shard_map/ppermute | solution.py:190
  25.8 0.8 %shard_map.99 = (f32[128,2048]{1,0:T(8,128)S(1)}, bf16[1024,128]{1,0:T(8,128)(2,1)S(1)}) custom-call(s32[8]{0:T(128)S(1)} %copy-done.4, bf16[1024,128]{1,0:T(8,128)(2,1)S(1)} %collective-permute-done.1.kv, bf16[2048,128]{1,0:T(8,128)(2,1)S(1)} %get-tuple-element.24.q4, bf16[2048,128]{1,0:T(8,128)(2,1)S(1)} %get-tuple-element.25.g4, ...), custom_call_target="tpu_custom_call", output_to_operand_aliasing={{0}: (8, {})} | custom-call | flops 1342177280 | tf_op jit(solution)/shard_map/pallas_call | solution.py:202
  26.6 5.6 %collective-permute-start.5 = (bf16[1024,128]{1,0:T(8,128)(2,1)S(1)}, bf16[1024,128]{1,0:T(8,128)(2,1)S(1)}, u32[]{:S(2)}, u32[]{:S(2)}) collective-permute-start(bf16[1024,128]{1,0:T(8,128)(2,1)S(1)} %get-tuple-element.40), channel_id=1, source_target_pairs={{0,16},{8,24},{16,0},{24,8},{1,17},{9,25},{17,1},{25,9},{2,18},{10... | collective-permute-start | bytes 786440 | tf_op jit(solution)/shard_map/ppermute | solution.py:190
  32.2 1.0 %shard_map.100 = bf16[512,512]{1,0:T(8,128)(2,1)} custom-call(f32[128,2048]{1,0:T(8,128)S(1)} %get-tuple-element.35.dqt), custom_call_target="tpu_custom_call" | custom-call | tf_op jit(solution)/shard_map/pallas_call | solution.py:240
  33.2 6.7 %collective-permute-done.4.refs_1_ = bf16[1024,128]{1,0:T(8,128)(2,1)S(1)} collective-permute-done((bf16[1024,128]{1,0:T(8,128)(2,1)S(1)}, bf16[1024,128]{1,0:T(8,128)(2,1)S(1)}, u32[]{:S(2)}, u32[]{:S(2)}) %collective-permute-start.4) | collective-permute-done | bytes 262176 | tf_op jit(solution)/shard_map/ppermute | solution.py:190
  39.9 0.0 collective-permute-done.3.refs_0_
  39.9 0.1 shard_map.101
  40.0 5.0 %collective-permute-done.5.refs_0_ = bf16[1024,128]{1,0:T(8,128)(2,1)S(1)} collective-permute-done((bf16[1024,128]{1,0:T(8,128)(2,1)S(1)}, bf16[1024,128]{1,0:T(8,128)(2,1)S(1)}, u32[]{:S(2)}, u32[]{:S(2)}) %collective-permute-start.5) | collective-permute-done | bytes 262176 | tf_op jit(solution)/shard_map/ppermute | solution.py:190
  45.0 0.7 %shard_map.102 = (bf16[512,128]{1,0:T(8,128)(2,1)}, bf16[512,128]{1,0:T(8,128)(2,1)}) custom-call(f32[512,128]{1,0:T(8,128)S(1)} %get-tuple-element.38.dk, f32[512,128]{1,0:T(8,128)S(1)} %get-tuple-element.39.dv, bf16[1024,128]{1,0:T(8,128)(2,1)S(1)} %collective-permute-done.5.refs_0_), custom_call_target="tpu_custom_call" | custom-call | bytes 1048576 | tf_op jit(solution)/shard_map/pallas_call | solution.py:212
  (9 shorter events, 0.0 us)
Async XLA Ops:
  0.6 6.2 %copy-start.1 = (bf16[512,512]{1,0:T(8,128)(2,1)S(1)}, bf16[512,512]{1,0:T(8,128)(2,1)}, u32[]{:S(2)}) copy-start(bf16[512,512]{1,0:T(8,128)(2,1)} %g.1) | copy-start | bytes 1572868
  0.6 6.2 %copy-start = (bf16[512,512]{1,0:T(8,128)(2,1)S(1)}, bf16[512,512]{1,0:T(8,128)(2,1)}, u32[]{:S(2)}) copy-start(bf16[512,512]{1,0:T(8,128)(2,1)} %q.1) | copy-start | bytes 1572868
  1.7 5.2 %copy-start.4 = (s32[8]{0:T(128)S(1)}, s32[8]{0:T(128)}, u32[]{:S(2)}) copy-start(s32[8]{0:T(128)} %order.7) | copy-start | bytes 100
  1.7 11.6 %collective-permute-start = (bf16[1024,128]{1,0:T(8,128)(2,1)S(1)}, bf16[1024,128]{1,0:T(8,128)(2,1)S(1)}, u32[]{:S(2)}, u32[]{:S(2)}) collective-permute-start(bf16[1024,128]{1,0:T(8,128)(2,1)S(1)} %pad_maximum_fusion.kv), channel_id=1, source_target_pairs={{0,24},{8,16},{16,8},{24,0},{1,25},{9,17},{17,9},{25,1},{2,26},{10... | collective-permute-start | bytes 786440 | tf_op jit(solution)/shard_map/ppermute | solution.py:190
  6.9 1.0 %copy-start.2 = (bf16[512,512]{1,0:T(8,128)(2,1)S(1)}, bf16[512,512]{1,0:T(8,128)(2,1)}, u32[]{:S(2)}) copy-start(bf16[512,512]{1,0:T(8,128)(2,1)} %o.1) | copy-start | bytes 1572868
  7.9 0.7 %copy-start.3 = (f32[4,512]{1,0:T(4,128)S(1)}, f32[4,512]{1,0:T(4,128)}, u32[]{:S(2)}) copy-start(f32[4,512]{1,0:T(4,128)} %log_norms.1) | copy-start | bytes 24580
  11.5 12.3 %collective-permute-start.2 = (bf16[1024,128]{1,0:T(8,128)(2,1)S(1)}, bf16[1024,128]{1,0:T(8,128)(2,1)S(1)}, u32[]{:S(2)}, u32[]{:S(2)}) collective-permute-start(bf16[1024,128]{1,0:T(8,128)(2,1)S(1)} %get-tuple-element.30), channel_id=1, source_target_pairs={{0,8},{8,0},{16,24},{24,16},{1,9},{9,1},{17,25},{25,17},{2,10},{10... | collective-permute-start | bytes 786440 | tf_op jit(solution)/shard_map/ppermute | solution.py:190
  13.3 12.5 %collective-permute-start.1 = (bf16[1024,128]{1,0:T(8,128)(2,1)S(1)}, bf16[1024,128]{1,0:T(8,128)(2,1)S(1)}, u32[]{:S(2)}, u32[]{:S(2)}) collective-permute-start(bf16[1024,128]{1,0:T(8,128)(2,1)S(1)} %shard_map.95.kv), channel_id=1, source_target_pairs={{0,8},{8,0},{16,24},{24,16},{1,9},{9,1},{17,25},{25,17},{2,10},{10... | collective-permute-start | bytes 786440 | tf_op jit(solution)/shard_map/ppermute | solution.py:190
  20.0 19.9 %collective-permute-start.3 = (bf16[1024,128]{1,0:T(8,128)(2,1)S(1)}, bf16[1024,128]{1,0:T(8,128)(2,1)S(1)}, u32[]{:S(2)}, u32[]{:S(2)}) collective-permute-start(bf16[1024,128]{1,0:T(8,128)(2,1)S(1)} %get-tuple-element.32.refs_0_), channel_id=1, source_target_pairs={{0,24},{8,16},{16,8},{24,0},{1,25},{9,17},{17,9},{25,1},{2,26},{10... | collective-permute-start | bytes 786440 | tf_op jit(solution)/shard_map/ppermute | solution.py:190
  24.8 15.2 %collective-permute-start.4 = (bf16[1024,128]{1,0:T(8,128)(2,1)S(1)}, bf16[1024,128]{1,0:T(8,128)(2,1)S(1)}, u32[]{:S(2)}, u32[]{:S(2)}) collective-permute-start(bf16[1024,128]{1,0:T(8,128)(2,1)S(1)} %get-tuple-element.37), channel_id=1, source_target_pairs={{0,8},{8,0},{16,24},{24,16},{1,9},{9,1},{17,25},{25,17},{2,10},{10... | collective-permute-start | bytes 786440 | tf_op jit(solution)/shard_map/ppermute | solution.py:190
  26.6 18.4 %collective-permute-start.5 = (bf16[1024,128]{1,0:T(8,128)(2,1)S(1)}, bf16[1024,128]{1,0:T(8,128)(2,1)S(1)}, u32[]{:S(2)}, u32[]{:S(2)}) collective-permute-start(bf16[1024,128]{1,0:T(8,128)(2,1)S(1)} %get-tuple-element.40), channel_id=1, source_target_pairs={{0,16},{8,24},{16,0},{24,8},{1,17},{9,25},{17,1},{25,9},{2,18},{10... | collective-permute-start | bytes 786440 | tf_op jit(solution)/shard_map/ppermute | solution.py:190

commit v4 on v3

--- a/solution.py
+++ b/solution.py
@@ -10,6 +10,7 @@
 
 HD = 128
 SCALE = HD ** (-0.5)
+WEIGHT = 10
 LOG2E = math.log2(math.e)
 F32 = jnp.float32
 BF16 = jnp.bfloat16
@@ -40,12 +41,10 @@
     return grad_key * SCALE, grad_value
 
 
-def own_kernel(order, kv, log_norms, q, g, o, kv_out, q4, g4, qt, gt, norm, delta, dqt, dk, dv, ps, ds):
-    me = lax.axis_index("ctx")
+def prepare_kernel(log_norms, q, g, o, q4, g4, qt, gt, norm, delta):
     size = q.shape[0] // 2
     heads = log_norms.shape[0]
     width = heads * size
-    kv_out[...] = kv[...]
     for a in range(2):
         rows = pl.ds(a * size, size)
         for h in range(heads):
@@ -59,44 +58,48 @@
             prod = grad.astype(F32) * o[rows, lanes].astype(F32)
             delta[:, cols] = jnp.sum(prod.T, axis=0, keepdims=True)
             norm[:, cols] = log_norms[pl.ds(h, 1), rows] * LOG2E
+
+
+def own_kernel(order, k, v, q4, g4, qt, gt, norm, delta, dqt, dk, dv, ps, ds):
+    me = lax.axis_index("ctx")
+    size, width = ps.shape
     state = (q4, g4, qt, gt, norm, delta)
     for a in range(2):
-        key, value = kv[pl.ds(2 * a * size, size), :], kv[pl.ds((2 * a + 1) * size, size), :]
         rows, cols = pl.ds(a * size, size), pl.ds(a * width, width)
+        key, value = k[rows, :], v[rows, :]
         low_terms(a * width, width, key, value, state, True, ps, ds)
         dk[rows, :], dv[rows, :] = key_terms(a * width, width, state, ps, ds)
         dqt[:, cols] = jnp.dot(key.T, ds[...], preferred_element_type=F32)
     late = (order[2 * me] < order[2 * me + 1]).astype(jnp.int32)
     start = pl.multiple_of(late * width, width)
-    key_at = pl.multiple_of((1 - late) * 2 * size, size)
-    key, value = kv[pl.ds(key_at, size), :], kv[pl.ds(key_at + size, size), :]
+    rows = pl.ds(pl.multiple_of((1 - late) * size, size), size)
+    key, value = k[rows, :], v[rows, :]
     low_terms(start, width, key, value, state, False, ps, ds)
-    rows = pl.ds(pl.multiple_of((1 - late) * size, size), size)
     grad_key, grad_value = key_terms(start, width, state, ps, ds)
     dk[rows, :] += grad_key
     dv[rows, :] += grad_value
     dqt[:, pl.ds(start, width)] += jnp.dot(key.T, ds[...], preferred_element_type=F32)
 
 
-def remote_kernel(partner, first, order, kv, q4, g4, qt, gt, norm, delta, dqt_in, dqt, part, ps, ds):
+def remote_kernel(partner, order, k, v, q4, g4, qt, gt, norm, delta, dqt_in, dqt, part, ps, ds):
     me = lax.axis_index("ctx")
     other = partner(me)
     total = q4.shape[0]
     width = total // 2
     size = ps.shape[0]
     state = (q4, g4, qt, gt, norm, delta)
-    for b in range(kv.shape[0] // (2 * size)):
-        keys_at, values_at = pl.ds(2 * b * size, size), pl.ds((2 * b + 1) * size, size)
+    for b in range(2):
+        rows, values_to = pl.ds(b * size, size), pl.ds((2 + b) * size, size)
         before = dqt_in if b == 0 else dqt
-        sees = [order[2 * other + first + b] < order[2 * me + a] for a in range(2)]
+        sees = [order[2 * other + b] < order[2 * me + a] for a in range(2)]
         count = sees[0].astype(jnp.int32) + sees[1].astype(jnp.int32)
 
         def some(start, span):
-            key, value = kv[keys_at, :], kv[values_at, :]
+            key, value = k[rows, :], v[rows, :]
             low_terms(start, span, key, value, state, False, ps, ds)
             grad_key, grad_value = key_terms(start, span, state, ps, ds)
-            part[keys_at, :] = grad_key.astype(BF16)
-            part[values_at, :] = grad_value.astype(BF16)
+            part[rows, :] = grad_key.astype(BF16)
+            part[values_to, :] = grad_value.astype(BF16)
             cols = pl.ds(start, span)
             dqt[:, cols] = before[:, cols] + jnp.dot(key.T, ds[:, :span], preferred_element_type=F32)
 
@@ -114,8 +117,8 @@
 
         @pl.when(count == 0)
         def _():
-            part[keys_at, :] = jnp.zeros((size, HD), BF16)
-            part[values_at, :] = jnp.zeros((size, HD), BF16)
+            part[rows, :] = jnp.zeros((size, HD), BF16)
+            part[values_to, :] = jnp.zeros((size, HD), BF16)
             if b == 0:
                 dqt[...] = dqt_in[...]
 
@@ -131,15 +134,17 @@
 
 def sums_kernel(dk, dv, *refs):
     parts, (out_k, out_v) = refs[:-2], refs[-2:]
-    size = dk.shape[0] // 2
-    for b in range(2):
-        rows = pl.ds(b * size, size)
-        key_sum, value_sum = dk[rows, :], dv[rows, :]
-        for part in parts:
-            key_sum += part[pl.ds(2 * b * size, size), :].astype(F32)
-            value_sum += part[pl.ds((2 * b + 1) * size, size), :].astype(F32)
-        out_k[rows, :] = key_sum.astype(out_k.dtype)
-        out_v[rows, :] = value_sum.astype(out_v.dtype)
+    rows = dk.shape[0]
+    key_sum, value_sum = dk[...], dv[...]
+    for part in parts:
+        key_sum += part[:rows, :].astype(F32)
+        value_sum += part[rows:, :].astype(F32)
+    out_k[...] = key_sum.astype(out_k.dtype)
+    out_v[...] = value_sum.astype(out_v.dtype)
+
+
+def add_kernel(first, second, both):
+    both[...] = (first[...].astype(F32) + second[...].astype(F32)).astype(BF16)
 
 
 def token_kernel(x, *refs):
@@ -183,61 +188,76 @@
     wide = (HD, total)
     tall = (total, HD)
     line = (1, total)
-    whole_type = ((4 * size, HD), BF16)
+    part_type = ((4 * size, HD), BF16)
     sums_type = ((rows, HD), F32)
 
     def send(x, pairs):
         return lax.ppermute(x, "ctx", pairs)
 
-    def own(kv):
+    def prepare():
+        return call(
+            prepare_kernel,
+            [(tall, BF16), (tall, BF16), (wide, BF16), (wide, BF16), (line, F32), (line, F32)],
+            [VMEM] * 4,
+            flops=work,
+        )(log_norms, queries, out_grads, outputs)
+
+    def own(same):
         return call(
             own_kernel,
-            [whole_type, (tall, BF16), (tall, BF16), (wide, BF16), (wide, BF16), (line, F32), (line, F32), (wide, F32), sums_type, sums_type],
-            [SMEM] + [VMEM] * 5,
+            [(wide, F32), sums_type, sums_type],
+            [SMEM] + [VMEM] * 8,
             scratch=[pltpu.VMEM((size, heads * size), BF16)] * 2,
             flops=work,
-        )(stretch_order, kv, log_norms, queries, out_grads, outputs)
-
-    def remote(partner, first, kv, *state):
+        )(stretch_order, keys, values, *same)
+
+    def remote(s, kv, same, dqt):
+        partner = s if callable(s) else lambda i: i ^ s
         return call(
-            functools.partial(remote_kernel, partner, first),
-            [(wide, F32), (kv.shape, BF16)],
-            [SMEM] + [VMEM] * 8,
+            functools.partial(remote_kernel, partner),
+            [(wide, F32), part_type],
+            [SMEM] + [VMEM] * 9,
             scratch=[pltpu.VMEM((size, total), BF16)] * 2,
-            aliases={8: 0},
-            flops=work * kv.shape[0] // (4 * size),
-        )(stretch_order, kv, *state)
+            aliases={9: 0},
+            flops=WEIGHT * work,
+        )(stretch_order, *kv, *same, dqt)
 
     def sums(dk, dv, parts, outs):
-        return call(sums_kernel, outs, [VMEM] * (2 + len(parts)), moved=16 * rows * HD)(dk, dv, *parts)
+        return call(sums_kernel, outs, [VMEM] * (2 + len(parts)))(dk, dv, *parts)
+
+    def add(first, second):
+        return call(add_kernel, [part_type], [VMEM] * 2)(first, second)[0]
 
     last = [(keys.shape, BF16), (values.shape, BF16)]
-    kv = jnp.concatenate([keys[:size], values[:size], keys[size:], values[size:]], axis=0)
     if n == 4:
         swap = [[(i, i ^ s) for i in range(n)] for s in range(n)]
-        kv_3 = send(kv, swap[3])
-        kv, *same, dqt, dk, dv = own(kv)
-        kv_1 = send(kv, swap[1])
-        kv_3 = after(kv_3, dk)
-        kv_2 = send(kv_3, swap[1])
-        dqt, part_3 = remote(lambda i: i ^ 3, 0, kv_3, *same, dqt)
-        back_3 = send(part_3, swap[3])
-        kv_1 = after(kv_1, part_3)
-        dqt, part_1 = remote(lambda i: i ^ 1, 0, kv_1, *same, dqt)
-        back_1 = send(part_1, swap[1])
-        dqt, part_2 = remote(lambda i: i ^ 2, 0, kv_2, *same, dqt)
-        back_2 = send(part_2, swap[2])
-        dk, dv = sums(dk, dv, [back_3, back_1], [sums_type] * 2)
-        returned = [back_2]
+        own_rows = (keys, values)
+        kv_3 = [send(x, swap[3]) for x in own_rows]
+        same = prepare()
+        kv_1 = [send(x, swap[1]) for x in own_rows]
+        dqt, dk, dv = own(same)
+        kv_3 = [after(x, dk) for x in kv_3]
+        kv_2 = [send(x, swap[1]) for x in kv_3]
+        dqt, part_3 = remote(3, kv_3, same, dqt)
+        aside_3 = send(part_3, swap[1])
+        kv_1 = [after(x, part_3) for x in kv_1]
+        dqt, part_1 = remote(1, kv_1, same, dqt)
+        kv_2 = [after(x, part_1) for x in kv_2]
+        dqt, part_2 = remote(2, kv_2, same, dqt)
+        both = add(after(aside_3, part_2), part_2)
+        back_2 = send(both, swap[2])
+        back_1 = send(after(part_1, both), swap[1])
+        returned = [back_1, back_2]
     else:
-        kv, *same, dqt, dk, dv = own(kv)
+        same = prepare()
+        dqt, dk, dv = own(same)
         partners = [partner_of(n, s) for s in range(1, n)]
-        arrived = [send(kv, [(p(i), i) for i in range(n)]) for p in partners]
+        arrived = [[send(x, [(p(i), i) for i in range(n)]) for x in (keys, values)] for p in partners]
         returned = []
         for p, got in zip(partners, arrived):
-            dqt, part = remote(p, 0, got, *same, dqt)
+            dqt, part = remote(p, got, same, dqt)
             returned.append(send(part, [(i, p(i)) for i in range(n)]))
-    (grad_queries,) = call(queries_kernel, [(queries.shape, BF16)], [VMEM])(dqt)
+    (grad_queries,) = call(queries_kernel, [(queries.shape, BF16)], [VMEM], flops=WEIGHT * work)(dqt)
     grad_keys, grad_values = sums(dk, dv, returned, last)
     return grad_queries, grad_keys, grad_values
 

time: 46.1 us -> 44.3 us (0.961)
  starting transfers between devices: 20.3 us -> 14.1 us
  Pallas kernels: 7.94 us -> 13.6 us
  waiting for transfers between devices: 13.9 us -> 10.7 us
  local copies, waits for them, and re-layouts: 2.79 us -> 4.5 us
    ppermute x6 -> x9, starting transfers between devices: 20.3 us -> 14.1 us  [send(): return lax.ppermute(x, 'ctx', pairs)]
    pallas_call x7 -> x8, Pallas kernels: 7.94 us -> 13.6 us  [the longest x3 8.52 us: remote(): call(functools.partial(remote_kernel, partner), [(wide, F32), part_type],...]
    ppermute x6 -> x9, waiting for transfers between devices: 13.9 us -> 10.7 us  [send(): return lax.ppermute(x, 'ctx', pairs)]
    unnamed x10 -> x14, local copies, waits for them, and re-layouts: 1.75 us -> 4.5 us
    slice x1 -> x0, local copies, waits for them, and re-layouts: 1.04 us -> none  [shards(): keys[:size]]
  transfers between devices with their start and end apart: 6 -> 9, of which waited for: 4 -> 3; matrix products, arithmetic and copies ran while one was open for 0% -> 0% of each run, Pallas kernels for 16% -> 29%
where the time goes in v4:
time: 44.3 us; the launch traced here: 43.7 us
  starting transfers between devices  14.1 us (32%)
  Pallas kernels  13.6 us (31%)
  waiting for transfers between devices  10.7 us (24%)
  local copies, waits for them, and re-layouts  4.5 us (10%)
  between operations  0.78 us (2%)
    ppermute x9, starting transfers between devices, send(): return lax.ppermute(x, 'ctx', pairs)  14.1 us
    ppermute x9, waiting for transfers between devices, send(): return lax.ppermute(x, 'ctx', pairs)  10.7 us
    pallas_call x3, Pallas kernels, remote(): call(functools.partial(remote_kernel, partner), [(wide, F32), part_type],...  8.52 us
    unnamed x14, local copies, waits for them, and re-layouts  4.5 us
    pallas_call x1, Pallas kernels, own(): call(own_kernel, [(wide, F32), sums_type, sums_type], [SMEM] + [VMEM] * 8...  2.56 us
    pallas_call x1, Pallas kernels, shards(): call(queries_kernel, [(queries.shape, BF16)], [VMEM], flops=WEIGHT * work)  1 us
  transfers between devices with their start and end apart: 9, of which 3 were waited for; matrix products, arithmetic and copies ran while one was open for 0% of the time, Pallas kernels for 29%

profile of v4, /device:TPU:0, one launch (start us, length us, event | category | flops | bytes accessed | tf_op | source)
XLA Modules:
  0.0 43.7 jit_solution(4700278363241024395)
XLA Ops:
  0.6 5.1 %collective-permute-start = (bf16[512,128]{1,0:T(8,128)(2,1)}, bf16[512,128]{1,0:T(8,128)(2,1)S(1)}, u32[]{:S(2)}, u32[]{:S(2)}) collective-permute-start(bf16[512,128]{1,0:T(8,128)(2,1)} %k.1), channel_id=1, source_target_pairs={{0,24},{8,16},{16,8},{24,0},{1,25},{9,17},{17,9},{25,1},{2,26},{10... | collective-permute-start | bytes 393224 | tf_op jit(solution)/shard_map/ppermute | solution.py:195
  5.7 2.0 %collective-permute-start.4 = (bf16[512,128]{1,0:T(8,128)(2,1)}, bf16[512,128]{1,0:T(8,128)(2,1)S(1)}, u32[]{:S(2)}, u32[]{:S(2)}) collective-permute-start(bf16[512,128]{1,0:T(8,128)(2,1)} %v.1), channel_id=1, source_target_pairs={{0,8},{8,0},{16,24},{24,16},{1,9},{9,1},{17,25},{25,17},{2,10},{10... | collective-permute-start | bytes 393224 | tf_op jit(solution)/shard_map/ppermute | solution.py:195
  7.8 0.1 collective-permute-start.3
  7.9 1.0 %copy-done = bf16[512,512]{1,0:T(8,128)(2,1)S(1)} copy-done((bf16[512,512]{1,0:T(8,128)(2,1)S(1)}, bf16[512,512]{1,0:T(8,128)(2,1)}, u32[]{:S(2)}) %copy-start) | copy-done | bytes 524312
  8.9 1.0 %copy-done.1 = bf16[512,512]{1,0:T(8,128)(2,1)S(1)} copy-done((bf16[512,512]{1,0:T(8,128)(2,1)S(1)}, bf16[512,512]{1,0:T(8,128)(2,1)}, u32[]{:S(2)}) %copy-start.1) | copy-done | bytes 524312
  9.9 1.0 %copy-done.2 = bf16[512,512]{1,0:T(8,128)(2,1)S(1)} copy-done((bf16[512,512]{1,0:T(8,128)(2,1)S(1)}, bf16[512,512]{1,0:T(8,128)(2,1)}, u32[]{:S(2)}) %copy-start.2) | copy-done | bytes 524312
  11.0 0.7 %copy-done.5 = f32[4,512]{1,0:T(4,128)S(1)} copy-done((f32[4,512]{1,0:T(4,128)S(1)}, f32[4,512]{1,0:T(4,128)}, u32[]{:S(2)}) %copy-start.5) | copy-done | bytes 8216
  11.7 0.7 %shard_map.94 = (bf16[2048,128]{1,0:T(8,128)(2,1)S(1)}, bf16[2048,128]{1,0:T(8,128)(2,1)S(1)}, bf16[128,2048]{1,0:T(8,128)(2,1)S(1)}, bf16[128,2048]{1,0:T(8,128...) custom-call(f32[4,512]{1,0:T(4,128)S(1)} %copy-done.5, bf16[512,512]{1,0:T(8,128)(2,1)S(1)} %copy-done, ...), custom_call_target="tpu_custom_call" | custom-call | flops 1342177280 | tf_op jit(solution)/shard_map/pallas_call | solution.py:198
  12.4 0.1 copy-done.3
  12.6 0.5 %copy-done.6 = s32[8]{0:T(128)S(1)} copy-done((s32[8]{0:T(128)S(1)}, s32[8]{0:T(128)}, u32[]{:S(2)}) %copy-start.6) | copy-done | bytes 56
  13.1 2.6 %shard_map.95 = (f32[128,2048]{1,0:T(8,128)S(1)}, f32[512,128]{1,0:T(8,128)S(1)}, f32[512,128]{1,0:T(8,128)S(1)}) custom-call(s32[8]{0:T(128)S(1)} %copy-done.6, bf16[512,128]{1,0:T(8,128)(2,1)S(1)} %copy-done.4, bf16[512,128]{1,0:T(8,128)(2,1)S(1)} %copy-done.3, bf16[2048,128]{1,0:T(8,128)(2,1)S(1)} %get-tuple-element.20.q4, ...), custom_call_target="tpu_custom_call" | custom-call | flops 1342177280 | tf_op jit(solution)/shard_map/pallas_call | solution.py:206
  15.7 0.1 collective-permute-start.1
  15.8 2.6 %collective-permute-done.3.x = bf16[512,128]{1,0:T(8,128)(2,1)S(1)} collective-permute-done((bf16[512,128]{1,0:T(8,128)(2,1)}, bf16[512,128]{1,0:T(8,128)(2,1)S(1)}, u32[]{:S(2)}, u32[]{:S(2)}) %collective-permute-start.3) | collective-permute-done | bytes 131104 | tf_op jit(solution)/shard_map/ppermute | solution.py:195
  18.4 2.1 %shard_map.98 = (f32[128,2048]{1,0:T(8,128)S(1)}, bf16[1024,128]{1,0:T(8,128)(2,1)S(1)}) custom-call(s32[8]{0:T(128)S(1)} %copy-done.6, bf16[512,128]{1,0:T(8,128)(2,1)S(1)} %shard_map.96.k, bf16[512,128]{1,0:T(8,128)(2,1)S(1)} %shard_map.97.v, bf16[2048,128]{1,0:T(8,128)(2,1)S(1)} %get-tuple-element.20.q4, ...), custom_call_target="tpu_custom_call", output_to_operand_aliasing={{0}: (9, {})} | custom-call | flops 13421772800 | tf_op jit(solution)/shard_map/pallas_call | solution.py:216
  20.5 2.3 %collective-permute-start.6 = (bf16[1024,128]{1,0:T(8,128)(2,1)S(1)}, bf16[1024,128]{1,0:T(8,128)(2,1)S(1)}, u32[]{:S(2)}, u32[]{:S(2)}) collective-permute-start(bf16[1024,128]{1,0:T(8,128)(2,1)S(1)} %get-tuple-element.28.refs_0_), channel_id=1, source_target_pairs={{0,8},{8,0},{16,24},{24,16},{1,9},{9,1},{17,25},{25,17},{2,10},{10... | collective-permute-start | bytes 786440 | tf_op jit(solution)/shard_map/ppermute | solution.py:195
  22.8 3.0 %shard_map.101 = (f32[128,2048]{1,0:T(8,128)S(1)}, bf16[1024,128]{1,0:T(8,128)(2,1)S(1)}) custom-call(s32[8]{0:T(128)S(1)} %copy-done.6, bf16[512,128]{1,0:T(8,128)(2,1)S(1)} %shard_map.99.k, bf16[512,128]{1,0:T(8,128)(2,1)S(1)} %shard_map.100.v, bf16[2048,128]{1,0:T(8,128)(2,1)S(1)} %get-tuple-element.20.q4, ...), custom_call_target="tpu_custom_call", output_to_operand_aliasing={{0}: (9, {})} | custom-call | flops 13421772800 | tf_op jit(solution)/shard_map/pallas_call | solution.py:216
  25.9 3.4 %shard_map.104 = (f32[128,2048]{1,0:T(8,128)S(1)}, bf16[1024,128]{1,0:T(8,128)(2,1)S(1)}) custom-call(s32[8]{0:T(128)S(1)} %copy-done.6, bf16[512,128]{1,0:T(8,128)(2,1)S(1)} %shard_map.102.k, bf16[512,128]{1,0:T(8,128)(2,1)S(1)} %shard_map.103.v, bf16[2048,128]{1,0:T(8,128)(2,1)S(1)} %get-tuple-element.20.q4, ...), custom_call_target="tpu_custom_call", output_to_operand_aliasing={{0}: (9, {})} | custom-call | flops 13421772800 | tf_op jit(solution)/shard_map/pallas_call | solution.py:216
  29.3 0.1 shard_map.107.refs_0_
  29.4 2.5 %collective-permute-start.8 = (bf16[1024,128]{1,0:T(8,128)(2,1)S(1)}, bf16[1024,128]{1,0:T(8,128)(2,1)S(1)}, u32[]{:S(2)}, u32[]{:S(2)}) collective-permute-start(bf16[1024,128]{1,0:T(8,128)(2,1)S(1)} %shard_map.107.refs_0_), channel_id=1, source_target_pairs={{0,16},{8,24},{16,0},{24,8},{1,17},{9,25},{17,1},{25,9},{2,18},{10... | collective-permute-start | bytes 786440 | tf_op jit(solution)/shard_map/ppermute | solution.py:195
  31.8 2.0 %collective-permute-start.7 = (bf16[1024,128]{1,0:T(8,128)(2,1)S(1)}, bf16[1024,128]{1,0:T(8,128)(2,1)S(1)}, u32[]{:S(2)}, u32[]{:S(2)}) collective-permute-start(bf16[1024,128]{1,0:T(8,128)(2,1)S(1)} %shard_map.108), channel_id=1, source_target_pairs={{0,8},{8,0},{16,24},{24,16},{1,9},{9,1},{17,25},{25,17},{2,10},{10... | collective-permute-start | bytes 786440 | tf_op jit(solution)/shard_map/ppermute | solution.py:195
  33.9 1.0 %shard_map.105 = bf16[512,512]{1,0:T(8,128)(2,1)} custom-call(f32[128,2048]{1,0:T(8,128)S(1)} %get-tuple-element.32.dqt), custom_call_target="tpu_custom_call" | custom-call | flops 13421772800 | tf_op jit(solution)/shard_map/pallas_call | solution.py:260
  34.9 6.1 %collective-permute-done.7.refs_0_ = bf16[1024,128]{1,0:T(8,128)(2,1)S(1)} collective-permute-done((bf16[1024,128]{1,0:T(8,128)(2,1)S(1)}, bf16[1024,128]{1,0:T(8,128)(2,1)S(1)}, u32[]{:S(2)}, u32[]{:S(2)}) %collective-permute-start.7) | collective-permute-done | bytes 262176 | tf_op jit(solution)/shard_map/ppermute | solution.py:195
  41.0 2.0 %collective-permute-done.8.refs_1_ = bf16[1024,128]{1,0:T(8,128)(2,1)S(1)} collective-permute-done((bf16[1024,128]{1,0:T(8,128)(2,1)S(1)}, bf16[1024,128]{1,0:T(8,128)(2,1)S(1)}, u32[]{:S(2)}, u32[]{:S(2)}) %collective-permute-start.8) | collective-permute-done | bytes 262176 | tf_op jit(solution)/shard_map/ppermute | solution.py:195
  43.0 0.7 %shard_map.109 = (bf16[512,128]{1,0:T(8,128)(2,1)}, bf16[512,128]{1,0:T(8,128)(2,1)}) custom-call(f32[512,128]{1,0:T(8,128)S(1)} %get-tuple-element.26.refs_0_.dk, f32[512,128]{1,0:T(8,128)S(1)} %get-tuple-element.33.dv, bf16[1024,128]{1,0:T(8,128)(2,1)S(1)} %collective-permute-done.7.refs_0_, bf16[1024,128]{1,0:T(8,128)(2,1)S(1)} %collective-permute-done.8.refs_1_), custom_call_target="tpu_custom_call" | custom-call | tf_op jit(solution)/shard_map/pallas_call | solution.py:226
  (24 shorter events, 0.1 us)
Async XLA Ops:
  0.6 15.1 %collective-permute-start = (bf16[512,128]{1,0:T(8,128)(2,1)}, bf16[512,128]{1,0:T(8,128)(2,1)S(1)}, u32[]{:S(2)}, u32[]{:S(2)}) collective-permute-start(bf16[512,128]{1,0:T(8,128)(2,1)} %k.1), channel_id=1, source_target_pairs={{0,24},{8,16},{16,8},{24,0},{1,25},{9,17},{17,9},{25,1},{2,26},{10... | collective-permute-start | bytes 393224 | tf_op jit(solution)/shard_map/ppermute | solution.py:195
  5.7 17.1 %collective-permute-start.2 = (bf16[512,128]{1,0:T(8,128)(2,1)}, bf16[512,128]{1,0:T(8,128)(2,1)S(1)}, u32[]{:S(2)}, u32[]{:S(2)}) collective-permute-start(bf16[512,128]{1,0:T(8,128)(2,1)} %k.1), channel_id=1, source_target_pairs={{0,8},{8,0},{16,24},{24,16},{1,9},{9,1},{17,25},{25,17},{2,10},{10... | collective-permute-start | bytes 393224 | tf_op jit(solution)/shard_map/ppermute | solution.py:195
  5.7 17.1 %collective-permute-start.4 = (bf16[512,128]{1,0:T(8,128)(2,1)}, bf16[512,128]{1,0:T(8,128)(2,1)S(1)}, u32[]{:S(2)}, u32[]{:S(2)}) collective-permute-start(bf16[512,128]{1,0:T(8,128)(2,1)} %v.1), channel_id=1, source_target_pairs={{0,8},{8,0},{16,24},{24,16},{1,9},{9,1},{17,25},{25,17},{2,10},{10... | collective-permute-start | bytes 393224 | tf_op jit(solution)/shard_map/ppermute | solution.py:195
  7.8 10.6 %collective-permute-start.3 = (bf16[512,128]{1,0:T(8,128)(2,1)}, bf16[512,128]{1,0:T(8,128)(2,1)S(1)}, u32[]{:S(2)}, u32[]{:S(2)}) collective-permute-start(bf16[512,128]{1,0:T(8,128)(2,1)} %v.1), channel_id=1, source_target_pairs={{0,24},{8,16},{16,8},{24,0},{1,25},{9,17},{17,9},{25,1},{2,26},{10... | collective-permute-start | bytes 393224 | tf_op jit(solution)/shard_map/ppermute | solution.py:195
  7.9 1.0 %copy-start = (bf16[512,512]{1,0:T(8,128)(2,1)S(1)}, bf16[512,512]{1,0:T(8,128)(2,1)}, u32[]{:S(2)}) copy-start(bf16[512,512]{1,0:T(8,128)(2,1)} %q.1) | copy-start | bytes 1572868
  8.9 1.0 %copy-start.1 = (bf16[512,512]{1,0:T(8,128)(2,1)S(1)}, bf16[512,512]{1,0:T(8,128)(2,1)}, u32[]{:S(2)}) copy-start(bf16[512,512]{1,0:T(8,128)(2,1)} %g.1) | copy-start | bytes 1572868
  9.9 1.0 %copy-start.2 = (bf16[512,512]{1,0:T(8,128)(2,1)S(1)}, bf16[512,512]{1,0:T(8,128)(2,1)}, u32[]{:S(2)}) copy-start(bf16[512,512]{1,0:T(8,128)(2,1)} %o.1) | copy-start | bytes 1572868
  11.0 0.7 %copy-start.5 = (f32[4,512]{1,0:T(4,128)S(1)}, f32[4,512]{1,0:T(4,128)}, u32[]{:S(2)}) copy-start(f32[4,512]{1,0:T(4,128)} %log_norms.1) | copy-start | bytes 24580
  11.7 0.9 %copy-start.3 = (bf16[512,128]{1,0:T(8,128)(2,1)S(1)}, bf16[512,128]{1,0:T(8,128)(2,1)}, u32[]{:S(2)}) copy-start(bf16[512,128]{1,0:T(8,128)(2,1)} %v.1) | copy-start | bytes 393220
  11.7 1.0 %copy-start.4 = (bf16[512,128]{1,0:T(8,128)(2,1)S(1)}, bf16[512,128]{1,0:T(8,128)(2,1)}, u32[]{:S(2)}) copy-start(bf16[512,128]{1,0:T(8,128)(2,1)} %k.1) | copy-start | bytes 393220
  12.4 0.7 %copy-start.6 = (s32[8]{0:T(128)S(1)}, s32[8]{0:T(128)}, u32[]{:S(2)}) copy-start(s32[8]{0:T(128)} %order.7) | copy-start | bytes 100
  15.7 10.1 %collective-permute-start.1 = (bf16[512,128]{1,0:T(8,128)(2,1)S(1)}, bf16[512,128]{1,0:T(8,128)(2,1)S(1)}, u32[]{:S(2)}, u32[]{:S(2)}) collective-permute-start(bf16[512,128]{1,0:T(8,128)(2,1)S(1)} %shard_map.96.k), channel_id=1, source_target_pairs={{0,8},{8,0},{16,24},{24,16},{1,9},{9,1},{17,25},{25,17},{2,10},{10... | collective-permute-start | bytes 393224 | tf_op jit(solution)/shard_map/ppermute | solution.py:195
  18.4 7.4 %collective-permute-start.5 = (bf16[512,128]{1,0:T(8,128)(2,1)S(1)}, bf16[512,128]{1,0:T(8,128)(2,1)S(1)}, u32[]{:S(2)}, u32[]{:S(2)}) collective-permute-start(bf16[512,128]{1,0:T(8,128)(2,1)S(1)} %shard_map.97.v), channel_id=1, source_target_pairs={{0,8},{8,0},{16,24},{24,16},{1,9},{9,1},{17,25},{25,17},{2,10},{10... | collective-permute-start | bytes 393224 | tf_op jit(solution)/shard_map/ppermute | solution.py:195
  20.5 8.7 %collective-permute-start.6 = (bf16[1024,128]{1,0:T(8,128)(2,1)S(1)}, bf16[1024,128]{1,0:T(8,128)(2,1)S(1)}, u32[]{:S(2)}, u32[]{:S(2)}) collective-permute-start(bf16[1024,128]{1,0:T(8,128)(2,1)S(1)} %get-tuple-element.28.refs_0_), channel_id=1, source_target_pairs={{0,8},{8,0},{16,24},{24,16},{1,9},{9,1},{17,25},{25,17},{2,10},{10... | collective-permute-start | bytes 786440 | tf_op jit(solution)/shard_map/ppermute | solution.py:195
  29.4 13.6 %collective-permute-start.8 = (bf16[1024,128]{1,0:T(8,128)(2,1)S(1)}, bf16[1024,128]{1,0:T(8,128)(2,1)S(1)}, u32[]{:S(2)}, u32[]{:S(2)}) collective-permute-start(bf16[1024,128]{1,0:T(8,128)(2,1)S(1)} %shard_map.107.refs_0_), channel_id=1, source_target_pairs={{0,16},{8,24},{16,0},{24,8},{1,17},{9,25},{17,1},{25,9},{2,18},{10... | collective-permute-start | bytes 786440 | tf_op jit(solution)/shard_map/ppermute | solution.py:195
  31.8 9.1 %collective-permute-start.7 = (bf16[1024,128]{1,0:T(8,128)(2,1)S(1)}, bf16[1024,128]{1,0:T(8,128)(2,1)S(1)}, u32[]{:S(2)}, u32[]{:S(2)}) collective-permute-start(bf16[1024,128]{1,0:T(8,128)(2,1)S(1)} %shard_map.108), channel_id=1, source_target_pairs={{0,8},{8,0},{16,24},{24,16},{1,9},{9,1},{17,25},{25,17},{2,10},{10... | collective-permute-start | bytes 786440 | tf_op jit(solution)/shard_map/ppermute | solution.py:195

commit v5 on v4

--- a/solution.py
+++ b/solution.py
@@ -30,7 +30,7 @@
             query_at = lax.broadcasted_iota(jnp.int32, probs.shape, 1)
             probs = jnp.where(key_at <= query_at, probs, 0.0)
         ps[:, at : at + size] = probs.astype(BF16)
-        ds[:, at : at + size] = (probs * (grad_probs - delta[:, cols])).astype(BF16)
+        ds[:, at : at + size] = ((probs * SCALE) * (grad_probs - delta[:, cols])).astype(BF16)
 
 
 def key_terms(start, width, state, ps, ds):
@@ -38,7 +38,7 @@
     rows = pl.ds(start, width)
     grad_key = jnp.dot(ds[:, :width], q4[rows, :], preferred_element_type=F32)
     grad_value = jnp.dot(ps[:, :width], g4[rows, :], preferred_element_type=F32)
-    return grad_key * SCALE, grad_value
+    return grad_key, grad_value
 
 
 def prepare_kernel(log_norms, q, g, o, q4, g4, qt, gt, norm, delta):
@@ -128,7 +128,7 @@
     heads = dq.shape[1] // HD
     for a in range(2):
         for h in range(heads):
-            tile = dqt[:, pl.ds((a * heads + h) * size, size)] * SCALE
+            tile = dqt[:, pl.ds((a * heads + h) * size, size)]
             dq[pl.ds(a * size, size), pl.ds(h * HD, HD)] = tile.T.astype(BF16)
 
 
@@ -236,7 +236,7 @@
         same = prepare()
         kv_1 = [send(x, swap[1]) for x in own_rows]
         dqt, dk, dv = own(same)
-        kv_3 = [after(x, dk) for x in kv_3]
+        kv_3 = [after(kv_3[0], same[0]), after(kv_3[1], dk)]
         kv_2 = [send(x, swap[1]) for x in kv_3]
         dqt, part_3 = remote(3, kv_3, same, dqt)
         aside_3 = send(part_3, swap[1])

time: 44.3 us -> 44 us (level)
  Pallas kernels: 13.6 us -> 9.62 us
  waiting for transfers between devices: 10.7 us -> 14.6 us
    pallas_call x3, Pallas kernels: 8.52 us -> 4.5 us  [remote(): call(functools.partial(remote_kernel, partner), [(wide, F32), part_type],...]
    ppermute x9, waiting for transfers between devices: 10.7 us -> 14.6 us  [send(): return lax.ppermute(x, 'ctx', pairs)]
  transfers between devices with their start and end apart: 9 -> 9, of which waited for: 3 -> 4; matrix products, arithmetic and copies ran while one was open for 0% -> 0% of each run, Pallas kernels for 29% -> 20%
where the time goes in v5:
time: 44 us; the launch traced here: 43.6 us
  waiting for transfers between devices  14.6 us (33%)
  starting transfers between devices  14.2 us (32%)
  Pallas kernels  9.62 us (22%)
  local copies, waits for them, and re-layouts  4.5 us (10%)
  between operations  0.74 us (2%)
    ppermute x9, waiting for transfers between devices, send(): return lax.ppermute(x, 'ctx', pairs)  14.6 us
    ppermute x9, starting transfers between devices, send(): return lax.ppermute(x, 'ctx', pairs)  14.2 us
    unnamed x14, local copies, waits for them, and re-layouts  4.5 us
    pallas_call x3, Pallas kernels, remote(): call(functools.partial(remote_kernel, partner), [(wide, F32), part_type],...  4.5 us
    pallas_call x1, Pallas kernels, own(): call(own_kernel, [(wide, F32), sums_type, sums_type], [SMEM] + [VMEM] * 8...  2.57 us
    pallas_call x1, Pallas kernels, shards(): call(queries_kernel, [(queries.shape, BF16)], [VMEM], flops=WEIGHT * work)  1 us
  transfers between devices with their start and end apart: 9, of which 4 were waited for; matrix products, arithmetic and copies ran while one was open for 0% of the time, Pallas kernels for 20%

profile of v5, /device:TPU:0, one launch (start us, length us, event | category | flops | bytes accessed | tf_op | source)
XLA Modules:
  0.0 43.6 jit_solution(17374477873547463751)
XLA Ops:
  0.6 5.1 %collective-permute-start = (bf16[512,128]{1,0:T(8,128)(2,1)}, bf16[512,128]{1,0:T(8,128)(2,1)S(1)}, u32[]{:S(2)}, u32[]{:S(2)}) collective-permute-start(bf16[512,128]{1,0:T(8,128)(2,1)} %k.1), channel_id=1, source_target_pairs={{0,24},{8,16},{16,8},{24,0},{1,25},{9,17},{17,9},{25,1},{2,26},{10... | collective-permute-start | bytes 393224 | tf_op jit(solution)/shard_map/ppermute | solution.py:195
  5.7 0.9 %collective-permute-start.3 = (bf16[512,128]{1,0:T(8,128)(2,1)}, bf16[512,128]{1,0:T(8,128)(2,1)S(1)}, u32[]{:S(2)}, u32[]{:S(2)}) collective-permute-start(bf16[512,128]{1,0:T(8,128)(2,1)} %v.1), channel_id=1, source_target_pairs={{0,24},{8,16},{16,8},{24,0},{1,25},{9,17},{17,9},{25,1},{2,26},{10... | collective-permute-start | bytes 393224 | tf_op jit(solution)/shard_map/ppermute | solution.py:195
  6.6 1.1 %collective-permute-start.4 = (bf16[512,128]{1,0:T(8,128)(2,1)}, bf16[512,128]{1,0:T(8,128)(2,1)S(1)}, u32[]{:S(2)}, u32[]{:S(2)}) collective-permute-start(bf16[512,128]{1,0:T(8,128)(2,1)} %v.1), channel_id=1, source_target_pairs={{0,8},{8,0},{16,24},{24,16},{1,9},{9,1},{17,25},{25,17},{2,10},{10... | collective-permute-start | bytes 393224 | tf_op jit(solution)/shard_map/ppermute | solution.py:195
  7.8 1.0 %copy-done = bf16[512,512]{1,0:T(8,128)(2,1)S(1)} copy-done((bf16[512,512]{1,0:T(8,128)(2,1)S(1)}, bf16[512,512]{1,0:T(8,128)(2,1)}, u32[]{:S(2)}) %copy-start) | copy-done | bytes 524312
  8.8 1.0 %copy-done.1 = bf16[512,512]{1,0:T(8,128)(2,1)S(1)} copy-done((bf16[512,512]{1,0:T(8,128)(2,1)S(1)}, bf16[512,512]{1,0:T(8,128)(2,1)}, u32[]{:S(2)}) %copy-start.1) | copy-done | bytes 524312
  9.9 1.0 %copy-done.2 = bf16[512,512]{1,0:T(8,128)(2,1)S(1)} copy-done((bf16[512,512]{1,0:T(8,128)(2,1)S(1)}, bf16[512,512]{1,0:T(8,128)(2,1)}, u32[]{:S(2)}) %copy-start.2) | copy-done | bytes 524312
  10.9 0.7 %copy-done.5 = f32[4,512]{1,0:T(4,128)S(1)} copy-done((f32[4,512]{1,0:T(4,128)S(1)}, f32[4,512]{1,0:T(4,128)}, u32[]{:S(2)}) %copy-start.5) | copy-done | bytes 8216
  11.6 0.7 %shard_map.94 = (bf16[2048,128]{1,0:T(8,128)(2,1)S(1)}, bf16[2048,128]{1,0:T(8,128)(2,1)S(1)}, bf16[128,2048]{1,0:T(8,128)(2,1)S(1)}, bf16[128,2048]{1,0:T(8,128...) custom-call(f32[4,512]{1,0:T(4,128)S(1)} %copy-done.5, bf16[512,512]{1,0:T(8,128)(2,1)S(1)} %copy-done, ...), custom_call_target="tpu_custom_call" | custom-call | flops 1342177280 | tf_op jit(solution)/shard_map/pallas_call | solution.py:198
  12.6 0.5 %copy-done.6 = s32[8]{0:T(128)S(1)} copy-done((s32[8]{0:T(128)S(1)}, s32[8]{0:T(128)}, u32[]{:S(2)}) %copy-start.6) | copy-done | bytes 56
  13.0 2.6 %shard_map.96 = (f32[128,2048]{1,0:T(8,128)S(1)}, f32[512,128]{1,0:T(8,128)S(1)}, f32[512,128]{1,0:T(8,128)S(1)}) custom-call(s32[8]{0:T(128)S(1)} %copy-done.6, bf16[512,128]{1,0:T(8,128)(2,1)S(1)} %copy-done.4, bf16[512,128]{1,0:T(8,128)(2,1)S(1)} %copy-done.3, bf16[2048,128]{1,0:T(8,128)(2,1)S(1)} %get-tuple-element.20.refs_0_.q4, ...), custom_call_target="tpu_custom_call" | custom-call | flops 1342177280 | tf_op jit(solution)/shard_map/pallas_call | solution.py:206
  15.6 1.0 %collective-permute-start.1 = (bf16[512,128]{1,0:T(8,128)(2,1)S(1)}, bf16[512,128]{1,0:T(8,128)(2,1)S(1)}, u32[]{:S(2)}, u32[]{:S(2)}) collective-permute-start(bf16[512,128]{1,0:T(8,128)(2,1)S(1)} %shard_map.95.k), channel_id=1, source_target_pairs={{0,8},{8,0},{16,24},{24,16},{1,9},{9,1},{17,25},{25,17},{2,10},{10... | collective-permute-start | bytes 393224 | tf_op jit(solution)/shard_map/ppermute | solution.py:195
  16.6 1.1 %collective-permute-start.5 = (bf16[512,128]{1,0:T(8,128)(2,1)S(1)}, bf16[512,128]{1,0:T(8,128)(2,1)S(1)}, u32[]{:S(2)}, u32[]{:S(2)}) collective-permute-start(bf16[512,128]{1,0:T(8,128)(2,1)S(1)} %shard_map.97.v), channel_id=1, source_target_pairs={{0,8},{8,0},{16,24},{24,16},{1,9},{9,1},{17,25},{25,17},{2,10},{10... | collective-permute-start | bytes 393224 | tf_op jit(solution)/shard_map/ppermute | solution.py:195
  17.7 2.0 %shard_map.98 = (f32[128,2048]{1,0:T(8,128)S(1)}, bf16[1024,128]{1,0:T(8,128)(2,1)S(1)}) custom-call(s32[8]{0:T(128)S(1)} %copy-done.6, bf16[512,128]{1,0:T(8,128)(2,1)S(1)} %shard_map.95.k, bf16[512,128]{1,0:T(8,128)(2,1)S(1)} %shard_map.97.v, bf16[2048,128]{1,0:T(8,128)(2,1)S(1)} %get-tuple-element.20.refs_0_.q4, ...), custom_call_target="tpu_custom_call", output_to_operand_aliasing={{0}: (9, {})} | custom-call | flops 13421772800 | tf_op jit(solution)/shard_map/pallas_call | solution.py:216
  19.8 2.4 %collective-permute-start.6 = (bf16[1024,128]{1,0:T(8,128)(2,1)S(1)}, bf16[1024,128]{1,0:T(8,128)(2,1)S(1)}, u32[]{:S(2)}, u32[]{:S(2)}) collective-permute-start(bf16[1024,128]{1,0:T(8,128)(2,1)S(1)} %get-tuple-element.28.refs_0_), channel_id=1, source_target_pairs={{0,8},{8,0},{16,24},{24,16},{1,9},{9,1},{17,25},{25,17},{2,10},{10... | collective-permute-start | bytes 786440 | tf_op jit(solution)/shard_map/ppermute | solution.py:195
  22.1 0.9 %shard_map.101 = (f32[128,2048]{1,0:T(8,128)S(1)}, bf16[1024,128]{1,0:T(8,128)(2,1)S(1)}) custom-call(s32[8]{0:T(128)S(1)} %copy-done.6, bf16[512,128]{1,0:T(8,128)(2,1)S(1)} %shard_map.99.k, bf16[512,128]{1,0:T(8,128)(2,1)S(1)} %shard_map.100.v, bf16[2048,128]{1,0:T(8,128)(2,1)S(1)} %get-tuple-element.20.refs_0_.q4, ...), custom_call_target="tpu_custom_call", output_to_operand_aliasing={{0}: (9, {})} | custom-call | flops 13421772800 | tf_op jit(solution)/shard_map/pallas_call | solution.py:216
  23.1 1.8 %collective-permute-done.5.x = bf16[512,128]{1,0:T(8,128)(2,1)S(1)} collective-permute-done((bf16[512,128]{1,0:T(8,128)(2,1)S(1)}, bf16[512,128]{1,0:T(8,128)(2,1)S(1)}, u32[]{:S(2)}, u32[]{:S(2)}) %collective-permute-start.5) | collective-permute-done | bytes 131104 | tf_op jit(solution)/shard_map/ppermute | solution.py:195
  24.9 1.5 %shard_map.104 = (f32[128,2048]{1,0:T(8,128)S(1)}, bf16[1024,128]{1,0:T(8,128)(2,1)S(1)}) custom-call(s32[8]{0:T(128)S(1)} %copy-done.6, bf16[512,128]{1,0:T(8,128)(2,1)S(1)} %shard_map.102.k, bf16[512,128]{1,0:T(8,128)(2,1)S(1)} %shard_map.103.v, bf16[2048,128]{1,0:T(8,128)(2,1)S(1)} %get-tuple-element.20.refs_0_.q4, ...), custom_call_target="tpu_custom_call", output_to_operand_aliasing={{0}: (9, {})} | custom-call | flops 13421772800 | tf_op jit(solution)/shard_map/pallas_call | solution.py:216
  26.5 2.7 %collective-permute-done.6.x = bf16[1024,128]{1,0:T(8,128)(2,1)S(1)} collective-permute-done((bf16[1024,128]{1,0:T(8,128)(2,1)S(1)}, bf16[1024,128]{1,0:T(8,128)(2,1)S(1)}, u32[]{:S(2)}, u32[]{:S(2)}) %collective-permute-start.6) | collective-permute-done | bytes 262176 | tf_op jit(solution)/shard_map/ppermute | solution.py:195
  29.3 1.7 %collective-permute-start.8 = (bf16[1024,128]{1,0:T(8,128)(2,1)S(1)}, bf16[1024,128]{1,0:T(8,128)(2,1)S(1)}, u32[]{:S(2)}, u32[]{:S(2)}) collective-permute-start(bf16[1024,128]{1,0:T(8,128)(2,1)S(1)} %shard_map.107.refs_0_), channel_id=1, source_target_pairs={{0,16},{8,24},{16,0},{24,8},{1,17},{9,25},{17,1},{25,9},{2,18},{10... | collective-permute-start | bytes 786440 | tf_op jit(solution)/shard_map/ppermute | solution.py:195
  31.0 0.8 %collective-permute-start.7 = (bf16[1024,128]{1,0:T(8,128)(2,1)S(1)}, bf16[1024,128]{1,0:T(8,128)(2,1)S(1)}, u32[]{:S(2)}, u32[]{:S(2)}) collective-permute-start(bf16[1024,128]{1,0:T(8,128)(2,1)S(1)} %shard_map.108), channel_id=1, source_target_pairs={{0,8},{8,0},{16,24},{24,16},{1,9},{9,1},{17,25},{25,17},{2,10},{10... | collective-permute-start | bytes 786440 | tf_op jit(solution)/shard_map/ppermute | solution.py:195
  31.9 1.0 %shard_map.105 = bf16[512,512]{1,0:T(8,128)(2,1)} custom-call(f32[128,2048]{1,0:T(8,128)S(1)} %get-tuple-element.32.dqt), custom_call_target="tpu_custom_call" | custom-call | flops 13421772800 | tf_op jit(solution)/shard_map/pallas_call | solution.py:260
  32.9 7.6 %collective-permute-done.7.refs_0_ = bf16[1024,128]{1,0:T(8,128)(2,1)S(1)} collective-permute-done((bf16[1024,128]{1,0:T(8,128)(2,1)S(1)}, bf16[1024,128]{1,0:T(8,128)(2,1)S(1)}, u32[]{:S(2)}, u32[]{:S(2)}) %collective-permute-start.7) | collective-permute-done | bytes 262176 | tf_op jit(solution)/shard_map/ppermute | solution.py:195
  40.5 2.4 %collective-permute-done.8.refs_1_ = bf16[1024,128]{1,0:T(8,128)(2,1)S(1)} collective-permute-done((bf16[1024,128]{1,0:T(8,128)(2,1)S(1)}, bf16[1024,128]{1,0:T(8,128)(2,1)S(1)}, u32[]{:S(2)}, u32[]{:S(2)}) %collective-permute-start.8) | collective-permute-done | bytes 262176 | tf_op jit(solution)/shard_map/ppermute | solution.py:195
  42.9 0.7 %shard_map.109 = (bf16[512,128]{1,0:T(8,128)(2,1)}, bf16[512,128]{1,0:T(8,128)(2,1)}) custom-call(f32[512,128]{1,0:T(8,128)S(1)} %get-tuple-element.26.refs_0_.dk, f32[512,128]{1,0:T(8,128)S(1)} %get-tuple-element.33.dv, bf16[1024,128]{1,0:T(8,128)(2,1)S(1)} %collective-permute-done.7.refs_0_, bf16[1024,128]{1,0:T(8,128)(2,1)S(1)} %collective-permute-done.8.refs_1_), custom_call_target="tpu_custom_call" | custom-call | tf_op jit(solution)/shard_map/pallas_call | solution.py:226
  (24 shorter events, 0.3 us)
Async XLA Ops:
  0.6 15.0 %collective-permute-start = (bf16[512,128]{1,0:T(8,128)(2,1)}, bf16[512,128]{1,0:T(8,128)(2,1)S(1)}, u32[]{:S(2)}, u32[]{:S(2)}) collective-permute-start(bf16[512,128]{1,0:T(8,128)(2,1)} %k.1), channel_id=1, source_target_pairs={{0,24},{8,16},{16,8},{24,0},{1,25},{9,17},{17,9},{25,1},{2,26},{10... | collective-permute-start | bytes 393224 | tf_op jit(solution)/shard_map/ppermute | solution.py:195
  5.7 16.4 %collective-permute-start.2 = (bf16[512,128]{1,0:T(8,128)(2,1)}, bf16[512,128]{1,0:T(8,128)(2,1)S(1)}, u32[]{:S(2)}, u32[]{:S(2)}) collective-permute-start(bf16[512,128]{1,0:T(8,128)(2,1)} %k.1), channel_id=1, source_target_pairs={{0,8},{8,0},{16,24},{24,16},{1,9},{9,1},{17,25},{25,17},{2,10},{10... | collective-permute-start | bytes 393224 | tf_op jit(solution)/shard_map/ppermute | solution.py:195
  5.7 10.9 %collective-permute-start.3 = (bf16[512,128]{1,0:T(8,128)(2,1)}, bf16[512,128]{1,0:T(8,128)(2,1)S(1)}, u32[]{:S(2)}, u32[]{:S(2)}) collective-permute-start(bf16[512,128]{1,0:T(8,128)(2,1)} %v.1), channel_id=1, source_target_pairs={{0,24},{8,16},{16,8},{24,0},{1,25},{9,17},{17,9},{25,1},{2,26},{10... | collective-permute-start | bytes 393224 | tf_op jit(solution)/shard_map/ppermute | solution.py:195
  6.6 15.5 %collective-permute-start.4 = (bf16[512,128]{1,0:T(8,128)(2,1)}, bf16[512,128]{1,0:T(8,128)(2,1)S(1)}, u32[]{:S(2)}, u32[]{:S(2)}) collective-permute-start(bf16[512,128]{1,0:T(8,128)(2,1)} %v.1), channel_id=1, source_target_pairs={{0,8},{8,0},{16,24},{24,16},{1,9},{9,1},{17,25},{25,17},{2,10},{10... | collective-permute-start | bytes 393224 | tf_op jit(solution)/shard_map/ppermute | solution.py:195
  7.8 1.0 %copy-start = (bf16[512,512]{1,0:T(8,128)(2,1)S(1)}, bf16[512,512]{1,0:T(8,128)(2,1)}, u32[]{:S(2)}) copy-start(bf16[512,512]{1,0:T(8,128)(2,1)} %q.1) | copy-start | bytes 1572868
  8.8 1.0 %copy-start.1 = (bf16[512,512]{1,0:T(8,128)(2,1)S(1)}, bf16[512,512]{1,0:T(8,128)(2,1)}, u32[]{:S(2)}) copy-start(bf16[512,512]{1,0:T(8,128)(2,1)} %g.1) | copy-start | bytes 1572868
  9.9 1.0 %copy-start.2 = (bf16[512,512]{1,0:T(8,128)(2,1)S(1)}, bf16[512,512]{1,0:T(8,128)(2,1)}, u32[]{:S(2)}) copy-start(bf16[512,512]{1,0:T(8,128)(2,1)} %o.1) | copy-start | bytes 1572868
  10.9 0.7 %copy-start.5 = (f32[4,512]{1,0:T(4,128)S(1)}, f32[4,512]{1,0:T(4,128)}, u32[]{:S(2)}) copy-start(f32[4,512]{1,0:T(4,128)} %log_norms.1) | copy-start | bytes 24580
  11.6 0.9 %copy-start.3 = (bf16[512,128]{1,0:T(8,128)(2,1)S(1)}, bf16[512,128]{1,0:T(8,128)(2,1)}, u32[]{:S(2)}) copy-start(bf16[512,128]{1,0:T(8,128)(2,1)} %v.1) | copy-start | bytes 393220
  11.6 1.0 %copy-start.4 = (bf16[512,128]{1,0:T(8,128)(2,1)S(1)}, bf16[512,128]{1,0:T(8,128)(2,1)}, u32[]{:S(2)}) copy-start(bf16[512,128]{1,0:T(8,128)(2,1)} %k.1) | copy-start | bytes 393220
  12.4 0.7 %copy-start.6 = (s32[8]{0:T(128)S(1)}, s32[8]{0:T(128)}, u32[]{:S(2)}) copy-start(s32[8]{0:T(128)} %order.7) | copy-start | bytes 100
  15.6 7.5 %collective-permute-start.1 = (bf16[512,128]{1,0:T(8,128)(2,1)S(1)}, bf16[512,128]{1,0:T(8,128)(2,1)S(1)}, u32[]{:S(2)}, u32[]{:S(2)}) collective-permute-start(bf16[512,128]{1,0:T(8,128)(2,1)S(1)} %shard_map.95.k), channel_id=1, source_target_pairs={{0,8},{8,0},{16,24},{24,16},{1,9},{9,1},{17,25},{25,17},{2,10},{10... | collective-permute-start | bytes 393224 | tf_op jit(solution)/shard_map/ppermute | solution.py:195
  16.6 8.3 %collective-permute-start.5 = (bf16[512,128]{1,0:T(8,128)(2,1)S(1)}, bf16[512,128]{1,0:T(8,128)(2,1)S(1)}, u32[]{:S(2)}, u32[]{:S(2)}) collective-permute-start(bf16[512,128]{1,0:T(8,128)(2,1)S(1)} %shard_map.97.v), channel_id=1, source_target_pairs={{0,8},{8,0},{16,24},{24,16},{1,9},{9,1},{17,25},{25,17},{2,10},{10... | collective-permute-start | bytes 393224 | tf_op jit(solution)/shard_map/ppermute | solution.py:195
  19.8 9.4 %collective-permute-start.6 = (bf16[1024,128]{1,0:T(8,128)(2,1)S(1)}, bf16[1024,128]{1,0:T(8,128)(2,1)S(1)}, u32[]{:S(2)}, u32[]{:S(2)}) collective-permute-start(bf16[1024,128]{1,0:T(8,128)(2,1)S(1)} %get-tuple-element.28.refs_0_), channel_id=1, source_target_pairs={{0,8},{8,0},{16,24},{24,16},{1,9},{9,1},{17,25},{25,17},{2,10},{10... | collective-permute-start | bytes 786440 | tf_op jit(solution)/shard_map/ppermute | solution.py:195
  29.3 13.6 %collective-permute-start.8 = (bf16[1024,128]{1,0:T(8,128)(2,1)S(1)}, bf16[1024,128]{1,0:T(8,128)(2,1)S(1)}, u32[]{:S(2)}, u32[]{:S(2)}) collective-permute-start(bf16[1024,128]{1,0:T(8,128)(2,1)S(1)} %shard_map.107.refs_0_), channel_id=1, source_target_pairs={{0,16},{8,24},{16,0},{24,8},{1,17},{9,25},{17,1},{25,9},{2,18},{10... | collective-permute-start | bytes 786440 | tf_op jit(solution)/shard_map/ppermute | solution.py:195
  31.0 9.5 %collective-permute-start.7 = (bf16[1024,128]{1,0:T(8,128)(2,1)S(1)}, bf16[1024,128]{1,0:T(8,128)(2,1)S(1)}, u32[]{:S(2)}, u32[]{:S(2)}) collective-permute-start(bf16[1024,128]{1,0:T(8,128)(2,1)S(1)} %shard_map.108), channel_id=1, source_target_pairs={{0,8},{8,0},{16,24},{24,16},{1,9},{9,1},{17,25},{25,17},{2,10},{10... | collective-permute-start | bytes 786440 | tf_op jit(solution)/shard_map/ppermute | solution.py:195

commit v6 on v5

--- a/solution.py
+++ b/solution.py
@@ -236,7 +236,7 @@
         same = prepare()
         kv_1 = [send(x, swap[1]) for x in own_rows]
         dqt, dk, dv = own(same)
-        kv_3 = [after(kv_3[0], same[0]), after(kv_3[1], dk)]
+        kv_3 = [after(x, dk) for x in kv_3]
         kv_2 = [send(x, swap[1]) for x in kv_3]
         dqt, part_3 = remote(3, kv_3, same, dqt)
         aside_3 = send(part_3, swap[1])

time: 44 us -> 43.9 us (level)
  Pallas kernels: 9.62 us -> 13.4 us
  waiting for transfers between devices: 14.6 us -> 11.7 us
  starting transfers between devices: 14.2 us -> 13.1 us
    pallas_call x3, Pallas kernels: 4.5 us -> 8.25 us  [remote(): call(functools.partial(remote_kernel, partner), [(wide, F32), part_type],...]
    ppermute x9, waiting for transfers between devices: 14.6 us -> 11.7 us  [send(): return lax.ppermute(x, 'ctx', pairs)]
    ppermute x9, starting transfers between devices: 14.2 us -> 13.1 us  [send(): return lax.ppermute(x, 'ctx', pairs)]
  transfers between devices with their start and end apart: 9 -> 9, of which waited for: 4 -> 4; matrix products, arithmetic and copies ran while one was open for 0% -> 0% of each run, Pallas kernels for 20% -> 29%
where the time goes in v6:
time: 43.9 us; the launch traced here: 43.5 us
  Pallas kernels  13.4 us (31%)
  starting transfers between devices  13.1 us (30%)
  waiting for transfers between devices  11.7 us (27%)
  local copies, waits for them, and re-layouts  4.5 us (10%)
  between operations  0.76 us (2%)
    ppermute x9, starting transfers between devices, send(): return lax.ppermute(x, 'ctx', pairs)  13.1 us
    ppermute x9, waiting for transfers between devices, send(): return lax.ppermute(x, 'ctx', pairs)  11.7 us
    pallas_call x3, Pallas kernels, remote(): call(functools.partial(remote_kernel, partner), [(wide, F32), part_type],...  8.25 us
    unnamed x14, local copies, waits for them, and re-layouts  4.5 us
    pallas_call x1, Pallas kernels, own(): call(own_kernel, [(wide, F32), sums_type, sums_type], [SMEM] + [VMEM] * 8...  2.57 us
    pallas_call x1, Pallas kernels, shards(): call(queries_kernel, [(queries.shape, BF16)], [VMEM], flops=WEIGHT * work)  1 us
  transfers between devices with their start and end apart: 9, of which 4 were waited for; matrix products, arithmetic and copies ran while one was open for 0% of the time, Pallas kernels for 29%

profile of v6, /device:TPU:0, one launch (start us, length us, event | category | flops | bytes accessed | tf_op | source)
XLA Modules:
  0.0 43.5 jit_solution(10517932065405603549)
XLA Ops:
  0.6 5.1 %collective-permute-start = (bf16[512,128]{1,0:T(8,128)(2,1)}, bf16[512,128]{1,0:T(8,128)(2,1)S(1)}, u32[]{:S(2)}, u32[]{:S(2)}) collective-permute-start(bf16[512,128]{1,0:T(8,128)(2,1)} %k.1), channel_id=1, source_target_pairs={{0,24},{8,16},{16,8},{24,0},{1,25},{9,17},{17,9},{25,1},{2,26},{10... | collective-permute-start | bytes 393224 | tf_op jit(solution)/shard_map/ppermute | solution.py:195
  5.7 2.0 %collective-permute-start.4 = (bf16[512,128]{1,0:T(8,128)(2,1)}, bf16[512,128]{1,0:T(8,128)(2,1)S(1)}, u32[]{:S(2)}, u32[]{:S(2)}) collective-permute-start(bf16[512,128]{1,0:T(8,128)(2,1)} %v.1), channel_id=1, source_target_pairs={{0,8},{8,0},{16,24},{24,16},{1,9},{9,1},{17,25},{25,17},{2,10},{10... | collective-permute-start | bytes 393224 | tf_op jit(solution)/shard_map/ppermute | solution.py:195
  7.8 0.1 collective-permute-start.3
  7.9 1.0 %copy-done = bf16[512,512]{1,0:T(8,128)(2,1)S(1)} copy-done((bf16[512,512]{1,0:T(8,128)(2,1)S(1)}, bf16[512,512]{1,0:T(8,128)(2,1)}, u32[]{:S(2)}) %copy-start) | copy-done | bytes 524312
  8.9 1.0 %copy-done.1 = bf16[512,512]{1,0:T(8,128)(2,1)S(1)} copy-done((bf16[512,512]{1,0:T(8,128)(2,1)S(1)}, bf16[512,512]{1,0:T(8,128)(2,1)}, u32[]{:S(2)}) %copy-start.1) | copy-done | bytes 524312
  9.9 1.0 %copy-done.2 = bf16[512,512]{1,0:T(8,128)(2,1)S(1)} copy-done((bf16[512,512]{1,0:T(8,128)(2,1)S(1)}, bf16[512,512]{1,0:T(8,128)(2,1)}, u32[]{:S(2)}) %copy-start.2) | copy-done | bytes 524312
  11.0 0.7 %copy-done.5 = f32[4,512]{1,0:T(4,128)S(1)} copy-done((f32[4,512]{1,0:T(4,128)S(1)}, f32[4,512]{1,0:T(4,128)}, u32[]{:S(2)}) %copy-start.5) | copy-done | bytes 8216
  11.7 0.7 %shard_map.94 = (bf16[2048,128]{1,0:T(8,128)(2,1)S(1)}, bf16[2048,128]{1,0:T(8,128)(2,1)S(1)}, bf16[128,2048]{1,0:T(8,128)(2,1)S(1)}, bf16[128,2048]{1,0:T(8,128...) custom-call(f32[4,512]{1,0:T(4,128)S(1)} %copy-done.5, bf16[512,512]{1,0:T(8,128)(2,1)S(1)} %copy-done, ...), custom_call_target="tpu_custom_call" | custom-call | flops 1342177280 | tf_op jit(solution)/shard_map/pallas_call | solution.py:198
  12.4 0.1 copy-done.3
  12.6 0.5 %copy-done.6 = s32[8]{0:T(128)S(1)} copy-done((s32[8]{0:T(128)S(1)}, s32[8]{0:T(128)}, u32[]{:S(2)}) %copy-start.6) | copy-done | bytes 56
  13.1 2.6 %shard_map.95 = (f32[128,2048]{1,0:T(8,128)S(1)}, f32[512,128]{1,0:T(8,128)S(1)}, f32[512,128]{1,0:T(8,128)S(1)}) custom-call(s32[8]{0:T(128)S(1)} %copy-done.6, bf16[512,128]{1,0:T(8,128)(2,1)S(1)} %copy-done.4, bf16[512,128]{1,0:T(8,128)(2,1)S(1)} %copy-done.3, bf16[2048,128]{1,0:T(8,128)(2,1)S(1)} %get-tuple-element.20.q4, ...), custom_call_target="tpu_custom_call" | custom-call | flops 1342177280 | tf_op jit(solution)/shard_map/pallas_call | solution.py:206
  15.7 0.1 collective-permute-start.1
  15.8 2.6 %collective-permute-done.3.x = bf16[512,128]{1,0:T(8,128)(2,1)S(1)} collective-permute-done((bf16[512,128]{1,0:T(8,128)(2,1)}, bf16[512,128]{1,0:T(8,128)(2,1)S(1)}, u32[]{:S(2)}, u32[]{:S(2)}) %collective-permute-start.3) | collective-permute-done | bytes 131104 | tf_op jit(solution)/shard_map/ppermute | solution.py:195
  18.4 3.0 %shard_map.98 = (f32[128,2048]{1,0:T(8,128)S(1)}, bf16[1024,128]{1,0:T(8,128)(2,1)S(1)}) custom-call(s32[8]{0:T(128)S(1)} %copy-done.6, bf16[512,128]{1,0:T(8,128)(2,1)S(1)} %shard_map.96.k, bf16[512,128]{1,0:T(8,128)(2,1)S(1)} %shard_map.97.v, bf16[2048,128]{1,0:T(8,128)(2,1)S(1)} %get-tuple-element.20.q4, ...), custom_call_target="tpu_custom_call", output_to_operand_aliasing={{0}: (9, {})} | custom-call | flops 13421772800 | tf_op jit(solution)/shard_map/pallas_call | solution.py:216
  21.4 1.5 %collective-permute-start.6 = (bf16[1024,128]{1,0:T(8,128)(2,1)S(1)}, bf16[1024,128]{1,0:T(8,128)(2,1)S(1)}, u32[]{:S(2)}, u32[]{:S(2)}) collective-permute-start(bf16[1024,128]{1,0:T(8,128)(2,1)S(1)} %get-tuple-element.28.refs_0_), channel_id=1, source_target_pairs={{0,8},{8,0},{16,24},{24,16},{1,9},{9,1},{17,25},{25,17},{2,10},{10... | collective-permute-start | bytes 786440 | tf_op jit(solution)/shard_map/ppermute | solution.py:195
  22.8 3.0 %shard_map.101 = (f32[128,2048]{1,0:T(8,128)S(1)}, bf16[1024,128]{1,0:T(8,128)(2,1)S(1)}) custom-call(s32[8]{0:T(128)S(1)} %copy-done.6, bf16[512,128]{1,0:T(8,128)(2,1)S(1)} %shard_map.99.k, bf16[512,128]{1,0:T(8,128)(2,1)S(1)} %shard_map.100.v, bf16[2048,128]{1,0:T(8,128)(2,1)S(1)} %get-tuple-element.20.q4, ...), custom_call_target="tpu_custom_call", output_to_operand_aliasing={{0}: (9, {})} | custom-call | flops 13421772800 | tf_op jit(solution)/shard_map/pallas_call | solution.py:216
  25.9 2.3 %shard_map.104 = (f32[128,2048]{1,0:T(8,128)S(1)}, bf16[1024,128]{1,0:T(8,128)(2,1)S(1)}) custom-call(s32[8]{0:T(128)S(1)} %copy-done.6, bf16[512,128]{1,0:T(8,128)(2,1)S(1)} %shard_map.102.k, bf16[512,128]{1,0:T(8,128)(2,1)S(1)} %shard_map.103.v, bf16[2048,128]{1,0:T(8,128)(2,1)S(1)} %get-tuple-element.20.q4, ...), custom_call_target="tpu_custom_call", output_to_operand_aliasing={{0}: (9, {})} | custom-call | flops 13421772800 | tf_op jit(solution)/shard_map/pallas_call | solution.py:216
  28.2 1.0 %collective-permute-done.6.x = bf16[1024,128]{1,0:T(8,128)(2,1)S(1)} collective-permute-done((bf16[1024,128]{1,0:T(8,128)(2,1)S(1)}, bf16[1024,128]{1,0:T(8,128)(2,1)S(1)}, u32[]{:S(2)}, u32[]{:S(2)}) %collective-permute-start.6) | collective-permute-done | bytes 262176 | tf_op jit(solution)/shard_map/ppermute | solution.py:195
  29.3 2.5 %collective-permute-start.8 = (bf16[1024,128]{1,0:T(8,128)(2,1)S(1)}, bf16[1024,128]{1,0:T(8,128)(2,1)S(1)}, u32[]{:S(2)}, u32[]{:S(2)}) collective-permute-start(bf16[1024,128]{1,0:T(8,128)(2,1)S(1)} %shard_map.107.refs_0_), channel_id=1, source_target_pairs={{0,16},{8,24},{16,0},{24,8},{1,17},{9,25},{17,1},{25,9},{2,18},{10... | collective-permute-start | bytes 786440 | tf_op jit(solution)/shard_map/ppermute | solution.py:195
  31.8 1.8 %collective-permute-start.7 = (bf16[1024,128]{1,0:T(8,128)(2,1)S(1)}, bf16[1024,128]{1,0:T(8,128)(2,1)S(1)}, u32[]{:S(2)}, u32[]{:S(2)}) collective-permute-start(bf16[1024,128]{1,0:T(8,128)(2,1)S(1)} %shard_map.108), channel_id=1, source_target_pairs={{0,8},{8,0},{16,24},{24,16},{1,9},{9,1},{17,25},{25,17},{2,10},{10... | collective-permute-start | bytes 786440 | tf_op jit(solution)/shard_map/ppermute | solution.py:195
  33.6 1.0 %shard_map.105 = bf16[512,512]{1,0:T(8,128)(2,1)} custom-call(f32[128,2048]{1,0:T(8,128)S(1)} %get-tuple-element.32.dqt), custom_call_target="tpu_custom_call" | custom-call | flops 13421772800 | tf_op jit(solution)/shard_map/pallas_call | solution.py:260
  34.6 6.3 %collective-permute-done.7.refs_0_ = bf16[1024,128]{1,0:T(8,128)(2,1)S(1)} collective-permute-done((bf16[1024,128]{1,0:T(8,128)(2,1)S(1)}, bf16[1024,128]{1,0:T(8,128)(2,1)S(1)}, u32[]{:S(2)}, u32[]{:S(2)}) %collective-permute-start.7) | collective-permute-done | bytes 262176 | tf_op jit(solution)/shard_map/ppermute | solution.py:195
  41.0 1.8 %collective-permute-done.8.refs_1_ = bf16[1024,128]{1,0:T(8,128)(2,1)S(1)} collective-permute-done((bf16[1024,128]{1,0:T(8,128)(2,1)S(1)}, bf16[1024,128]{1,0:T(8,128)(2,1)S(1)}, u32[]{:S(2)}, u32[]{:S(2)}) %collective-permute-start.8) | collective-permute-done | bytes 262176 | tf_op jit(solution)/shard_map/ppermute | solution.py:195
  42.7 0.7 %shard_map.109 = (bf16[512,128]{1,0:T(8,128)(2,1)}, bf16[512,128]{1,0:T(8,128)(2,1)}) custom-call(f32[512,128]{1,0:T(8,128)S(1)} %get-tuple-element.26.refs_0_.dk, f32[512,128]{1,0:T(8,128)S(1)} %get-tuple-element.33.dv, bf16[1024,128]{1,0:T(8,128)(2,1)S(1)} %collective-permute-done.7.refs_0_, bf16[1024,128]{1,0:T(8,128)(2,1)S(1)} %collective-permute-done.8.refs_1_), custom_call_target="tpu_custom_call" | custom-call | tf_op jit(solution)/shard_map/pallas_call | solution.py:226
  (24 shorter events, 0.2 us)
Async XLA Ops:
  0.6 15.1 %collective-permute-start = (bf16[512,128]{1,0:T(8,128)(2,1)}, bf16[512,128]{1,0:T(8,128)(2,1)S(1)}, u32[]{:S(2)}, u32[]{:S(2)}) collective-permute-start(bf16[512,128]{1,0:T(8,128)(2,1)} %k.1), channel_id=1, source_target_pairs={{0,24},{8,16},{16,8},{24,0},{1,25},{9,17},{17,9},{25,1},{2,26},{10... | collective-permute-start | bytes 393224 | tf_op jit(solution)/shard_map/ppermute | solution.py:195
  5.7 17.1 %collective-permute-start.2 = (bf16[512,128]{1,0:T(8,128)(2,1)}, bf16[512,128]{1,0:T(8,128)(2,1)S(1)}, u32[]{:S(2)}, u32[]{:S(2)}) collective-permute-start(bf16[512,128]{1,0:T(8,128)(2,1)} %k.1), channel_id=1, source_target_pairs={{0,8},{8,0},{16,24},{24,16},{1,9},{9,1},{17,25},{25,17},{2,10},{10... | collective-permute-start | bytes 393224 | tf_op jit(solution)/shard_map/ppermute | solution.py:195
  5.7 17.1 %collective-permute-start.4 = (bf16[512,128]{1,0:T(8,128)(2,1)}, bf16[512,128]{1,0:T(8,128)(2,1)S(1)}, u32[]{:S(2)}, u32[]{:S(2)}) collective-permute-start(bf16[512,128]{1,0:T(8,128)(2,1)} %v.1), channel_id=1, source_target_pairs={{0,8},{8,0},{16,24},{24,16},{1,9},{9,1},{17,25},{25,17},{2,10},{10... | collective-permute-start | bytes 393224 | tf_op jit(solution)/shard_map/ppermute | solution.py:195
  7.8 10.6 %collective-permute-start.3 = (bf16[512,128]{1,0:T(8,128)(2,1)}, bf16[512,128]{1,0:T(8,128)(2,1)S(1)}, u32[]{:S(2)}, u32[]{:S(2)}) collective-permute-start(bf16[512,128]{1,0:T(8,128)(2,1)} %v.1), channel_id=1, source_target_pairs={{0,24},{8,16},{16,8},{24,0},{1,25},{9,17},{17,9},{25,1},{2,26},{10... | collective-permute-start | bytes 393224 | tf_op jit(solution)/shard_map/ppermute | solution.py:195
  7.9 1.0 %copy-start = (bf16[512,512]{1,0:T(8,128)(2,1)S(1)}, bf16[512,512]{1,0:T(8,128)(2,1)}, u32[]{:S(2)}) copy-start(bf16[512,512]{1,0:T(8,128)(2,1)} %q.1) | copy-start | bytes 1572868
  8.9 1.0 %copy-start.1 = (bf16[512,512]{1,0:T(8,128)(2,1)S(1)}, bf16[512,512]{1,0:T(8,128)(2,1)}, u32[]{:S(2)}) copy-start(bf16[512,512]{1,0:T(8,128)(2,1)} %g.1) | copy-start | bytes 1572868
  9.9 1.0 %copy-start.2 = (bf16[512,512]{1,0:T(8,128)(2,1)S(1)}, bf16[512,512]{1,0:T(8,128)(2,1)}, u32[]{:S(2)}) copy-start(bf16[512,512]{1,0:T(8,128)(2,1)} %o.1) | copy-start | bytes 1572868
  11.0 0.7 %copy-start.5 = (f32[4,512]{1,0:T(4,128)S(1)}, f32[4,512]{1,0:T(4,128)}, u32[]{:S(2)}) copy-start(f32[4,512]{1,0:T(4,128)} %log_norms.1) | copy-start | bytes 24580
  11.7 0.9 %copy-start.3 = (bf16[512,128]{1,0:T(8,128)(2,1)S(1)}, bf16[512,128]{1,0:T(8,128)(2,1)}, u32[]{:S(2)}) copy-start(bf16[512,128]{1,0:T(8,128)(2,1)} %v.1) | copy-start | bytes 393220
  11.7 1.0 %copy-start.4 = (bf16[512,128]{1,0:T(8,128)(2,1)S(1)}, bf16[512,128]{1,0:T(8,128)(2,1)}, u32[]{:S(2)}) copy-start(bf16[512,128]{1,0:T(8,128)(2,1)} %k.1) | copy-start | bytes 393220
  12.4 0.7 %copy-start.6 = (s32[8]{0:T(128)S(1)}, s32[8]{0:T(128)}, u32[]{:S(2)}) copy-start(s32[8]{0:T(128)} %order.7) | copy-start | bytes 100
  15.7 10.1 %collective-permute-start.1 = (bf16[512,128]{1,0:T(8,128)(2,1)S(1)}, bf16[512,128]{1,0:T(8,128)(2,1)S(1)}, u32[]{:S(2)}, u32[]{:S(2)}) collective-permute-start(bf16[512,128]{1,0:T(8,128)(2,1)S(1)} %shard_map.96.k), channel_id=1, source_target_pairs={{0,8},{8,0},{16,24},{24,16},{1,9},{9,1},{17,25},{25,17},{2,10},{10... | collective-permute-start | bytes 393224 | tf_op jit(solution)/shard_map/ppermute | solution.py:195
  18.4 7.4 %collective-permute-start.5 = (bf16[512,128]{1,0:T(8,128)(2,1)S(1)}, bf16[512,128]{1,0:T(8,128)(2,1)S(1)}, u32[]{:S(2)}, u32[]{:S(2)}) collective-permute-start(bf16[512,128]{1,0:T(8,128)(2,1)S(1)} %shard_map.97.v), channel_id=1, source_target_pairs={{0,8},{8,0},{16,24},{24,16},{1,9},{9,1},{17,25},{25,17},{2,10},{10... | collective-permute-start | bytes 393224 | tf_op jit(solution)/shard_map/ppermute | solution.py:195
  21.4 7.9 %collective-permute-start.6 = (bf16[1024,128]{1,0:T(8,128)(2,1)S(1)}, bf16[1024,128]{1,0:T(8,128)(2,1)S(1)}, u32[]{:S(2)}, u32[]{:S(2)}) collective-permute-start(bf16[1024,128]{1,0:T(8,128)(2,1)S(1)} %get-tuple-element.28.refs_0_), channel_id=1, source_target_pairs={{0,8},{8,0},{16,24},{24,16},{1,9},{9,1},{17,25},{25,17},{2,10},{10... | collective-permute-start | bytes 786440 | tf_op jit(solution)/shard_map/ppermute | solution.py:195
  29.3 13.4 %collective-permute-start.8 = (bf16[1024,128]{1,0:T(8,128)(2,1)S(1)}, bf16[1024,128]{1,0:T(8,128)(2,1)S(1)}, u32[]{:S(2)}, u32[]{:S(2)}) collective-permute-start(bf16[1024,128]{1,0:T(8,128)(2,1)S(1)} %shard_map.107.refs_0_), channel_id=1, source_target_pairs={{0,16},{8,24},{16,0},{24,8},{1,17},{9,25},{17,1},{25,9},{2,18},{10... | collective-permute-start | bytes 786440 | tf_op jit(solution)/shard_map/ppermute | solution.py:195
  31.8 9.1 %collective-permute-start.7 = (bf16[1024,128]{1,0:T(8,128)(2,1)S(1)}, bf16[1024,128]{1,0:T(8,128)(2,1)S(1)}, u32[]{:S(2)}, u32[]{:S(2)}) collective-permute-start(bf16[1024,128]{1,0:T(8,128)(2,1)S(1)} %shard_map.108), channel_id=1, source_target_pairs={{0,8},{8,0},{16,24},{24,16},{1,9},{9,1},{17,25},{25,17},{2,10},{10... | collective-permute-start | bytes 786440 | tf_op jit(solution)/shard_map/ppermute | solution.py:195

commit v7 on v5

--- a/solution.py
+++ b/solution.py
@@ -247,7 +247,8 @@
         both = add(after(aside_3, part_2), part_2)
         back_2 = send(both, swap[2])
         back_1 = send(after(part_1, both), swap[1])
-        returned = [back_1, back_2]
+        dk, dv = sums(dk, dv, [back_1], [sums_type] * 2)
+        returned = [back_2]
     else:
         same = prepare()
         dqt, dk, dv = own(same)

time: 44 us -> 44 us (level)
  starting transfers between devices: 14.2 us -> 12.2 us
  Pallas kernels: 9.62 us -> 11.4 us
    ppermute x9, starting transfers between devices: 14.2 us -> 12.2 us  [send(): return lax.ppermute(x, 'ctx', pairs)]
    pallas_call x3, Pallas kernels: 4.5 us -> 6.28 us  [remote(): call(functools.partial(remote_kernel, partner), [(wide, F32), part_type],...]
  transfers between devices with their start and end apart: 9 -> 9, of which waited for: 4 -> 4; matrix products, arithmetic and copies ran while one was open for 0% -> 0% of each run, Pallas kernels for 20% -> 24%
where the time goes in v7:
time: 44 us; the launch traced here: 43.6 us
  waiting for transfers between devices  14.8 us (34%)
  starting transfers between devices  12.2 us (28%)
  Pallas kernels  11.4 us (26%)
  local copies, waits for them, and re-layouts  4.5 us (10%)
  between operations  0.74 us (2%)
    ppermute x9, waiting for transfers between devices, send(): return lax.ppermute(x, 'ctx', pairs)  14.8 us
    ppermute x9, starting transfers between devices, send(): return lax.ppermute(x, 'ctx', pairs)  12.2 us
    pallas_call x3, Pallas kernels, remote(): call(functools.partial(remote_kernel, partner), [(wide, F32), part_type],...  6.28 us
    unnamed x14, local copies, waits for them, and re-layouts  4.5 us
    pallas_call x1, Pallas kernels, own(): call(own_kernel, [(wide, F32), sums_type, sums_type], [SMEM] + [VMEM] * 8...  2.57 us
    pallas_call x1, Pallas kernels, shards(): call(queries_kernel, [(queries.shape, BF16)], [VMEM], flops=WEIGHT * work)  1 us
  transfers between devices with their start and end apart: 9, of which 4 were waited for; matrix products, arithmetic and copies ran while one was open for 0% of the time, Pallas kernels for 24%

profile of v7, /device:TPU:0, one launch (start us, length us, event | category | flops | bytes accessed | tf_op | source)
XLA Modules:
  0.0 43.6 jit_solution(8544167357691054563)
XLA Ops:
  0.6 5.1 %collective-permute-start = (bf16[512,128]{1,0:T(8,128)(2,1)}, bf16[512,128]{1,0:T(8,128)(2,1)S(1)}, u32[]{:S(2)}, u32[]{:S(2)}) collective-permute-start(bf16[512,128]{1,0:T(8,128)(2,1)} %k.1), channel_id=1, source_target_pairs={{0,24},{8,16},{16,8},{24,0},{1,25},{9,17},{17,9},{25,1},{2,26},{10... | collective-permute-start | bytes 393224 | tf_op jit(solution)/shard_map/ppermute | solution.py:195
  5.7 0.9 %collective-permute-start.3 = (bf16[512,128]{1,0:T(8,128)(2,1)}, bf16[512,128]{1,0:T(8,128)(2,1)S(1)}, u32[]{:S(2)}, u32[]{:S(2)}) collective-permute-start(bf16[512,128]{1,0:T(8,128)(2,1)} %v.1), channel_id=1, source_target_pairs={{0,24},{8,16},{16,8},{24,0},{1,25},{9,17},{17,9},{25,1},{2,26},{10... | collective-permute-start | bytes 393224 | tf_op jit(solution)/shard_map/ppermute | solution.py:195
  6.6 1.1 %collective-permute-start.4 = (bf16[512,128]{1,0:T(8,128)(2,1)}, bf16[512,128]{1,0:T(8,128)(2,1)S(1)}, u32[]{:S(2)}, u32[]{:S(2)}) collective-permute-start(bf16[512,128]{1,0:T(8,128)(2,1)} %v.1), channel_id=1, source_target_pairs={{0,8},{8,0},{16,24},{24,16},{1,9},{9,1},{17,25},{25,17},{2,10},{10... | collective-permute-start | bytes 393224 | tf_op jit(solution)/shard_map/ppermute | solution.py:195
  7.8 1.0 %copy-done = bf16[512,512]{1,0:T(8,128)(2,1)S(1)} copy-done((bf16[512,512]{1,0:T(8,128)(2,1)S(1)}, bf16[512,512]{1,0:T(8,128)(2,1)}, u32[]{:S(2)}) %copy-start) | copy-done | bytes 524312
  8.8 1.0 %copy-done.1 = bf16[512,512]{1,0:T(8,128)(2,1)S(1)} copy-done((bf16[512,512]{1,0:T(8,128)(2,1)S(1)}, bf16[512,512]{1,0:T(8,128)(2,1)}, u32[]{:S(2)}) %copy-start.1) | copy-done | bytes 524312
  9.9 1.0 %copy-done.2 = bf16[512,512]{1,0:T(8,128)(2,1)S(1)} copy-done((bf16[512,512]{1,0:T(8,128)(2,1)S(1)}, bf16[512,512]{1,0:T(8,128)(2,1)}, u32[]{:S(2)}) %copy-start.2) | copy-done | bytes 524312
  10.9 0.7 %copy-done.5 = f32[4,512]{1,0:T(4,128)S(1)} copy-done((f32[4,512]{1,0:T(4,128)S(1)}, f32[4,512]{1,0:T(4,128)}, u32[]{:S(2)}) %copy-start.5) | copy-done | bytes 8216
  11.6 0.7 %shard_map.94 = (bf16[2048,128]{1,0:T(8,128)(2,1)S(1)}, bf16[2048,128]{1,0:T(8,128)(2,1)S(1)}, bf16[128,2048]{1,0:T(8,128)(2,1)S(1)}, bf16[128,2048]{1,0:T(8,128...) custom-call(f32[4,512]{1,0:T(4,128)S(1)} %copy-done.5, bf16[512,512]{1,0:T(8,128)(2,1)S(1)} %copy-done, ...), custom_call_target="tpu_custom_call" | custom-call | flops 1342177280 | tf_op jit(solution)/shard_map/pallas_call | solution.py:198
  12.6 0.5 %copy-done.6 = s32[8]{0:T(128)S(1)} copy-done((s32[8]{0:T(128)S(1)}, s32[8]{0:T(128)}, u32[]{:S(2)}) %copy-start.6) | copy-done | bytes 56
  13.0 2.6 %shard_map.96 = (f32[128,2048]{1,0:T(8,128)S(1)}, f32[512,128]{1,0:T(8,128)S(1)}, f32[512,128]{1,0:T(8,128)S(1)}) custom-call(s32[8]{0:T(128)S(1)} %copy-done.6, bf16[512,128]{1,0:T(8,128)(2,1)S(1)} %copy-done.4, bf16[512,128]{1,0:T(8,128)(2,1)S(1)} %copy-done.3, bf16[2048,128]{1,0:T(8,128)(2,1)S(1)} %get-tuple-element.22.refs_0_.q4, ...), custom_call_target="tpu_custom_call" | custom-call | flops 1342177280 | tf_op jit(solution)/shard_map/pallas_call | solution.py:206
  15.6 1.0 %collective-permute-start.1 = (bf16[512,128]{1,0:T(8,128)(2,1)S(1)}, bf16[512,128]{1,0:T(8,128)(2,1)S(1)}, u32[]{:S(2)}, u32[]{:S(2)}) collective-permute-start(bf16[512,128]{1,0:T(8,128)(2,1)S(1)} %shard_map.95.k), channel_id=1, source_target_pairs={{0,8},{8,0},{16,24},{24,16},{1,9},{9,1},{17,25},{25,17},{2,10},{10... | collective-permute-start | bytes 393224 | tf_op jit(solution)/shard_map/ppermute | solution.py:195
  16.6 1.1 %collective-permute-start.5 = (bf16[512,128]{1,0:T(8,128)(2,1)S(1)}, bf16[512,128]{1,0:T(8,128)(2,1)S(1)}, u32[]{:S(2)}, u32[]{:S(2)}) collective-permute-start(bf16[512,128]{1,0:T(8,128)(2,1)S(1)} %shard_map.97.v), channel_id=1, source_target_pairs={{0,8},{8,0},{16,24},{24,16},{1,9},{9,1},{17,25},{25,17},{2,10},{10... | collective-permute-start | bytes 393224 | tf_op jit(solution)/shard_map/ppermute | solution.py:195
  17.7 3.0 %shard_map.98 = (f32[128,2048]{1,0:T(8,128)S(1)}, bf16[1024,128]{1,0:T(8,128)(2,1)S(1)}) custom-call(s32[8]{0:T(128)S(1)} %copy-done.6, bf16[512,128]{1,0:T(8,128)(2,1)S(1)} %shard_map.95.k, bf16[512,128]{1,0:T(8,128)(2,1)S(1)} %shard_map.97.v, bf16[2048,128]{1,0:T(8,128)(2,1)S(1)} %get-tuple-element.22.refs_0_.q4, ...), custom_call_target="tpu_custom_call", output_to_operand_aliasing={{0}: (9, {})} | custom-call | flops 13421772800 | tf_op jit(solution)/shard_map/pallas_call | solution.py:216
  20.7 0.3 collective-permute-start.6
  21.0 1.8 %shard_map.101 = (f32[128,2048]{1,0:T(8,128)S(1)}, bf16[1024,128]{1,0:T(8,128)(2,1)S(1)}) custom-call(s32[8]{0:T(128)S(1)} %copy-done.6, bf16[512,128]{1,0:T(8,128)(2,1)S(1)} %shard_map.99.k, bf16[512,128]{1,0:T(8,128)(2,1)S(1)} %shard_map.100.v, bf16[2048,128]{1,0:T(8,128)(2,1)S(1)} %get-tuple-element.22.refs_0_.q4, ...), custom_call_target="tpu_custom_call", output_to_operand_aliasing={{0}: (9, {})} | custom-call | flops 13421772800 | tf_op jit(solution)/shard_map/pallas_call | solution.py:216
  22.8 2.1 %collective-permute-done.5.x = bf16[512,128]{1,0:T(8,128)(2,1)S(1)} collective-permute-done((bf16[512,128]{1,0:T(8,128)(2,1)S(1)}, bf16[512,128]{1,0:T(8,128)(2,1)S(1)}, u32[]{:S(2)}, u32[]{:S(2)}) %collective-permute-start.5) | collective-permute-done | bytes 131104 | tf_op jit(solution)/shard_map/ppermute | solution.py:195
  24.9 1.6 %shard_map.104 = (f32[128,2048]{1,0:T(8,128)S(1)}, bf16[1024,128]{1,0:T(8,128)(2,1)S(1)}) custom-call(s32[8]{0:T(128)S(1)} %copy-done.6, bf16[512,128]{1,0:T(8,128)(2,1)S(1)} %shard_map.102.k, bf16[512,128]{1,0:T(8,128)(2,1)S(1)} %shard_map.103.v, bf16[2048,128]{1,0:T(8,128)(2,1)S(1)} %get-tuple-element.22.refs_0_.q4, ...), custom_call_target="tpu_custom_call", output_to_operand_aliasing={{0}: (9, {})} | custom-call | flops 13421772800 | tf_op jit(solution)/shard_map/pallas_call | solution.py:216
  26.5 2.7 %collective-permute-done.6.x = bf16[1024,128]{1,0:T(8,128)(2,1)S(1)} collective-permute-done((bf16[1024,128]{1,0:T(8,128)(2,1)S(1)}, bf16[1024,128]{1,0:T(8,128)(2,1)S(1)}, u32[]{:S(2)}, u32[]{:S(2)}) %collective-permute-start.6) | collective-permute-done | bytes 262176 | tf_op jit(solution)/shard_map/ppermute | solution.py:195
  29.3 1.7 %collective-permute-start.8 = (bf16[1024,128]{1,0:T(8,128)(2,1)S(1)}, bf16[1024,128]{1,0:T(8,128)(2,1)S(1)}, u32[]{:S(2)}, u32[]{:S(2)}) collective-permute-start(bf16[1024,128]{1,0:T(8,128)(2,1)S(1)} %shard_map.107.refs_0_), channel_id=1, source_target_pairs={{0,16},{8,24},{16,0},{24,8},{1,17},{9,25},{17,1},{25,9},{2,18},{10... | collective-permute-start | bytes 786440 | tf_op jit(solution)/shard_map/ppermute | solution.py:195
  31.0 0.8 %collective-permute-start.7 = (bf16[1024,128]{1,0:T(8,128)(2,1)S(1)}, bf16[1024,128]{1,0:T(8,128)(2,1)S(1)}, u32[]{:S(2)}, u32[]{:S(2)}) collective-permute-start(bf16[1024,128]{1,0:T(8,128)(2,1)S(1)} %shard_map.108), channel_id=1, source_target_pairs={{0,8},{8,0},{16,24},{24,16},{1,9},{9,1},{17,25},{25,17},{2,10},{10... | collective-permute-start | bytes 786440 | tf_op jit(solution)/shard_map/ppermute | solution.py:195
  31.9 1.0 %shard_map.105 = bf16[512,512]{1,0:T(8,128)(2,1)} custom-call(f32[128,2048]{1,0:T(8,128)S(1)} %get-tuple-element.34.dqt), custom_call_target="tpu_custom_call" | custom-call | flops 13421772800 | tf_op jit(solution)/shard_map/pallas_call | solution.py:261
  32.9 7.7 %collective-permute-done.7.refs_0_ = bf16[1024,128]{1,0:T(8,128)(2,1)S(1)} collective-permute-done((bf16[1024,128]{1,0:T(8,128)(2,1)S(1)}, bf16[1024,128]{1,0:T(8,128)(2,1)S(1)}, u32[]{:S(2)}, u32[]{:S(2)}) %collective-permute-start.7) | collective-permute-done | bytes 262176 | tf_op jit(solution)/shard_map/ppermute | solution.py:195
  40.6 2.3 %collective-permute-done.8.refs_0_ = bf16[1024,128]{1,0:T(8,128)(2,1)S(1)} collective-permute-done((bf16[1024,128]{1,0:T(8,128)(2,1)S(1)}, bf16[1024,128]{1,0:T(8,128)(2,1)S(1)}, u32[]{:S(2)}, u32[]{:S(2)}) %collective-permute-start.8) | collective-permute-done | bytes 262176 | tf_op jit(solution)/shard_map/ppermute | solution.py:195
  42.9 0.7 %shard_map.110 = (bf16[512,128]{1,0:T(8,128)(2,1)}, bf16[512,128]{1,0:T(8,128)(2,1)}) custom-call(f32[512,128]{1,0:T(8,128)S(1)} %get-tuple-element.37.dk, f32[512,128]{1,0:T(8,128)S(1)} %get-tuple-element.38.dv, bf16[1024,128]{1,0:T(8,128)(2,1)S(1)} %collective-permute-done.8.refs_0_), custom_call_target="tpu_custom_call" | custom-call | tf_op jit(solution)/shard_map/pallas_call | solution.py:226
  (25 shorter events, 0.3 us)
Async XLA Ops:
  0.6 15.0 %collective-permute-start = (bf16[512,128]{1,0:T(8,128)(2,1)}, bf16[512,128]{1,0:T(8,128)(2,1)S(1)}, u32[]{:S(2)}, u32[]{:S(2)}) collective-permute-start(bf16[512,128]{1,0:T(8,128)(2,1)} %k.1), channel_id=1, source_target_pairs={{0,24},{8,16},{16,8},{24,0},{1,25},{9,17},{17,9},{25,1},{2,26},{10... | collective-permute-start | bytes 393224 | tf_op jit(solution)/shard_map/ppermute | solution.py:195
  5.7 15.3 %collective-permute-start.2 = (bf16[512,128]{1,0:T(8,128)(2,1)}, bf16[512,128]{1,0:T(8,128)(2,1)S(1)}, u32[]{:S(2)}, u32[]{:S(2)}) collective-permute-start(bf16[512,128]{1,0:T(8,128)(2,1)} %k.1), channel_id=1, source_target_pairs={{0,8},{8,0},{16,24},{24,16},{1,9},{9,1},{17,25},{25,17},{2,10},{10... | collective-permute-start | bytes 393224 | tf_op jit(solution)/shard_map/ppermute | solution.py:195
  5.7 10.9 %collective-permute-start.3 = (bf16[512,128]{1,0:T(8,128)(2,1)}, bf16[512,128]{1,0:T(8,128)(2,1)S(1)}, u32[]{:S(2)}, u32[]{:S(2)}) collective-permute-start(bf16[512,128]{1,0:T(8,128)(2,1)} %v.1), channel_id=1, source_target_pairs={{0,24},{8,16},{16,8},{24,0},{1,25},{9,17},{17,9},{25,1},{2,26},{10... | collective-permute-start | bytes 393224 | tf_op jit(solution)/shard_map/ppermute | solution.py:195
  6.6 14.4 %collective-permute-start.4 = (bf16[512,128]{1,0:T(8,128)(2,1)}, bf16[512,128]{1,0:T(8,128)(2,1)S(1)}, u32[]{:S(2)}, u32[]{:S(2)}) collective-permute-start(bf16[512,128]{1,0:T(8,128)(2,1)} %v.1), channel_id=1, source_target_pairs={{0,8},{8,0},{16,24},{24,16},{1,9},{9,1},{17,25},{25,17},{2,10},{10... | collective-permute-start | bytes 393224 | tf_op jit(solution)/shard_map/ppermute | solution.py:195
  7.8 1.0 %copy-start = (bf16[512,512]{1,0:T(8,128)(2,1)S(1)}, bf16[512,512]{1,0:T(8,128)(2,1)}, u32[]{:S(2)}) copy-start(bf16[512,512]{1,0:T(8,128)(2,1)} %q.1) | copy-start | bytes 1572868
  8.8 1.0 %copy-start.1 = (bf16[512,512]{1,0:T(8,128)(2,1)S(1)}, bf16[512,512]{1,0:T(8,128)(2,1)}, u32[]{:S(2)}) copy-start(bf16[512,512]{1,0:T(8,128)(2,1)} %g.1) | copy-start | bytes 1572868
  9.9 1.0 %copy-start.2 = (bf16[512,512]{1,0:T(8,128)(2,1)S(1)}, bf16[512,512]{1,0:T(8,128)(2,1)}, u32[]{:S(2)}) copy-start(bf16[512,512]{1,0:T(8,128)(2,1)} %o.1) | copy-start | bytes 1572868
  10.9 0.7 %copy-start.5 = (f32[4,512]{1,0:T(4,128)S(1)}, f32[4,512]{1,0:T(4,128)}, u32[]{:S(2)}) copy-start(f32[4,512]{1,0:T(4,128)} %log_norms.1) | copy-start | bytes 24580
  11.6 0.9 %copy-start.3 = (bf16[512,128]{1,0:T(8,128)(2,1)S(1)}, bf16[512,128]{1,0:T(8,128)(2,1)}, u32[]{:S(2)}) copy-start(bf16[512,128]{1,0:T(8,128)(2,1)} %v.1) | copy-start | bytes 393220
  11.6 1.0 %copy-start.4 = (bf16[512,128]{1,0:T(8,128)(2,1)S(1)}, bf16[512,128]{1,0:T(8,128)(2,1)}, u32[]{:S(2)}) copy-start(bf16[512,128]{1,0:T(8,128)(2,1)} %k.1) | copy-start | bytes 393220
  12.4 0.7 %copy-start.6 = (s32[8]{0:T(128)S(1)}, s32[8]{0:T(128)}, u32[]{:S(2)}) copy-start(s32[8]{0:T(128)} %order.7) | copy-start | bytes 100
  15.6 7.2 %collective-permute-start.1 = (bf16[512,128]{1,0:T(8,128)(2,1)S(1)}, bf16[512,128]{1,0:T(8,128)(2,1)S(1)}, u32[]{:S(2)}, u32[]{:S(2)}) collective-permute-start(bf16[512,128]{1,0:T(8,128)(2,1)S(1)} %shard_map.95.k), channel_id=1, source_target_pairs={{0,8},{8,0},{16,24},{24,16},{1,9},{9,1},{17,25},{25,17},{2,10},{10... | collective-permute-start | bytes 393224 | tf_op jit(solution)/shard_map/ppermute | solution.py:195
  16.6 8.3 %collective-permute-start.5 = (bf16[512,128]{1,0:T(8,128)(2,1)S(1)}, bf16[512,128]{1,0:T(8,128)(2,1)S(1)}, u32[]{:S(2)}, u32[]{:S(2)}) collective-permute-start(bf16[512,128]{1,0:T(8,128)(2,1)S(1)} %shard_map.97.v), channel_id=1, source_target_pairs={{0,8},{8,0},{16,24},{24,16},{1,9},{9,1},{17,25},{25,17},{2,10},{10... | collective-permute-start | bytes 393224 | tf_op jit(solution)/shard_map/ppermute | solution.py:195
  20.7 8.5 %collective-permute-start.6 = (bf16[1024,128]{1,0:T(8,128)(2,1)S(1)}, bf16[1024,128]{1,0:T(8,128)(2,1)S(1)}, u32[]{:S(2)}, u32[]{:S(2)}) collective-permute-start(bf16[1024,128]{1,0:T(8,128)(2,1)S(1)} %get-tuple-element.30.refs_0_), channel_id=1, source_target_pairs={{0,8},{8,0},{16,24},{24,16},{1,9},{9,1},{17,25},{25,17},{2,10},{10... | collective-permute-start | bytes 786440 | tf_op jit(solution)/shard_map/ppermute | solution.py:195
  29.3 13.6 %collective-permute-start.8 = (bf16[1024,128]{1,0:T(8,128)(2,1)S(1)}, bf16[1024,128]{1,0:T(8,128)(2,1)S(1)}, u32[]{:S(2)}, u32[]{:S(2)}) collective-permute-start(bf16[1024,128]{1,0:T(8,128)(2,1)S(1)} %shard_map.107.refs_0_), channel_id=1, source_target_pairs={{0,16},{8,24},{16,0},{24,8},{1,17},{9,25},{17,1},{25,9},{2,18},{10... | collective-permute-start | bytes 786440 | tf_op jit(solution)/shard_map/ppermute | solution.py:195
  31.0 9.5 %collective-permute-start.7 = (bf16[1024,128]{1,0:T(8,128)(2,1)S(1)}, bf16[1024,128]{1,0:T(8,128)(2,1)S(1)}, u32[]{:S(2)}, u32[]{:S(2)}) collective-permute-start(bf16[1024,128]{1,0:T(8,128)(2,1)S(1)} %shard_map.108), channel_id=1, source_target_pairs={{0,8},{8,0},{16,24},{24,16},{1,9},{9,1},{17,25},{25,17},{2,10},{10... | collective-permute-start | bytes 786440 | tf_op jit(solution)/shard_map/ppermute | solution.py:195
